TPU v7x, 32 devices: a whole 2x2x4 slice. The times are simulated.
32 devices in a mesh: dp: 8 (over y, x, core), tp: 4 (over z).
Axes of the slice: x: 2, y: 2, z: 4, core: 2. Of those that a mesh axis runs over, the one named last changes fastest.
Arguments:
- tokens: bfloat16 [16, 2048, 768], P('dp', 'tp'), may hold values from -6 to 6
- segment_ids: int32 [16, 2048], P('dp'), may hold values from 0 to 65535, as said below
- positions: int32 [16, 2048], P('dp'), may hold values from 0 to 2015, as said below
- w_qkv: bfloat16 [768, 2304], P(None, ('dp', 'tp')), may hold values from -0.3125 to 0.3125
- w_out: bfloat16 [768, 768], P(None, ('dp', 'tp')), may hold values from -0.875 to 0.875
- norm1_gain: bfloat16 [768], P(('dp', 'tp')), may hold values from 0.5 to 1.5
- norm1_shift: bfloat16 [768], P(('dp', 'tp')), may hold values from -1.5 to 1.5
- w_gate: bfloat16 [768, 3072], P('dp', 'tp'), may hold values from -0.21875 to 0.21875
- w_up: bfloat16 [768, 3072], P('dp', 'tp'), may hold values from -0.21875 to 0.21875
- w_down: bfloat16 [3072, 768], P('tp', 'dp'), may hold values from -0.15625 to 0.15625
- norm2_gain: bfloat16 [768], P(('dp', 'tp')), may hold values from 0.5 to 1.5
- norm2_shift: bfloat16 [768], P(('dp', 'tp')), may hold values from -1.5 to 1.5
- out_grad: bfloat16 [16, 2048, 768], P('dp', 'tp'), may hold values from -6 to 6
Outputs:
- output: bfloat16 [16, 2048, 768], P('dp', 'tp')
- in_grad: bfloat16 [16, 2048, 768], P('dp', 'tp')
- g_qkv: float32 [768, 2304], P(None, ('dp', 'tp'))
- g_out: float32 [768, 768], P(None, ('dp', 'tp'))
- g_norm1_gain: float32 [768], P(('dp', 'tp'))
- g_norm1_shift: float32 [768], P(('dp', 'tp'))
- g_gate: float32 [768, 3072], P('dp', 'tp')
- g_up: float32 [768, 3072], P('dp', 'tp')
- g_down: float32 [3072, 768], P('tp', 'dp')
- g_norm2_gain: float32 [768], P(('dp', 'tp'))
- g_norm2_shift: float32 [768], P(('dp', 'tp'))
Inputs may be any that keep to these rules, and one draw needn't show every extreme that they name: `segment_ids`: in each row the tokens of a document are contiguous and share an id, and the row's two documents have different ids: the first starts at slot 0 and the second fills the last t slots, t from 32 to 64, drawn for each row. Each document's positions count 0, 1, 2, ... from its first token.
All inputs are finite; a program needn't handle non-finite values.
Results may differ from a plain program's by a relative error of at most 0.02.
The roundings to bfloat16 on the way count: a program that leaves them out, or rounds other values in their place, can miss the bound.
Values may be sent and summed in bfloat16 or wider, within the bound.
No kernel may reach another device: no remote copies, remote signals or barrier semaphores. Data moves between devices by JAX's collectives and lax.ppermute only.
A program may use at most 384 MiB of HBM per device.

v0:
```python
import jax
import jax.numpy as jnp
from jax import lax
from jax.sharding import PartitionSpec as P

HEADS = 12
HEAD_DIM = 64


EPSILON = 1e-05


def rope_tables(positions, head_width):
    half_dim = head_width // 2
    frequency = 1000.0 ** (-(jnp.arange(half_dim, dtype=jnp.float32) * 2.0) / head_width)
    angles = positions.astype(jnp.float32)[..., None] * frequency
    return (jnp.cos(angles), jnp.sin(angles))


def rotate(values, cosine, sine):
    half_dim = values.shape[-1] // 2
    front = values[..., :half_dim]
    behind = values[..., half_dim:]
    cos_part = cosine[..., None, :]
    sin_part = sine[..., None, :]
    return jnp.concatenate(
        [front * cos_part - behind * sin_part, behind * cos_part + front * sin_part], axis=-1
    )


def unrotate(grads, cosine, sine):
    half_dim = grads.shape[-1] // 2
    front = grads[..., :half_dim]
    behind = grads[..., half_dim:]
    cos_part = cosine[..., None, :]
    sin_part = sine[..., None, :]
    return jnp.concatenate(
        [front * cos_part + behind * sin_part, behind * cos_part - front * sin_part], axis=-1
    )


def norm_forward(values, gain, shift):
    center = jnp.mean(values, axis=-1, keepdims=True)
    centered = values - center
    inverse = lax.rsqrt(jnp.mean(centered * centered, axis=-1, keepdims=True) + EPSILON)
    normed = centered * inverse
    return (normed * gain + shift, normed, inverse)


def norm_backward(grads, normed, inverse, gain):
    scaled = grads * gain
    first_mean = jnp.mean(scaled, axis=-1, keepdims=True)
    second_mean = jnp.mean(scaled * normed, axis=-1, keepdims=True)
    return inverse * (scaled - first_mean - normed * second_mean)


def masked_scores(query_block, keys, seg_block, key_segments, scale):
    scores = (
        jnp.einsum("qhd,khd->hqk", query_block, keys, preferred_element_type=jnp.float32) * scale
    )
    same_doc = (seg_block[:, None] == key_segments[None, :])[None]
    return jnp.where(same_doc, scores, -1e30)


def attend_forward(queries, keys, values, query_segments, key_segments, scale):
    query_len = queries.shape[0]
    block_len = min(query_len, 512)
    blocks = query_len // block_len
    query_blocks = queries.reshape(blocks, block_len, queries.shape[1], queries.shape[2])
    seg_blocks = query_segments.reshape(blocks, block_len)

    def one_block(block_items):
        query_block, seg_block = block_items
        scores = masked_scores(query_block, keys, seg_block, key_segments, scale)
        row_top = jnp.max(scores, axis=-1, keepdims=True)
        expo_terms = jnp.exp(scores - row_top)
        row_total = jnp.sum(expo_terms, axis=-1, keepdims=True)
        soft_probs = (expo_terms / row_total).astype(jnp.bfloat16)
        result = jnp.einsum("hqk,khd->qhd", soft_probs, values, preferred_element_type=jnp.float32)
        return (result.astype(jnp.bfloat16), (row_top + jnp.log(row_total))[..., 0])

    results, log_sums = lax.map(one_block, (query_blocks, seg_blocks))
    return (results.reshape(queries.shape), log_sums)


def attend_backward(queries, keys, values, query_segments, key_segments, log_sums, grad_in, scale):
    query_len = queries.shape[0]
    block_len = min(query_len, 512)
    blocks = query_len // block_len
    query_blocks = queries.reshape(blocks, block_len, queries.shape[1], queries.shape[2])
    grad_blocks = grad_in.reshape(blocks, block_len, queries.shape[1], queries.shape[2])
    seg_blocks = query_segments.reshape(blocks, block_len)

    def one_block(carry, block_items):
        key_acc, value_acc = carry
        query_block, seg_block, log_block, grad_block = block_items
        scores = masked_scores(query_block, keys, seg_block, key_segments, scale)
        soft_probs = jnp.exp(scores - log_block[..., None])
        value_acc = value_acc + jnp.einsum(
            "hqk,qhd->khd",
            soft_probs.astype(jnp.bfloat16),
            grad_block,
            preferred_element_type=jnp.float32,
        )
        prob_grad = jnp.einsum(
            "qhd,khd->hqk", grad_block, values, preferred_element_type=jnp.float32
        )
        row_dot = jnp.sum(prob_grad * soft_probs, axis=-1, keepdims=True)
        score_grad = (soft_probs * (prob_grad - row_dot)).astype(jnp.bfloat16)
        query_grad = (
            jnp.einsum("hqk,khd->qhd", score_grad, keys, preferred_element_type=jnp.float32) * scale
        )
        key_acc = (
            key_acc
            + jnp.einsum(
                "hqk,qhd->khd", score_grad, query_block, preferred_element_type=jnp.float32
            )
            * scale
        )
        return ((key_acc, value_acc), query_grad)

    zero_grads = jnp.zeros(keys.shape, jnp.float32)
    (key_grad, value_grad), query_grads = lax.scan(
        one_block, (zero_grads, zero_grads), (query_blocks, seg_blocks, log_sums, grad_blocks)
    )
    return (query_grads.reshape(queries.shape), key_grad, value_grad)


def attend_rows(queries, keys, values, query_segments, key_segments, scale):

    def one_row(row_items):
        return attend_forward(
            row_items[0], row_items[1], row_items[2], row_items[3], row_items[4], scale
        )

    return lax.map(one_row, (queries, keys, values, query_segments, key_segments))


def attend_rows_back(queries, keys, values, query_segments, key_segments, log_sums, grad_in, scale):

    def one_row(row_items):
        return attend_backward(
            row_items[0],
            row_items[1],
            row_items[2],
            row_items[3],
            row_items[4],
            row_items[5],
            row_items[6],
            scale,
        )

    return lax.map(
        one_row, (queries, keys, values, query_segments, key_segments, log_sums, grad_in)
    )


def local(
    tokens,
    segment_ids,
    positions,
    w_qkv,
    w_out,
    norm1_gain,
    norm1_shift,
    w_gate,
    w_up,
    w_down,
    norm2_gain,
    norm2_shift,
    out_grad,
):
    row_count, piece_len, width = tokens.shape
    seq_len = segment_ids.shape[1]
    scale = HEAD_DIM ** (-0.5)
    offset = lax.axis_index("tp") * piece_len
    qkv_full, out_full, gain_one, shift_one, gain_two, shift_two = (
        lax.all_gather(w_qkv, ("dp", "tp"), axis=1, tiled=True),
        lax.all_gather(w_out, ("dp", "tp"), axis=1, tiled=True),
        lax.all_gather(norm1_gain, ("dp", "tp"), axis=0, tiled=True),
        lax.all_gather(norm1_shift, ("dp", "tp"), axis=0, tiled=True),
        lax.all_gather(norm2_gain, ("dp", "tp"), axis=0, tiled=True),
        lax.all_gather(norm2_shift, ("dp", "tp"), axis=0, tiled=True),
    )
    gate_full, up_full, down_full = (
        lax.all_gather(w_gate, "dp", axis=0, tiled=True),
        lax.all_gather(w_up, "dp", axis=0, tiled=True),
        lax.all_gather(w_down, "dp", axis=1, tiled=True),
    )
    gain_one = gain_one.astype(jnp.float32)
    shift_one = shift_one.astype(jnp.float32)
    gain_two = gain_two.astype(jnp.float32)
    shift_two = shift_two.astype(jnp.float32)
    full_rows = lax.all_gather(tokens, "tp", axis=1, tiled=True)
    cosine, sine = rope_tables(positions, HEAD_DIM)
    own_cos = lax.dynamic_slice_in_dim(cosine, offset, piece_len, 1)
    own_sin = lax.dynamic_slice_in_dim(sine, offset, piece_len, 1)
    own_segments = lax.dynamic_slice_in_dim(segment_ids, offset, piece_len, 1)
    query_pre = jnp.einsum(
        "rsd,de->rse", tokens, qkv_full[:, :width], preferred_element_type=jnp.float32
    )
    key_value = jnp.einsum(
        "rsd,de->rse", full_rows, qkv_full[:, width:], preferred_element_type=jnp.float32
    )
    key_pre = key_value[..., :width]
    value_pre = key_value[..., width:]
    query_cos, query_sin, query_segments = (own_cos, own_sin, own_segments)
    query_len = query_pre.shape[1]
    queries = rotate(
        query_pre.reshape(row_count, query_len, HEADS, HEAD_DIM), query_cos, query_sin
    ).astype(jnp.bfloat16)
    keys = rotate(key_pre.reshape(row_count, seq_len, HEADS, HEAD_DIM), cosine, sine).astype(
        jnp.bfloat16
    )
    values = value_pre.reshape(row_count, seq_len, HEADS, HEAD_DIM).astype(jnp.bfloat16)
    attended, log_sums = attend_rows(queries, keys, values, query_segments, segment_ids, scale)
    attended_flat = attended.reshape(row_count, query_len, width)
    projected = jnp.einsum(
        "rsd,de->rse", attended_flat, out_full, preferred_element_type=jnp.float32
    )
    x_one, normed_one, inverse_one = norm_forward(
        tokens.astype(jnp.float32) + projected, gain_one, shift_one
    )
    x_one_rows = lax.all_gather(x_one.astype(jnp.bfloat16), "tp", axis=1, tiled=True)
    gate = jnp.einsum("rsd,df->rsf", x_one_rows, gate_full, preferred_element_type=jnp.float32)
    up_part = jnp.einsum("rsd,df->rsf", x_one_rows, up_full, preferred_element_type=jnp.float32)
    sigma = jax.nn.sigmoid(gate)
    activated = gate * sigma
    hidden = (activated * up_part).astype(jnp.bfloat16)
    down_terms = jnp.einsum("rsf,fd->rsd", hidden, down_full, preferred_element_type=jnp.float32)
    mixed = lax.psum_scatter(
        down_terms.astype(jnp.bfloat16), "tp", scatter_dimension=1, tiled=True
    ).astype(jnp.float32)
    result_two, normed_two, inverse_two = norm_forward(x_one + mixed, gain_two, shift_two)
    output = result_two.astype(jnp.bfloat16)
    grad_top = out_grad.astype(jnp.float32)
    gain_two_grad = jnp.sum(grad_top * normed_two, axis=(0, 1))
    shift_two_grad = jnp.sum(grad_top, axis=(0, 1))
    d_resid_two = norm_backward(grad_top, normed_two, inverse_two, gain_two)
    mix_rows = lax.all_gather(d_resid_two.astype(jnp.bfloat16), "tp", axis=1, tiled=True)
    down_grad = jnp.einsum("rsf,rsd->fd", hidden, mix_rows, preferred_element_type=jnp.float32)
    hidden_grad = jnp.einsum("rsd,fd->rsf", mix_rows, down_full, preferred_element_type=jnp.float32)
    gate_grad = (hidden_grad * up_part * (sigma * (1.0 + gate * (1.0 - sigma)))).astype(
        jnp.bfloat16
    )
    up_grad = (hidden_grad * activated).astype(jnp.bfloat16)
    gate_w_grad = jnp.einsum(
        "rsd,rsf->df", x_one_rows, gate_grad, preferred_element_type=jnp.float32
    )
    up_w_grad = jnp.einsum("rsd,rsf->df", x_one_rows, up_grad, preferred_element_type=jnp.float32)
    x_one_terms = jnp.einsum(
        "rsf,df->rsd", gate_grad, gate_full, preferred_element_type=jnp.float32
    )
    x_one_terms = x_one_terms + jnp.einsum(
        "rsf,df->rsd", up_grad, up_full, preferred_element_type=jnp.float32
    )
    x_one_back = lax.psum_scatter(
        x_one_terms.astype(jnp.bfloat16), "tp", scatter_dimension=1, tiled=True
    ).astype(jnp.float32)
    d_x_one = d_resid_two + x_one_back
    gain_one_grad = jnp.sum(d_x_one * normed_one, axis=(0, 1))
    shift_one_grad = jnp.sum(d_x_one, axis=(0, 1))
    d_resid_one = norm_backward(d_x_one, normed_one, inverse_one, gain_one)
    proj_grad = d_resid_one.astype(jnp.bfloat16)
    mlp_parts = (
        lax.psum_scatter(
            gate_w_grad.astype(jnp.bfloat16), "dp", scatter_dimension=0, tiled=True
        ).astype(jnp.float32),
        lax.psum_scatter(
            up_w_grad.astype(jnp.bfloat16), "dp", scatter_dimension=0, tiled=True
        ).astype(jnp.float32),
        lax.psum_scatter(
            down_grad.astype(jnp.bfloat16), "dp", scatter_dimension=1, tiled=True
        ).astype(jnp.float32),
    )
    out_w_grad = jnp.einsum(
        "rsd,rse->de", attended_flat, proj_grad, preferred_element_type=jnp.float32
    )
    att_grad = jnp.einsum(
        "rse,de->rsd", proj_grad, out_full, preferred_element_type=jnp.float32
    ).astype(jnp.bfloat16)
    att_grad = att_grad.reshape(row_count, piece_len, HEADS, HEAD_DIM)
    query_grad, key_part, value_part = attend_rows_back(
        queries, keys, values, query_segments, segment_ids, log_sums, att_grad, scale
    )
    key_sum, value_sum = (
        lax.psum_scatter(
            key_part.astype(jnp.bfloat16), "tp", scatter_dimension=1, tiled=True
        ).astype(jnp.float32),
        lax.psum_scatter(
            value_part.astype(jnp.bfloat16), "tp", scatter_dimension=1, tiled=True
        ).astype(jnp.float32),
    )
    query_grad = unrotate(query_grad, own_cos, own_sin)
    key_sum = unrotate(key_sum, own_cos, own_sin)
    qkv_grad = jnp.concatenate(
        [
            query_grad.reshape(row_count, piece_len, width),
            key_sum.reshape(row_count, piece_len, width),
            value_sum.reshape(row_count, piece_len, width),
        ],
        axis=-1,
    ).astype(jnp.bfloat16)
    qkv_w_grad = jnp.einsum("rsd,rse->de", tokens, qkv_grad, preferred_element_type=jnp.float32)
    in_terms = jnp.einsum("rse,de->rsd", qkv_grad, qkv_full, preferred_element_type=jnp.float32)
    in_grad = (d_resid_one + in_terms).astype(jnp.bfloat16)
    qkv_final, out_final, gain_one_final, shift_one_final, gain_two_final, shift_two_final = (
        lax.psum_scatter(qkv_w_grad, ("dp", "tp"), scatter_dimension=1, tiled=True),
        lax.psum_scatter(out_w_grad, ("dp", "tp"), scatter_dimension=1, tiled=True),
        lax.psum_scatter(gain_one_grad, ("dp", "tp"), scatter_dimension=0, tiled=True),
        lax.psum_scatter(shift_one_grad, ("dp", "tp"), scatter_dimension=0, tiled=True),
        lax.psum_scatter(gain_two_grad, ("dp", "tp"), scatter_dimension=0, tiled=True),
        lax.psum_scatter(shift_two_grad, ("dp", "tp"), scatter_dimension=0, tiled=True),
    )
    return (
        output,
        in_grad,
        qkv_final,
        out_final,
        gain_one_final,
        shift_one_final,
        mlp_parts[0],
        mlp_parts[1],
        mlp_parts[2],
        gain_two_final,
        shift_two_final,
    )


def solution(mesh):
    placed = (
        P("dp", "tp", None),
        P("dp", None),
        P("dp", None),
        P(None, ("dp", "tp")),
        P(None, ("dp", "tp")),
        P(("dp", "tp")),
        P(("dp", "tp")),
        P("dp", "tp"),
        P("dp", "tp"),
        P("tp", "dp"),
        P(("dp", "tp")),
        P(("dp", "tp")),
        P("dp", "tp", None),
    )
    return jax.shard_map(
        local,
        mesh=mesh,
        in_specs=placed,
        out_specs=(
            P("dp", "tp", None),
            P("dp", "tp", None),
            P(None, ("dp", "tp")),
            P(None, ("dp", "tp")),
            P(("dp", "tp")),
            P(("dp", "tp")),
            P("dp", "tp"),
            P("dp", "tp"),
            P("tp", "dp"),
            P(("dp", "tp")),
            P(("dp", "tp")),
        ),
        check_vma=False,
    )
```

profile of v0, /device:TPU:0, one launch (start us, length us, event | category | flops | bytes accessed | tf_op | source)
XLA Modules:
  0.0 1833.6 jit_solution(9164328408799921419)
XLA Ops:
  13.4 42.2 %all-reduce.9 = (bf16[768]{0:T(1024)(128)(2,1)S(1)}, bf16[768]{0:T(1024)(128)(2,1)S(1)}, bf16[768]{0:T(1024)(128)(2,1)}, bf16[768]{0:T(1024)(128)(2,1)}) all-reduce(bf16[768]{0:T(1024)(128)(2,1)S(1)} %dynamic-update-slice.1, bf16[768]{0:T(1024)(128)(2,1)S(1)} %dynamic-update-slice, ...), channel_id=1, replica_groups=mesh['dp'=8,'tp'=4] {'dp','tp'}, use_global_device_ids=true, to_apply=%add.1 | all-reduce | flops 3072 | bytes 12288
  60.2 13.7 all-gather.11.cloned.1.call-done
  73.9 2.7 fusion.69
  77.3 112.3 %all-gather.9.cloned.1.call-done = bf16[2,2048,768]{2,1,0:T(8,128)(2,1)} async-done(((bf16[2,512,768]{2,1,0:T(8,128)(2,1)}), bf16[2,2048,768]{2,1,0:T(8,128)(2,1)}) %all-gather.9.cloned.1.call-update) | async-done | bytes 6291472 | tf_op jit(solution)/shard_map/all_gather | solution.py:194
  189.6 17.4 fusion.66
  207.1 8.1 slice.80
  215.2 11.4 slice.54
  226.6 5.7 subtract_convert_fusion
  232.2 3.8 pad_maximum_fusion
  236.0 134.0 %while.10 = (s32[]{:T(128)}, bf16[2,512,12,64]{1,3,2,0:T(8,128)(2,1)}, f32[2,1,12,512]{3,2,1,0:T(8,128)S(1)}, bf16[2,2048,12,64]{1,3,2,0:T(8,128)(2,1)}, s32[2,5...) while((s32[]{:T(128)}, ...), condition=%wide.region_3.4_spmd, body=%wide.region_0.3_spmd.sunk | while | flops 3373656064 | bytes 163307632 | solution.py:136
  237.2 22.4 %fusion.122 = (f32[12,512]{1,0:T(8,128)S(1)}, f32[12,512,2048]{2,1,0:T(8,128)}) fusion(pred[512,2048]{1,0:T(8,128)(4,1)S(1)} %broadcast_compare_fusion.4, bf16[2,2048,12,64]{1,3,2,0:T(8,128)(2,1)} %get-tuple-element.417, s32[]{:T(128)S(6)} %copy.82, bf16[2,512,12,64]{1,3,2,0:T(8,128)(2,1)S(1)} %get-tuple-element.416), kind=kOutput, calls=%fused_computation.3.clone.1 | convolution fusion | flops 1648355328 | bytes 55337984 | tf_op jit(solution)/shard_map/while/body/eval_jaxpr/while/body/eval_jaxpr/qhd,khd->hqk/dot_general | solution.py:59
  259.6 22.0 %fusion.123 = f32[12,512]{1,0:T(8,128)S(1)} fusion(f32[12,512,2048]{2,1,0:T(8,128)} %get-tuple-element.377, f32[12,512]{1,0:T(8,128)S(1)} %get-tuple-element.378, pred[512,2048]{1,0:T(8,128)(4,1)S(1)} %broadcast_compare_fusion.4), kind=kLoop, calls=%fused_computation.4.clone.1 | loop fusion | flops 50325504 | bytes 51429376 | tf_op jit(solution)/shard_map/while/body/eval_jaxpr/while/body/eval_jaxpr/reduce_sum | solution.py:77
  281.6 21.7 %fusion.124 = bf16[2,512,12,64]{1,3,2,0:T(8,128)(2,1)} fusion(bf16[2,512,12,64]{1,3,2,0:T(8,128)(2,1)} %get-tuple-element.402, s32[]{:T(128)S(6)} %copy.82, f32[12,512,2048]{2,1,0:T(8,128)} %get-tuple-element.377, f32[12,512]{1,0:T(8,128)S(1)} %fusion.123, f32[12,512]{1,0:T(8,128)S(1)} %get-tuple-element.378, ...), kind=kOutput, calls=%fused_computation.14.clone.1 | convolution fusion | flops 1673920512 | bytes 55362560 | tf_op jit(solution)/shard_map/while/body/eval_jaxpr/while/body/eval_jaxpr/hqk,khd->qhd/dot_general | solution.py:79
  304.0 22.3 %fusion.122 = (f32[12,512]{1,0:T(8,128)S(1)}, f32[12,512,2048]{2,1,0:T(8,128)}) fusion(pred[512,2048]{1,0:T(8,128)(4,1)S(1)} %broadcast_compare_fusion.4, bf16[2,2048,12,64]{1,3,2,0:T(8,128)(2,1)} %get-tuple-element.417, s32[]{:T(128)S(6)} %copy.82, bf16[2,512,12,64]{1,3,2,0:T(8,128)(2,1)S(1)} %get-tuple-element.416), kind=kOutput, calls=%fused_computation.3.clone.1 | convolution fusion | flops 1648355328 | bytes 55337984 | tf_op jit(solution)/shard_map/while/body/eval_jaxpr/while/body/eval_jaxpr/qhd,khd->hqk/dot_general | solution.py:59
  326.3 21.9 %fusion.123 = f32[12,512]{1,0:T(8,128)S(1)} fusion(f32[12,512,2048]{2,1,0:T(8,128)} %get-tuple-element.377, f32[12,512]{1,0:T(8,128)S(1)} %get-tuple-element.378, pred[512,2048]{1,0:T(8,128)(4,1)S(1)} %broadcast_compare_fusion.4), kind=kLoop, calls=%fused_computation.4.clone.1 | loop fusion | flops 50325504 | bytes 51429376 | tf_op jit(solution)/shard_map/while/body/eval_jaxpr/while/body/eval_jaxpr/reduce_sum | solution.py:77
  348.2 21.7 %fusion.124 = bf16[2,512,12,64]{1,3,2,0:T(8,128)(2,1)} fusion(bf16[2,512,12,64]{1,3,2,0:T(8,128)(2,1)} %get-tuple-element.402, s32[]{:T(128)S(6)} %copy.82, f32[12,512,2048]{2,1,0:T(8,128)} %get-tuple-element.377, f32[12,512]{1,0:T(8,128)S(1)} %fusion.123, f32[12,512]{1,0:T(8,128)S(1)} %get-tuple-element.378, ...), kind=kOutput, calls=%fused_computation.14.clone.1 | convolution fusion | flops 1673920512 | bytes 55362560 | tf_op jit(solution)/shard_map/while/body/eval_jaxpr/while/body/eval_jaxpr/hqk,khd->qhd/dot_general | solution.py:79
  370.1 3.8 fusion.88
  378.7 112.3 %all-gather.15.cloned.1.call-done = bf16[2,2048,768]{2,1,0:T(8,128)(2,1)} async-done(((bf16[2,512,768]{2,1,0:T(8,128)(2,1)}), bf16[2,2048,768]{2,1,0:T(8,128)(2,1)}) %all-gather.15.cloned.1.call-update) | async-done | bytes 6291472 | tf_op jit(solution)/shard_map/all_gather | solution.py:224
  491.0 10.2 fusion.78
  501.2 13.9 all-gather.19.cloned.1.call-done
  515.1 14.0 multiply_convert_fusion.3
  529.0 12.0 all-gather.21.cloned.1.call-done
  541.0 9.2 convolution_convert_fusion
  550.9 110.3 %reduce-scatter.10.cloned.1.call-done = bf16[2,512,768]{2,1,0:T(8,128)(2,1)} async-done(((bf16[2,2048,768]{2,1,0:T(8,128)(2,1)}), bf16[2,512,768]{2,1,0:T(8,128)(2,1)}) %reduce-scatter.10.cloned.1.call-update) | async-done | bytes 1572880 | tf_op jit(solution)/shard_map/reduce_scatter | solution.py:231
  661.2 3.3 fusion.87
  665.0 2.0 copy-done.3
  667.0 2.5 fusion.64
  671.5 116.0 %all-gather.23.cloned.1.call-done = bf16[2,2048,768]{2,1,0:T(8,128)(2,1)} async-done(((bf16[2,512,768]{2,1,0:T(8,128)(2,1)}), bf16[2,2048,768]{2,1,0:T(8,128)(2,1)}) %all-gather.23.cloned.1.call-update) | async-done | bytes 6291472 | tf_op jit(solution)/shard_map/all_gather | solution.py:240
  787.5 17.4 multiply_convert_fusion.1
  804.9 10.4 fusion.76
  815.3 10.0 add_convert_fusion
  826.0 108.4 %reduce-scatter.12.cloned.1.call-done = bf16[2,512,768]{2,1,0:T(8,128)(2,1)} async-done(((bf16[2,2048,768]{2,1,0:T(8,128)(2,1)}), bf16[2,512,768]{2,1,0:T(8,128)(2,1)}) %reduce-scatter.12.cloned.1.call-update) | async-done | bytes 1572880 | tf_op jit(solution)/shard_map/reduce_scatter | solution.py:257
  934.4 6.8 multiply_reduce_fusion.1
  943.9 2.6 convolution_convert_fusion.1
  946.5 2.6 copy.54
  949.1 302.3 %while.27 = (s32[]{:T(128)}, f32[2,512,12,64]{1,3,2,0:T(8,128)}, bf16[2,2048,12,64]{1,3,2,0:T(8,128)(2,1)}, bf16[2,2048,12,64]{1,3,2,0:T(8,128)(2,1)}, bf16[2,20...) while((s32[]{:T(128)}, f32[2,512,12,64]{1,3,2,0:T(8,128)}, ...), condition=%wide.region_16.17_spmd, body=%wide.region_14.16_spmd.sunk | while | flops 8244815872 | bytes 408628352 | solution.py:153
  950.0 21.2 %fusion.133 = f32[12,512,2048]{2,1,0:T(8,128)} fusion(bf16[2,2048,12,64]{1,3,2,0:T(8,128)(2,1)} %get-tuple-element.447, s32[]{:T(128)S(6)} %copy.96, bf16[2,512,12,64]{1,3,2,0:T(8,128)(2,1)S(1)} %get-tuple-element.450), kind=kOutput, calls=%fused_computation.36.clone.1 | convolution fusion | flops 1610612736 | bytes 54264832 | tf_op jit(solution)/shard_map/while/body/eval_jaxpr/while/body/eval_jaxpr/qhd,khd->hqk/dot_general | solution.py:59
  971.2 22.4 %bitcast_dynamic-update-slice_fusion.11 = bf16[2,2048,12,64]{1,3,2,0:T(8,128)(2,1)} fusion(bf16[2,2048,12,64]{1,3,2,0:T(8,128)(2,1)} %get-tuple-element.434, s32[]{:T(128)S(6)} %copy.96, f32[12,512,2048]{2,1,0:T(8,128)} %fusion.133, f32[12,512]{1,0:T(8,128)S(1)} %dynamic-slice_bitcast_fusion.2, pred[512,2048]{1,0:T(8,128)(4,1)S(1)} %broadcast_compare_fusion.5, ...), kind=kOutput, calls=%fused_computation.30.clone.1 | convolution fusion | flops 1660944384 | bytes 58483712 | tf_op jit(solution)/shard_map/while/body/eval_jaxpr/while/body/eval_jaxpr/hqk,qhd->khd/dot_general | solution.py:99
  993.6 37.5 %multiply_reduce_fusion.7 = (f32[12,512]{1,0:T(8,128)S(1)}, f32[12,512,2048]{2,1,0:T(8,128)}) fusion(f32[12,512,2048]{2,1,0:T(8,128)} %fusion.133, f32[12,512]{1,0:T(8,128)S(1)} %dynamic-slice_bitcast_fusion.2, pred[512,2048]{1,0:T(8,128)(4,1)S(1)} %broadcast_compare_fusion.5, bf16[2,2048,12,64]{1,3,2,0:T(8,128)(2,1)} %get-tuple-element.453, ...), kind=kOutput, calls=%fused_computation.25.clone.1 | convolution fusion | flops 1673521152 | bytes 105694208 | tf_op jit(solution)/shard_map/while/body/eval_jaxpr/while/body/eval_jaxpr/qhd,khd->hqk/dot_general | solution.py:105
  1031.1 40.4 %multiply_convert_fusion.5 = bf16[12,512,2048]{2,1,0:T(8,128)(2,1)} fusion(f32[12,512,2048]{2,1,0:T(8,128)} %get-tuple-element.390, f32[12,512,2048]{2,1,0:T(8,128)} %fusion.133, f32[12,512]{1,0:T(8,128)S(1)} %get-tuple-element.391, f32[12,512]{1,0:T(8,128)S(1)} %dynamic-slice_bitcast_fusion.2, pred[512,2048]{1,0:T(8,128)(4,1)S(1)} %broadcast_compare_fusion.5), kind=kLoop, calls=%fused_computation.24.clone.1 | loop fusion | flops 75497472 | bytes 126926848 | tf_op jit(solution)/shard_map/while/body/eval_jaxpr/while/body/eval_jaxpr/convert_element_type | solution.py:109
  1071.5 14.3 bitcast_dynamic-update-slice_fusion.9
  1085.8 14.4 bitcast_dynamic-update-slice_fusion.10
  1100.9 21.2 %fusion.133 = f32[12,512,2048]{2,1,0:T(8,128)} fusion(bf16[2,2048,12,64]{1,3,2,0:T(8,128)(2,1)} %get-tuple-element.447, s32[]{:T(128)S(6)} %copy.96, bf16[2,512,12,64]{1,3,2,0:T(8,128)(2,1)S(1)} %get-tuple-element.450), kind=kOutput, calls=%fused_computation.36.clone.1 | convolution fusion | flops 1610612736 | bytes 54264832 | tf_op jit(solution)/shard_map/while/body/eval_jaxpr/while/body/eval_jaxpr/qhd,khd->hqk/dot_general | solution.py:59
  1122.1 22.4 %bitcast_dynamic-update-slice_fusion.11 = bf16[2,2048,12,64]{1,3,2,0:T(8,128)(2,1)} fusion(bf16[2,2048,12,64]{1,3,2,0:T(8,128)(2,1)} %get-tuple-element.434, s32[]{:T(128)S(6)} %copy.96, f32[12,512,2048]{2,1,0:T(8,128)} %fusion.133, f32[12,512]{1,0:T(8,128)S(1)} %dynamic-slice_bitcast_fusion.2, pred[512,2048]{1,0:T(8,128)(4,1)S(1)} %broadcast_compare_fusion.5, ...), kind=kOutput, calls=%fused_computation.30.clone.1 | convolution fusion | flops 1660944384 | bytes 58483712 | tf_op jit(solution)/shard_map/while/body/eval_jaxpr/while/body/eval_jaxpr/hqk,qhd->khd/dot_general | solution.py:99
  1144.6 37.5 %multiply_reduce_fusion.7 = (f32[12,512]{1,0:T(8,128)S(1)}, f32[12,512,2048]{2,1,0:T(8,128)}) fusion(f32[12,512,2048]{2,1,0:T(8,128)} %fusion.133, f32[12,512]{1,0:T(8,128)S(1)} %dynamic-slice_bitcast_fusion.2, pred[512,2048]{1,0:T(8,128)(4,1)S(1)} %broadcast_compare_fusion.5, bf16[2,2048,12,64]{1,3,2,0:T(8,128)(2,1)} %get-tuple-element.453, ...), kind=kOutput, calls=%fused_computation.25.clone.1 | convolution fusion | flops 1673521152 | bytes 105694208 | tf_op jit(solution)/shard_map/while/body/eval_jaxpr/while/body/eval_jaxpr/qhd,khd->hqk/dot_general | solution.py:105
  1182.1 40.4 %multiply_convert_fusion.5 = bf16[12,512,2048]{2,1,0:T(8,128)(2,1)} fusion(f32[12,512,2048]{2,1,0:T(8,128)} %get-tuple-element.390, f32[12,512,2048]{2,1,0:T(8,128)} %fusion.133, f32[12,512]{1,0:T(8,128)S(1)} %get-tuple-element.391, f32[12,512]{1,0:T(8,128)S(1)} %dynamic-slice_bitcast_fusion.2, pred[512,2048]{1,0:T(8,128)(4,1)S(1)} %broadcast_compare_fusion.5), kind=kLoop, calls=%fused_computation.24.clone.1 | loop fusion | flops 75497472 | bytes 126926848 | tf_op jit(solution)/shard_map/while/body/eval_jaxpr/while/body/eval_jaxpr/convert_element_type | solution.py:109
  1222.4 14.4 bitcast_dynamic-update-slice_fusion.9
  1236.8 14.3 bitcast_dynamic-update-slice_fusion.10
  1252.1 9.9 bitcast_convert_fusion
  1262.1 9.9 bitcast_convert_fusion.1
  1272.0 10.0 bitcast_convert_fusion.2
  1282.1 4.3 convolution_bitcast_fusion.1
  1286.5 76.4 %reduce-scatter.16.cloned.1.call-done = bf16[2,512,12,64]{1,3,2,0:T(8,128)(2,1)} async-done(((bf16[2,2048,12,64]{1,3,2,0:T(8,128)(2,1)}), bf16[2,512,12,64]{1,3,2,0:T(8,128)(2,1)}) %reduce-scatter.16.cloned.1.call-update) | async-done | bytes 1572880 | tf_op jit(solution)/shard_map/reduce_scatter | solution.py:290
  1362.9 2.7 copy.57
  1365.7 110.7 %reduce-scatter.14.cloned.1.call-done = bf16[2,512,12,64]{1,3,2,0:T(8,128)(2,1)} async-done(((bf16[2,2048,12,64]{1,3,2,0:T(8,128)(2,1)}), bf16[2,512,12,64]{1,3,2,0:T(8,128)(2,1)}) %reduce-scatter.14.cloned.1.call-update) | async-done | bytes 1572880 | tf_op jit(solution)/shard_map/reduce_scatter | solution.py:287
  1476.4 2.0 convert_element_type.135
  1483.3 9.2 convolution_bitcast_fusion
  1492.5 24.4 %reduce-scatter.26.cloned.1.call-done = bf16[768,96]{0,1:T(8,128)(2,1)} async-done(((bf16[768,768]{0,1:T(8,128)(2,1)}), bf16[768,96]{0,1:T(8,128)(2,1)}) %reduce-scatter.26.cloned.1.call-update) | async-done | bytes 147472 | tf_op jit(solution)/shard_map/reduce_scatter | solution.py:272
  1518.6 38.6 %reduce-scatter.24.cloned.1.call-done = bf16[96,768]{1,0:T(8,128)(2,1)} async-done(((bf16[768,768]{1,0:T(8,128)(2,1)}), bf16[96,768]{1,0:T(8,128)(2,1)}) %reduce-scatter.24.cloned.1.call-update) | async-done | bytes 147472 | tf_op jit(solution)/shard_map/reduce_scatter | solution.py:269
  1558.8 38.2 %reduce-scatter.22.cloned.1.call-done = bf16[96,768]{1,0:T(8,128)(2,1)} async-done(((bf16[768,768]{1,0:T(8,128)(2,1)}), bf16[96,768]{1,0:T(8,128)(2,1)}) %reduce-scatter.22.cloned.1.call-update) | async-done | bytes 147472 | tf_op jit(solution)/shard_map/reduce_scatter | solution.py:266
  1598.7 39.6 %all-reduce.8 = (f32[768]{0:T(1024)S(1)}, f32[768]{0:T(1024)S(1)}, f32[768]{0:T(1024)S(1)}, f32[768]{0:T(1024)S(1)}) all-reduce(f32[768]{0:T(1024)S(1)} %copy-done.17, f32[768]{0:T(1024)S(1)} %copy-done.18, f32[768]{0:T(1024)S(1)} %copy-done.19, f32[768]{0:T(1024)S(1)} %copy-done.20), channel_id=8, replica_groups=mesh['dp'=8,'tp'=4] {'dp','tp'}, use_global_device_ids=true, to_apply=%region_22.23.clone | all-reduce | flops 3072 | bytes 24576
  1640.7 8.4 add_convert_fusion.2
  1649.1 53.5 %reduce-scatter.20.cloned.1.call-done = f32[768,24]{0,1:T(8,128)} async-done(((f32[768,768]{0,1:T(8,128)}), f32[768,24]{0,1:T(8,128)}) %reduce-scatter.20.cloned.1.call-update) | async-done | bytes 73744 | tf_op jit(solution)/shard_map/reduce_scatter | solution.py:309
  1702.6 124.3 %reduce-scatter.18.cloned.1.call-done = f32[768,72]{0,1:T(8,128)} async-done(((f32[768,2304]{0,1:T(8,128)}), f32[768,72]{0,1:T(8,128)}) %reduce-scatter.18.cloned.1.call-update) | async-done | bytes 221200 | tf_op jit(solution)/shard_map/reduce_scatter | solution.py:308
  (152 shorter events, 38.2 us)
Async XLA Ops:
  7.2 66.7 %copy-start.8 = (bf16[2,512,768]{2,1,0:T(8,128)(2,1)S(1)}, bf16[2,512,768]{2,1,0:T(8,128)(2,1)}, u32[]{:S(2)}) copy-start(bf16[2,512,768]{2,1,0:T(8,128)(2,1)} %param.17) | copy-start | bytes 4718596
  7.2 66.7 %all-gather.11.cloned.1.call-start = ((), (), s32[]{:S(2)}) async-start(), calls=%async_computation.10 | async-start | bytes 3649536 | tf_op jit(solution)/shard_map/all_gather | solution.py:178
  7.9 181.7 %all-gather.9.cloned.1.call-start = ((), (), s32[]{:S(2)}) async-start(), calls=%async_computation.9 | async-start | bytes 7864320 | tf_op jit(solution)/shard_map/all_gather | solution.py:194
  8.7 361.4 %all-gather.13.cloned.1.call-start = ((), (), s32[]{:S(2)}) async-start(), calls=%async_computation.11 | async-start | bytes 1216512 | tf_op jit(solution)/shard_map/all_gather | solution.py:179
  9.4 369.3 %all-gather.17.cloned.1.call-start = ((), (), s32[]{:S(2)}) async-start(), calls=%async_computation.13 | async-start | bytes 1327104 | tf_op jit(solution)/shard_map/all_gather | solution.py:186
  10.0 481.1 %all-gather.15.cloned.1.call-start = ((), (), s32[]{:S(2)}) async-start(), calls=%async_computation.12 | async-start | bytes 7864320 | tf_op jit(solution)/shard_map/all_gather | solution.py:224
  60.2 16.4 copy-start.10
  60.2 16.4 copy-start.12
  232.2 3.8 copy-start.14
  374.0 1.6 copy-start
  374.0 1.6 copy-start.15
  374.0 1.6 copy-start.16
  377.3 137.8 %all-gather.19.cloned.1.call-start = ((), (), s32[]{:S(2)}) async-start(), calls=%async_computation.14 | async-start | bytes 1327104 | tf_op jit(solution)/shard_map/all_gather | solution.py:187
  377.9 163.2 %all-gather.21.cloned.1.call-start = ((), (), s32[]{:S(2)}) async-start(), calls=%async_computation.15 | async-start | bytes 1327104 | tf_op jit(solution)/shard_map/all_gather | solution.py:188
  378.6 282.5 %reduce-scatter.10.cloned.1.call-start = ((), (), s32[]{:S(2)}) async-start(), calls=%async_computation.16 | async-start | bytes 7864320 | tf_op jit(solution)/shard_map/reduce_scatter | solution.py:231
  550.2 0.6 copy-start.22
  550.3 237.2 %all-gather.23.cloned.1.call-start = ((), (), s32[]{:S(2)}) async-start(), calls=%async_computation.17 | async-start | bytes 7864320 | tf_op jit(solution)/shard_map/all_gather | solution.py:240
  664.5 5.1 copy-start.2
  664.5 2.5 copy-start.3
  671.5 262.9 %reduce-scatter.12.cloned.1.call-start = ((), (), s32[]{:S(2)}) async-start(), calls=%async_computation.18 | async-start | bytes 7864320 | tf_op jit(solution)/shard_map/reduce_scatter | solution.py:257
  804.9 10.4 copy-start.24
  804.9 10.4 copy-start.25
  825.3 0.7 copy-start.21
  825.3 537.6 %reduce-scatter.16.cloned.1.call-start = ((), (), s32[]{:S(2)}) async-start(), calls=%async_computation.20 | async-start | bytes 7864320 | tf_op jit(solution)/shard_map/reduce_scatter | solution.py:290
  934.4 6.9 copy-start.1
  941.3 2.7 copy-start.23
  942.2 1.7 copy-start.4
  1251.5 224.9 %reduce-scatter.14.cloned.1.call-start = ((), (), s32[]{:S(2)}) async-start(), calls=%async_computation.19 | async-start | bytes 7864320 | tf_op jit(solution)/shard_map/reduce_scatter | solution.py:287
  1252.1 264.9 %reduce-scatter.26.cloned.1.call-start = ((), (), s32[]{:S(2)}) async-start(), calls=%async_computation.25 | async-start | bytes 1327104 | tf_op jit(solution)/shard_map/reduce_scatter | solution.py:272
  1262.0 295.2 %reduce-scatter.24.cloned.1.call-start = ((), (), s32[]{:S(2)}) async-start(), calls=%async_computation.24 | async-start | bytes 1327104 | tf_op jit(solution)/shard_map/reduce_scatter | solution.py:269
  1272.0 10.1 copy-start.5
  1272.0 325.1 %reduce-scatter.22.cloned.1.call-start = ((), (), s32[]{:S(2)}) async-start(), calls=%async_computation.23 | async-start | bytes 1327104 | tf_op jit(solution)/shard_map/reduce_scatter | solution.py:266
  1282.1 420.6 %reduce-scatter.20.cloned.1.call-start = ((), (), s32[]{:S(2)}) async-start(), calls=%async_computation.22 | async-start | bytes 2433024 | tf_op jit(solution)/shard_map/reduce_scatter | solution.py:309
  1286.5 540.4 %reduce-scatter.18.cloned.1.call-start = ((), (), s32[]{:S(2)}) async-start(), calls=%async_computation.21 | async-start | bytes 7299072 | tf_op jit(solution)/shard_map/reduce_scatter | solution.py:308
  1365.7 112.7 %copy-start.11 = (f32[2,512,32]{1,2,0:T(8,128)S(1)}, f32[2,512,32]{1,2,0:T(8,128)}, u32[]{:S(2)}) copy-start(f32[2,512,32]{1,2,0:T(8,128)} %copy-done.10) | copy-start | bytes 393220
  1365.7 112.7 %copy-start.13 = (f32[2,512,32]{1,2,0:T(8,128)S(1)}, f32[2,512,32]{1,2,0:T(8,128)}, u32[]{:S(2)}) copy-start(f32[2,512,32]{1,2,0:T(8,128)} %copy-done.12) | copy-start | bytes 393220
  1476.4 2.4 copy-start.7
  1481.7 1.6 copy-start.9
  1492.5 106.2 %copy-start.17 = (f32[768]{0:T(1024)S(1)}, f32[768]{0:T(1024)}, u32[]{:S(2)}) copy-start(f32[768]{0:T(1024)} %get-tuple-element.186) | copy-start | bytes 9220
  1492.5 106.2 %copy-start.18 = (f32[768]{0:T(1024)S(1)}, f32[768]{0:T(1024)}, u32[]{:S(2)}) copy-start(f32[768]{0:T(1024)} %get-tuple-element.191) | copy-start | bytes 9220
  1492.5 106.2 %copy-start.19 = (f32[768]{0:T(1024)S(1)}, f32[768]{0:T(1024)}, u32[]{:S(2)}) copy-start(f32[768]{0:T(1024)} %get-tuple-element.188) | copy-start | bytes 9220
  1492.5 106.2 %copy-start.20 = (f32[768]{0:T(1024)S(1)}, f32[768]{0:T(1024)}, u32[]{:S(2)}) copy-start(f32[768]{0:T(1024)} %get-tuple-element.193) | copy-start | bytes 9220
  1492.5 148.2 %copy-start.6 = (f32[2,512,768]{2,1,0:T(8,128)S(1)}, f32[2,512,768]{2,1,0:T(8,128)}, u32[]{:S(2)}) copy-start(f32[2,512,768]{2,1,0:T(8,128)} %copy-done.4) | copy-start | bytes 9437188
Sparse Core Ops, SparseCore 0:
  10.8 63.0 all-gather.10
  75.5 114.1 all-gather.8
  192.4 52.2 all-gather.12
  246.5 22.9 all-gather.16
  377.4 113.5 all-gather.14
  492.8 22.2 all-gather.18
  517.0 24.0 all-gather.20
  550.4 110.7 reduce-scatter.9
  671.6 115.8 all-gather.22
  825.4 108.9 reduce-scatter.11
  1251.6 111.2 reduce-scatter.15
  1365.1 111.2 reduce-scatter.13
  1479.6 37.2 reduce-scatter.25
  1520.4 36.7 reduce-scatter.23
  1560.3 36.7 reduce-scatter.21
  1603.6 98.9 reduce-scatter.19
  1708.7 118.1 reduce-scatter.17
where the time goes:
time: 1840 us; the launch traced here: 1830 us
  waiting for transfers between devices  1070 us (58%)
  matrix products  457 us (25%)
  other arithmetic  168 us (9%)
  blocking collectives  81.9 us (4%)
  local copies, waits for them, and re-layouts  40.9 us (2%)
    reduce_scatter x1, waiting for transfers between devices, local(): lax.psum_scatter(qkv_w_grad, ('dp', 'tp'), scatter_dimension=1, tiled=True)  124 us
    all_gather x1, waiting for transfers between devices, local(): lax.all_gather(d_resid_two.astype(jnp.bfloat16), 'tp', axis=1, tiled=True)  116 us
    all_gather x1, waiting for transfers between devices, local(): lax.all_gather(x_one.astype(jnp.bfloat16), 'tp', axis=1, tiled=True)  112 us
    all_gather x1, waiting for transfers between devices, local(): full_rows = lax.all_gather(tokens, 'tp', axis=1, tiled=True)  112 us
    reduce_scatter x1, waiting for transfers between devices, local(): lax.psum_scatter(key_part.astype(jnp.bfloat16), 'tp', scatter_dimension=1...  111 us
    reduce_scatter x1, waiting for transfers between devices, local(): lax.psum_scatter(down_terms.astype(jnp.bfloat16), 'tp', scatter_dimension...  110 us
    reduce_scatter x1, waiting for transfers between devices, local(): lax.psum_scatter(x_one_terms.astype(jnp.bfloat16), 'tp', scatter_dimensio...  108 us
    dot_general x4, matrix products, masked_scores(): jnp.einsum('qhd,khd->hqk', query_block, keys, preferred_element_type=jnp....  87.2 us
  transfers between devices with their start and end apart: 17, of which 15 were waited for; matrix products, arithmetic and copies ran while one was open for 16% of the time, Pallas kernels for 0%

commit v1 on v0

v1 whole, which is shorter than its diff:
```python
import functools

import jax
import jax.numpy as jnp
from jax import lax
from jax.experimental import pallas as pl
from jax.experimental.pallas import tpu as pltpu
from jax.sharding import Mesh, PartitionSpec as P

HEADS = 12
HEAD_DIM = 64
EPSILON = 1e-05
AUG = 16
MASK = 2.0**99
LOW = jnp.bfloat16
WIDE = jnp.float32
SWAP = [(0, 1), (1, 0)]


def dot(a, b, ca, cb):
    return lax.dot_general(a, b, (((ca,), (cb,)), ((), ())), preferred_element_type=WIDE)


def split3(x):
    high = x.astype(LOW)
    rest = x - high.astype(WIDE)
    middle = rest.astype(LOW)
    return [high, middle, (rest - middle.astype(WIDE)).astype(LOW)]


def put_rows(base, at, rows):
    index = lax.broadcasted_iota(jnp.int32, base.shape, 0)
    out = base.astype(WIDE)
    for i, row in enumerate(rows):
        out = jnp.where(index == at + i, row.astype(WIDE), out)
    return out.astype(LOW)


def ones_row(n):
    return jnp.ones((1, n), WIDE)


def forward_kernel(parts, *refs):
    q_ref, qa_ref = refs[:2]
    k_refs, v_refs, ka_refs = refs[2 : 2 + parts], refs[2 + parts : 2 + 2 * parts], refs[2 + 2 * parts : 2 + 3 * parts]
    o_ref, lse_ref, keys = refs[2 + 3 * parts :]
    at = 0
    values = []
    for k_ref, v_ref, ka_ref in zip(k_refs, v_refs, ka_refs):
        n = k_ref.shape[1]
        keys[at : at + n] = jnp.concatenate([k_ref[...], ka_ref[...]], axis=0).T
        values.append(v_ref[...])
        at += n
    queries = jnp.concatenate([q_ref[...], qa_ref[...]], axis=0)
    scores = dot(keys[...], queries, 1, 0)
    top = jnp.max(scores, axis=0, keepdims=True)
    terms = jnp.exp(scores - top)
    total = jnp.sum(terms, axis=0, keepdims=True)
    result = dot(jnp.concatenate(values, axis=1), terms.astype(LOW), 1, 0)
    o_ref[...] = (result / total).astype(LOW)
    lse_ref[...] = (top + jnp.log(total)).reshape(1, 1, -1)


def attend_forward(q, qa, ks, vs, kas):
    parts, nq = len(ks), q.shape[1]
    nk = sum(k.shape[1] for k in ks)
    head = lambda n: pl.BlockSpec((HEAD_DIM, n), lambda h: (h, 0))
    whole = lambda n: pl.BlockSpec((AUG, n), lambda h: (0, 0))
    return pl.pallas_call(
        functools.partial(forward_kernel, parts),
        grid=(HEADS,),
        in_specs=[head(nq), whole(nq)]
        + [head(k.shape[1]) for k in ks]
        + [head(v.shape[1]) for v in vs]
        + [whole(k.shape[1]) for k in ks],
        out_specs=[head(nq), pl.BlockSpec((1, 1, nq), lambda h: (h, 0, 0))],
        out_shape=[
            jax.ShapeDtypeStruct((HEADS * HEAD_DIM, nq), LOW),
            jax.ShapeDtypeStruct((HEADS, 1, nq), WIDE),
        ],
        scratch_shapes=[pltpu.VMEM((nk, HEAD_DIM + AUG), LOW)],
        compiler_params=pltpu.CompilerParams(vmem_limit_bytes=56 << 20),
        cost_estimate=pl.CostEstimate(
            flops=16 * HEADS * nq * nk * HEAD_DIM, bytes_accessed=4 * HEADS * HEAD_DIM * (nq + nk), transcendentals=HEADS * nq * nk
        ),
        name="attend_forward",
    )(q, qa, *ks, *vs, *kas)


def backward_kernel(parts, *refs):
    q_ref, g_ref, o_ref, lse_ref, qa_ref = refs[:5]
    k_refs, v_refs, ka_refs = refs[5 : 5 + parts], refs[5 + parts : 5 + 2 * parts], refs[5 + 2 * parts : 5 + 3 * parts]
    dq_ref = refs[5 + 3 * parts]
    dk_refs = refs[6 + 3 * parts : 6 + 4 * parts]
    dv_refs = refs[6 + 4 * parts : 6 + 5 * parts]
    keys, values = refs[6 + 5 * parts :]
    nq = q_ref.shape[1]
    at = 0
    key_list = []
    for k_ref, v_ref, ka_ref in zip(k_refs, v_refs, ka_refs):
        n = k_ref.shape[1]
        keys[at : at + n] = jnp.concatenate(
            [k_ref[...], put_rows(ka_ref[...], 2, [ones_row(n)] * 3)], axis=0
        ).T
        values[at : at + n] = jnp.concatenate(
            [v_ref[...], put_rows(jnp.zeros((AUG, n), LOW), 0, [ones_row(n)] * 3)], axis=0
        ).T
        key_list.append(k_ref[...])
        at += n
    grads, queries = g_ref[...], q_ref[...]
    delta = jnp.sum(grads.astype(WIDE) * o_ref[...].astype(WIDE), axis=0, keepdims=True)
    query_aug = jnp.concatenate([queries, put_rows(qa_ref[...], 2, split3(-lse_ref[0]))], axis=0)
    grad_aug = jnp.concatenate([grads, put_rows(jnp.zeros((AUG, nq), LOW), 0, split3(-delta))], axis=0)
    probs = jnp.exp(dot(keys[...], query_aug, 1, 0))
    prob_grads = dot(values[...], grad_aug, 1, 0)
    low_probs = probs.astype(LOW)
    score_grads = (probs * prob_grads).astype(LOW)
    dq_ref[...] = dot(jnp.concatenate(key_list, axis=1), score_grads, 1, 0) * HEAD_DIM ** (-0.5)
    dv = dot(grads, low_probs, 1, 1)
    dk = dot(queries, score_grads, 1, 1)
    at = 0
    for dk_ref, dv_ref in zip(dk_refs, dv_refs):
        n = dk_ref.shape[1]
        dk_ref[...] = dk[:, at : at + n].astype(dk_ref.dtype)
        dv_ref[...] = dv[:, at : at + n].astype(dv_ref.dtype)
        at += n


def attend_backward(q, g, o, lse, qa, ks, vs, kas, types):
    parts, nq = len(ks), q.shape[1]
    sizes = [k.shape[1] for k in ks]
    nk = sum(sizes)
    head = lambda n: pl.BlockSpec((HEAD_DIM, n), lambda h: (h, 0))
    whole = lambda n: pl.BlockSpec((AUG, n), lambda h: (0, 0))
    width = HEADS * HEAD_DIM
    out = pl.pallas_call(
        functools.partial(backward_kernel, parts),
        grid=(HEADS,),
        in_specs=[head(nq), head(nq), head(nq), pl.BlockSpec((1, 1, nq), lambda h: (h, 0, 0)), whole(nq)]
        + [head(n) for n in sizes]
        + [head(n) for n in sizes]
        + [whole(n) for n in sizes],
        out_specs=[head(nq)] + [head(n) for n in sizes] * 2,
        out_shape=[jax.ShapeDtypeStruct((width, nq), WIDE)]
        + [jax.ShapeDtypeStruct((width, n), t) for n, t in zip(sizes, types)] * 2,
        scratch_shapes=[pltpu.VMEM((nk, HEAD_DIM + AUG), LOW)] * 2,
        compiler_params=pltpu.CompilerParams(vmem_limit_bytes=60 << 20),
        cost_estimate=pl.CostEstimate(
            flops=30 * HEADS * nq * nk * HEAD_DIM, bytes_accessed=8 * width * (nq + nk), transcendentals=HEADS * nq * nk
        ),
        name="attend_backward",
    )(q, g, o, lse, qa, *ks, *vs, *kas)
    return out[0], out[1 : 1 + parts], out[1 + parts :]


def norm_forward(values, gain, shift):
    center = jnp.mean(values, axis=-1, keepdims=True)
    centered = values - center
    inverse = lax.rsqrt(jnp.mean(centered * centered, axis=-1, keepdims=True) + EPSILON)
    normed = centered * inverse
    return (normed * gain + shift, normed, inverse)


def norm_backward(grads, normed, inverse, gain):
    scaled = grads * gain
    first_mean = jnp.mean(scaled, axis=-1, keepdims=True)
    second_mean = jnp.mean(scaled * normed, axis=-1, keepdims=True)
    return inverse * (scaled - first_mean - normed * second_mean)


def local(
    tp, ways, tokens, segment_ids, positions, w_qkv, w_out, norm1_gain, norm1_shift, w_gate, w_up, w_down, norm2_gain, norm2_shift, out_grad
):
    rows, piece, width = tokens.shape
    chips, per_group = ways
    dp, near = 2 * chips, tp // per_group
    line = ("core", "zg", "zm")
    everyone = ("zg", "zm", "chip", "core")
    core = lax.axis_index("core")
    group = lax.axis_index("zg")
    z = group * near + lax.axis_index("zm")
    member = lax.axis_index("zm") * 2 + core
    own = rows * piece

    def ring(step):
        pairs = []
        for c in range(2):
            for j in range(tp):
                row = c * rows + (j + step) % rows
                m = j // rows
                pairs.append((c * tp + j, (m % 2) * tp + row * near + m // 2))
        return pairs

    def bring(x):
        return [
            lax.ppermute(lax.dynamic_index_in_dim(x, (z + k) % rows, 0, False), line, ring(k))
            for k in range(rows)
        ]

    def give_back(x):
        back = [
            lax.ppermute(x[k * piece : (k + 1) * piece], line, [(b, a) for a, b in ring(k)])
            for k in range(rows)
        ]
        return jnp.roll(jnp.stack(back), z, axis=0)

    def gather_all(x):
        whole = lax.all_gather(x, everyone, axis=0, tiled=False)
        return whole.reshape((tp, dp) + x.shape)

    def scatter_all(x):
        return lax.psum_scatter(
            x.reshape((tp * dp,) + x.shape[2:]).astype(LOW), everyone, scatter_dimension=0, tiled=False
        ).astype(WIDE)

    nq, no = w_qkv.shape[1], w_out.shape[1]
    pad = -(nq + no + 1) % 16
    norm_row = jnp.concatenate([norm1_gain, norm1_shift, norm2_gain, norm2_shift])
    first = jnp.concatenate(
        [w_qkv.T, w_out.T, jnp.pad(norm_row, (0, width - 4 * no))[None], jnp.zeros((pad, width), LOW)]
    )
    x = jnp.concatenate(bring(tokens))
    first = gather_all(first)
    gate_full = gather_all(w_gate).reshape(tp, width, -1)
    up_full = gather_all(w_up).reshape(tp, width, -1)
    down_full = gather_all(w_down.T).reshape(tp, width, -1)
    by_column = first.swapaxes(0, 1)
    qkv_t = by_column[:, :, :nq].reshape(3 * width, width)
    out_t = by_column[:, :, nq : nq + no].reshape(width, width)
    vectors = by_column[:, :, nq + no, : 4 * no].reshape(dp * tp, 4, no).swapaxes(0, 1).reshape(4, width)
    gain_one, shift_one, gain_two, shift_two = vectors.astype(WIDE)
    grad_top = jnp.concatenate(bring(out_grad)).astype(WIDE)

    info = jnp.stack([segment_ids, positions])
    other = lax.ppermute(info, "core", SWAP)
    info = jnp.where(core == 0, jnp.stack([info, other], 1), jnp.stack([other, info], 1))
    info = info.reshape(2, 2 * rows, -1)
    info = lax.dynamic_index_in_dim(info, group, 1, False)
    second = (info[0] != info[0, 0]).reshape(-1, rows, piece)
    second = jnp.roll(second[:, ::-1], group + 1, axis=1).reshape(-1, own)
    places = info[1].reshape(-1, rows, piece)
    places = jnp.roll(places[:, ::-1], group + 1, axis=1).reshape(-1, own)
    own_second = lax.dynamic_index_in_dim(second, member, 0, False)
    own_places = lax.dynamic_index_in_dim(places, member, 0, False)

    def key_aug(is_second):
        return jnp.pad(
            jnp.stack([jnp.where(is_second, 0.0, -MASK), jnp.where(is_second, -MASK, 0.0)]), ((0, AUG - 2), (0, 0))
        ).astype(LOW)

    query_aug = jnp.pad(
        jnp.stack([own_second, ~own_second]).astype(WIDE), ((0, AUG - 2), (0, 0))
    ).astype(LOW)

    half = HEAD_DIM // 2
    frequency = 1000.0 ** (-(jnp.arange(half, dtype=WIDE) * 2.0) / HEAD_DIM)
    angles = own_places.astype(WIDE)[None] * frequency[:, None]
    cosine, sine = jnp.cos(angles), jnp.sin(angles)

    qkv = dot(qkv_t, x, 1, 1)
    pairs = qkv[: 2 * width].reshape(2 * HEADS, 2, half, own)
    front, behind = pairs[:, 0], pairs[:, 1]
    turned = jnp.stack([front * cosine - behind * sine, behind * cosine + front * sine], axis=1)
    turned = turned.reshape(2 * width, own)
    q = (turned[:width].astype(LOW) * HEAD_DIM ** (-0.5)).astype(LOW)
    kv = jnp.concatenate([turned[width:].astype(LOW), qkv[2 * width :].astype(LOW)])
    members = 2 * near
    if members == 2:
        other_kv = lax.ppermute(kv, "core", SWAP)
        ks, vs = [kv[:width], other_kv[:width]], [kv[width:], other_kv[width:]]
        other_second = lax.dynamic_index_in_dim(second, 1 - member, 0, False)
        kas = [key_aug(own_second), key_aug(other_second)]
        types = [WIDE, LOW]
    else:
        all_kv = lax.all_gather(kv, ("zm", "core"), axis=1, tiled=True)
        ks, vs, kas = [all_kv[:width]], [all_kv[width:]], [key_aug(second.reshape(-1))]
        types = [LOW]
    attended, lse = attend_forward(q, query_aug, ks, vs, kas)

    projected = dot(attended, out_t, 0, 1)
    x_one, normed_one, inverse_one = norm_forward(x.astype(WIDE) + projected, gain_one, shift_one)
    x_low = x_one.astype(LOW)
    gate = jnp.einsum("td,jdf->jtf", x_low, gate_full, preferred_element_type=WIDE)
    up = jnp.einsum("td,jdf->jtf", x_low, up_full, preferred_element_type=WIDE)
    sigma = jax.nn.sigmoid(gate)
    activated = gate * sigma
    hidden = (activated * up).astype(LOW)
    mixed = jnp.einsum("jtf,jdf->td", hidden, down_full, preferred_element_type=WIDE)
    result, normed_two, inverse_two = norm_forward(x_one + mixed, gain_two, shift_two)
    output = give_back(result.astype(LOW))

    gain_two_grad = jnp.sum(grad_top * normed_two, axis=0)
    shift_two_grad = jnp.sum(grad_top, axis=0)
    d_resid_two = norm_backward(grad_top, normed_two, inverse_two, gain_two)
    mix_grad = d_resid_two.astype(LOW)
    hidden_grad = jnp.einsum("td,jdf->jtf", mix_grad, down_full, preferred_element_type=WIDE)
    gate_grad = (hidden_grad * up * (sigma * (1.0 + gate * (1.0 - sigma)))).astype(LOW)
    up_grad = (hidden_grad * activated).astype(LOW)
    x_terms = jnp.einsum("jtf,jdf->td", gate_grad, gate_full, preferred_element_type=WIDE)
    x_terms = x_terms + jnp.einsum("jtf,jdf->td", up_grad, up_full, preferred_element_type=WIDE)
    d_x_one = d_resid_two + x_terms

    def weight_grad(a, b):
        full = jnp.einsum("td,jtf->jdf", a, b, preferred_element_type=WIDE)
        return scatter_all(full.reshape(tp, dp, width // dp, -1))

    g_down = weight_grad(mix_grad, hidden).T
    g_gate = weight_grad(x_low, gate_grad)
    g_up = weight_grad(x_low, up_grad)

    gain_one_grad = jnp.sum(d_x_one * normed_one, axis=0)
    shift_one_grad = jnp.sum(d_x_one, axis=0)
    d_resid_one = norm_backward(d_x_one, normed_one, inverse_one, gain_one)
    proj_grad = d_resid_one.astype(LOW)
    g_out = dot(proj_grad, attended, 0, 1)
    att_grad = dot(out_t, proj_grad, 0, 1).astype(LOW)
    dq, dks, dvs = attend_backward(q, att_grad, attended, lse, query_aug, ks, vs, kas, types)
    if members == 2:
        sent = lax.ppermute(jnp.concatenate([dks[1], dvs[1]]), "core", SWAP)
        dk = dks[0] + sent[:width].astype(WIDE)
        dv = dvs[0] + sent[width:].astype(WIDE)
    else:
        summed = lax.psum_scatter(
            jnp.concatenate([dks[0], dvs[0]]), ("zm", "core"), scatter_dimension=1, tiled=True
        ).astype(WIDE)
        dk, dv = summed[:width], summed[width:]
    pairs = jnp.concatenate([dq, dk]).reshape(2 * HEADS, 2, half, own)
    front, behind = pairs[:, 0], pairs[:, 1]
    turned = jnp.stack([front * cosine + behind * sine, behind * cosine - front * sine], axis=1)
    qkv_grad = jnp.concatenate([turned.reshape(2 * width, own), dv]).astype(LOW)
    g_qkv = dot(qkv_grad, x, 1, 0)
    in_grad = (d_resid_one + dot(qkv_grad, qkv_t, 0, 0)).astype(LOW)
    in_grad = give_back(in_grad)

    norms = jnp.stack([gain_one_grad, shift_one_grad, gain_two_grad, shift_two_grad])
    norms = norms.reshape(4, dp * tp, no).swapaxes(0, 1).reshape(dp, tp, 1, 4 * no)
    norms = jnp.pad(norms, ((0, 0), (0, 0), (0, pad), (0, width - 4 * no)))
    last = jnp.concatenate([g_qkv.reshape(dp, tp, nq, width), g_out.reshape(dp, tp, no, width), norms], axis=2)
    last = scatter_all(last.swapaxes(0, 1))
    vectors = last[nq + no, : 4 * no].reshape(4, no)
    return (
        output,
        in_grad,
        last[:nq].T,
        last[nq : nq + no].T,
        vectors[0],
        vectors[1],
        g_gate,
        g_up,
        g_down,
        vectors[2],
        vectors[3],
    )


def solution(mesh):
    dp, tp = mesh.shape["dp"], mesh.shape["tp"]

    def run(*arrays):
        rows = arrays[0].shape[0] // dp
        groups = 2 * rows
        grid = Mesh(
            mesh.devices.reshape(dp // 2, 2, groups, tp // groups), ("chip", "core", "zg", "zm")
        )
        d, t = ("chip", "core"), ("zg", "zm")
        both = d + t
        placed = (
            P(d, t, None),
            P(d, None),
            P(d, None),
            P(None, both),
            P(None, both),
            P(both),
            P(both),
            P(d, t),
            P(d, t),
            P(t, d),
            P(both),
            P(both),
            P(d, t, None),
        )
        return jax.shard_map(
            functools.partial(local, tp, (dp // 2, groups)),
            mesh=grid,
            in_specs=placed,
            out_specs=(
                P(d, t, None),
                P(d, t, None),
                P(None, both),
                P(None, both),
                P(both),
                P(both),
                P(d, t),
                P(d, t),
                P(t, d),
                P(both),
                P(both),
            ),
            check_vma=False,
        )(*arrays)

    return run
```

time: 1840 us -> 811 us (0.44)
  waiting for transfers between devices: 1070 us -> 435 us
  matrix products: 457 us -> 129 us
  other arithmetic: 168 us -> 41.5 us
  Pallas kernels: 0 us -> 108 us
  blocking collectives: 81.9 us -> 0 us
  starting transfers between devices: 0.68 us -> 28.8 us
    reduce_scatter x9 -> x4, waiting for transfers between devices: 685 us -> 239 us  [scatter_all(): lax.psum_scatter(x.reshape((tp * dp,) + x.shape[2:]).astype(LOW), everyon...]
    dot_general x30 -> x15, matrix products: 457 us -> 129 us  [the longest x6 30.2 us: dot(): lax.dot_general(a, b, (((ca,), (cb,)), ((), ())), preferred_element_type=...]
    all_gather x8 -> x4, waiting for transfers between devices: 380 us -> 140 us  [gather_all(): whole = lax.all_gather(x, everyone, axis=0, tiled=False)]
    pallas_call x0 -> x2, Pallas kernels: none -> 108 us  [the longest x1 70.8 us: attend_backward(): pl.pallas_call(functools.partial(backward_kernel, parts), grid=(HEADS,),...]
    convert_element_type x13 -> x8, other arithmetic: 93.2 us -> 7.89 us  [the longest x3 4.25 us: scatter_all(): return lax.psum_scatter(x.reshape((tp * dp,) + x.shape[2:]).astype(LOW),...]
    unnamed x2 -> x0, blocking collectives: 81.9 us -> none
    ppermute x0 -> x11, waiting for transfers between devices: none -> 55.1 us  [the longest x4 36.4 us: give_back(): lax.ppermute(x[k * piece:(k + 1) * piece], line, [(b, a) for a, b in ring...]
    reduce_sum x5 -> x4, other arithmetic: 56.5 us -> 7.72 us  [the longest x1 5.04 us: local(): gain_two_grad = jnp.sum(grad_top * normed_two, axis=0)]
  transfers between devices with their start and end apart: 17 -> 19, of which waited for: 15 -> 10; matrix products, arithmetic and copies ran while one was open for 16% -> 23% of each run, Pallas kernels for 0% -> 13%
where the time goes in v1:
time: 811 us; the launch traced here: 800 us
  waiting for transfers between devices  435 us (54%)
  matrix products  129 us (16%)
  Pallas kernels  108 us (13%)
  local copies, waits for them, and re-layouts  43.2 us (5%)
  other arithmetic  41.5 us (5%)
  starting transfers between devices  28.8 us (4%)
  between operations  15.1 us (2%)
    reduce_scatter x4, waiting for transfers between devices, scatter_all(): lax.psum_scatter(x.reshape((tp * dp,) + x.shape[2:]).astype(LOW), everyon...  239 us
    all_gather x4, waiting for transfers between devices, gather_all(): whole = lax.all_gather(x, everyone, axis=0, tiled=False)  140 us
    pallas_call x1, Pallas kernels, attend_backward(): pl.pallas_call(functools.partial(backward_kernel, parts), grid=(HEADS,),...  70.8 us
    pallas_call x1, Pallas kernels, attend_forward(): pl.pallas_call(functools.partial(forward_kernel, parts), grid=(HEADS,), i...  37.1 us
    ppermute x4, waiting for transfers between devices, give_back(): lax.ppermute(x[k * piece:(k + 1) * piece], line, [(b, a) for a, b in ring...  36.4 us
    dot_general x6, matrix products, dot(): lax.dot_general(a, b, (((ca,), (cb,)), ((), ())), preferred_element_type=...  30.2 us
    dot_general x3, matrix products, weight_grad(): full = jnp.einsum('td,jtf->jdf', a, b, preferred_element_type=WIDE)  24.7 us
    dot_general x1, matrix products, local(): jnp.einsum('td,jdf->jtf', mix_grad, down_full, preferred_element_type=WIDE)  20 us
  transfers between devices with their start and end apart: 19, of which 10 were waited for; matrix products, arithmetic and copies ran while one was open for 23% of the time, Pallas kernels for 13%

profile of v1, /device:TPU:0, one launch (start us, length us, event | category | flops | bytes accessed | tf_op | source)
XLA Modules:
  0.0 800.3 jit_solution(17165654884588324389)
XLA Ops:
  8.1 1.7 maximum_maximum_fusion
  11.4 2.1 constant_dynamic-slice_fusion.1
  13.5 1.2 copy.72
  14.6 1.8 collective-permute-start
  17.6 3.0 collective-permute-start.1
  20.6 2.3 collective-permute-start.2
  25.7 17.8 %collective-permute-done.1 = bf16[512,768]{0,1:T(8,128)(2,1)} collective-permute-done((bf16[512,768]{0,1:T(8,128)(2,1)}, bf16[512,768]{0,1:T(8,128)(2,1)}, u32[]{:S(2)}, u32[]{:S(2)}) %collective-permute-start.1) | collective-permute-done | bytes 786464 | tf_op jit(solution)/shard_map/ppermute | solution.py:196
  43.5 2.1 constant_dynamic-update-slice_fusion
  45.6 43.7 %all-gather.9.cloned.1.call-done = bf16[3584,768]{1,0:T(8,128)(2,1)} async-done(((bf16[112,768]{1,0:T(8,128)(2,1)}), bf16[3584,768]{1,0:T(8,128)(2,1)}) %all-gather.9.cloned.1.call-update) | async-done | bytes 5505040 | tf_op jit(solution)/shard_map/all_gather | solution.py:208
  89.3 4.6 copy.107
  94.1 2.2 copy-done
  97.0 1.8 copy-done.6
  98.7 5.4 fusion.66
  107.0 1.3 fusion.62
  108.3 2.2 pad_maximum_fusion.2
  110.7 1.2 copy.81
  111.9 7.4 collective-permute-start.6
  119.3 1.2 copy.82
  120.5 2.0 collective-permute-start.7
  125.8 1.4 slice.140
  127.2 1.3 copy.77
  129.9 3.9 fusion.61
  133.8 37.1 %attend_forward.1 = (bf16[768,1024]{1,0:T(8,128)(2,1)}, f32[12,1,1024]{2,1,0:T(1,128)}) custom-call(bf16[768,1024]{1,0:T(8,128)(2,1)} %bitcast.189, bf16[16,1024]{1,0:T(8,128)(2,1)} %convert_convert_fusion.refs_1_.refs_4_, bf16[768,1024]{1,0:T(8,128)(2,1)} %bitcast.178, bf16[768,1024]{1,0:T(8,128)(2,1)} %get-tuple-element.95.refs_3_.refs_6_, ...), custom_call_target="tpu_custom_call" | custom-call | flops 25769803776 | bytes 9437184 | tf_op jit(solution)/shard_map/attend_forward/pallas_call | solution.py:69
  170.9 3.3 fusion.60
  174.5 1.7 fusion.22
  176.2 10.4 %fusion.67 = f32[1024,4,768]{2,0,1:T(8,128)} fusion(bf16[1024,768,1]{0,1,2:T(8,128)(2,1)} %fusion.22, bf16[4,768,768]{2,1,0:T(8,128)(2,1)} %bitcast.209), kind=kOutput, calls=%fused_computation.170 | convolution fusion | flops 4831838208 | bytes 18874368 | tf_op jit(solution)/shard_map/td,jdf->jtf/dot_general | solution.py:283
  186.6 45.2 %all-gather.13.cloned.1.call-done = bf16[3072,768]{1,0:T(8,128)(2,1)} async-done(((bf16[96,768]{1,0:T(8,128)(2,1)}), bf16[3072,768]{1,0:T(8,128)(2,1)}) %all-gather.13.cloned.1.call-update) | async-done | bytes 4718608 | tf_op jit(solution)/shard_map/all_gather | solution.py:208
  231.8 14.6 %fusion.3 = (bf16[4,1024,768]{2,1,0:T(8,128)(2,1)}, f32[1024,4,768]{2,0,1:T(8,128)}) fusion(f32[1024,4,768]{2,0,1:T(8,128)} %fusion.67, bf16[1024,768,1]{0,1,2:T(8,128)(2,1)} %fusion.22, bf16[4,768,768]{2,1,0:T(8,128)(2,1)} %bitcast.211), kind=kOutput, calls=%fused_computation.6 | convolution fusion | flops 4850712576 | bytes 37748736 | tf_op jit(solution)/shard_map/td,jdf->jtf/dot_general | solution.py:284
  246.4 50.7 %all-gather.15.cloned.1.call-done = bf16[3072,768]{1,0:T(8,128)(2,1)} async-done(((bf16[96,768]{1,0:T(8,128)(2,1)}), bf16[3072,768]{1,0:T(8,128)(2,1)}) %all-gather.15.cloned.1.call-update) | async-done | bytes 4718608 | tf_op jit(solution)/shard_map/all_gather | solution.py:208
  297.1 8.9 %fusion.65 = (f32[1024]{0:T(1024)S(1)}, f32[1024,768]{0,1:T(8,128)S(1)}) fusion(bf16[4,1024,768]{2,1,0:T(8,128)(2,1)} %get-tuple-element.120, bf16[4,768,768]{2,1,0:T(8,128)(2,1)} %bitcast.213, f32[768]{0:T(1024)S(1)} %add.158, f32[768]{0:T(1024)S(1)} %mul.231, f32[1024]{0:T(1024)S(1)} %add_rsqrt_fusion.1, f32[1024,768]{0,1:T(8,128)S(1)} %get-tuple-element.82, ...), kind=kOutput, calls=%fused_computation.168 | convolution fusion | flops 4836555776 | bytes 17319936 | tf_op jit(solution)/shard_map/jtf,jdf->td/dot_general | solution.py:288
  306.4 5.0 fusion.18
  311.5 8.8 %convolution_convert_fusion.1 = bf16[4,768,768]{1,2,0:T(8,128)(2,1)} fusion(bf16[4,1024,768]{2,1,0:T(8,128)(2,1)S(1)} %copy-done.25, f32[1024,768]{0,1:T(8,128)S(1)} %get-tuple-element.123, f32[1024]{0:T(1024)S(1)} %broadcast_multiply_fusion.2, f32[1024]{0:T(1024)S(1)} %broadcast_multiply_fusion.3, f32[768]{0:T(1024)S(1)} %mul.239, ...), kind=kOutput, calls=%fused_computation.66 | convolution fusion | flops 4843634688 | bytes 15748096 | tf_op jit(solution)/shard_map/td,jtf->jdf/dot_general | solution.py:304
  320.3 20.0 %fusion.2 = (bf16[4,1024,768]{2,1,0:T(8,128)(2,1)}, bf16[4,1024,768]{2,1,0:T(8,128)(2,1)}) fusion(f32[1024,4,768]{2,0,1:T(8,128)} %fusion.67, f32[1024,4,768]{2,0,1:T(8,128)} %get-tuple-element.121, bf16[4,768,768]{2,1,0:T(8,128)(2,1)} %bitcast.214, f32[1024]{0:T(1024)S(1)} %broadcast_multiply_fusion.2, f32[1024,768]{0,1:T(8,128)} %copy-done.1, ...), kind=kOutput, calls=%fused_computation.4 | convolution fusion | flops 4882169856 | bytes 47205376 | tf_op jit(solution)/shard_map/td,jdf->jtf/dot_general | solution.py:296
  340.4 9.2 %convolution_convert_fusion.2 = bf16[4,768,768]{1,2,0:T(8,128)(2,1)} fusion(bf16[1024,768,1]{0,1,2:T(8,128)(2,1)} %fusion.22, bf16[4,1024,768]{2,1,0:T(8,128)(2,1)} %get-tuple-element.85), kind=kOutput, calls=%fused_computation.67 | convolution fusion | flops 4834197504 | bytes 12582912 | tf_op jit(solution)/shard_map/td,jtf->jdf/dot_general | solution.py:304
  349.6 9.1 %fusion.68 = f32[1024,768,1]{0,1,2:T(8,128)S(1)} fusion(bf16[4,1024,768]{2,1,0:T(8,128)(2,1)} %get-tuple-element.86, bf16[4,768,768]{2,1,0:T(8,128)(2,1)} %bitcast.210), kind=kOutput, calls=%fused_computation.171 | convolution fusion | flops 4831838208 | bytes 14155776 | tf_op jit(solution)/shard_map/jtf,jdf->td/dot_general | solution.py:299
  358.8 10.9 %multiply_reduce_fusion = (bf16[768]{0:T(1024)(128)(2,1)S(1)}, f32[1024]{0:T(1024)S(1)}, f32[1024]{0:T(1024)S(1)}, bf16[768]{0:T(1024)(128)(2,1)S(1)}, f32[1024,768]{0,1:T(8,128)S(1)}) fusion(f32[1024,768]{0,1:T(8,128)S(1)} %get-tuple-element.82, f32[1024]{0:T(1024)S(1)} %add_rsqrt_fusion.1, f32[1024]{0:T(1024)S(1)} %broadcast_multiply_fusion.5, ...), kind=kOutput, calls=%fused_computation.48 | convolution fusion | flops 4849135616 | bytes 25207808 | tf_op jit(solution)/shard_map/jtf,jdf->td/dot_general | solution.py:300
  371.0 2.6 convolution_convert_fusion.4.refs_1_
  375.1 6.7 convolution_convert_fusion.3
  381.9 70.8 %attend_backward.1 = (f32[768,1024]{1,0:T(8,128)}, f32[768,1024]{1,0:T(8,128)}, bf16[768,1024]{1,0:T(8,128)(2,1)}, f32[768,1024]{1,0:T(8,128)}, bf16[768,1024]{1,0:T(8,128)(2,1)}) custom-call(bf16[768,1024]{1,0:T(8,128)(2,1)} %bitcast.190, bf16[768,1024]{1,0:T(8,128)(2,1)} %convolution_convert_fusion.4.refs_1_, bf16[768,1024]{1,0:T(8,128)(2,1)} %get-tuple-element.19.refs_2_, ...), custom_call_target="tpu_custom_call" | custom-call | flops 48318382080 | bytes 18874368 | tf_op jit(solution)/shard_map/attend_backward/pallas_call | solution.py:136
  452.7 3.9 pad_maximum_fusion.3
  456.8 1.3 reduce.1
  458.2 1.3 reduce.2
  460.1 4.0 convolution_convert_fusion.5
  464.6 1.2 convert_add_fusion
  469.0 8.3 %convolution_convert_fusion = bf16[2304,768]{1,0:T(8,128)(2,1)S(1)} fusion(bf16[1024,768]{0,1:T(8,128)(2,1)} %constant_dynamic-update-slice_fusion, bf16[768,1024]{1,0:T(8,128)(2,1)S(1)} %get-tuple-element.93, bf16[1536,1024]{1,0:T(8,128)(2,1)S(1)} %bitcast.187), kind=kOutput, calls=%fused_computation.22 | convolution fusion | flops 3635085312 | bytes 9830400 | tf_op jit(solution)/shard_map/dot_general | solution.py:21
  478.0 2.9 copy.89
  480.9 1.4 copy-done.4
  482.2 1.3 fusion.64
  483.5 7.4 collective-permute-start.4
  490.9 1.9 collective-permute-start.5
  492.8 6.6 add_convert_fusion
  499.6 1.6 collective-permute-start.9
  501.3 22.5 %collective-permute-done.5 = bf16[512,768]{0,1:T(8,128)(2,1)} collective-permute-done((bf16[512,768]{0,1:T(8,128)(2,1)}, bf16[512,768]{0,1:T(8,128)(2,1)}, u32[]{:S(2)}, u32[]{:S(2)}) %collective-permute-start.5) | collective-permute-done | bytes 786464 | tf_op jit(solution)/shard_map/ppermute | solution.py:202
  523.8 2.9 fusion.27
  526.7 1.6 copy.90
  528.3 13.9 %collective-permute-done.10 = bf16[512,768]{0,1:T(8,128)(2,1)} collective-permute-done((bf16[512,768]{0,1:T(8,128)(2,1)S(1)}, bf16[512,768]{0,1:T(8,128)(2,1)}, u32[]{:S(2)}, u32[]{:S(2)}) %collective-permute-start.10) | collective-permute-done | bytes 786464 | tf_op jit(solution)/shard_map/ppermute | solution.py:202
  542.1 2.8 fusion.24
  544.9 1.6 copy.91
  546.5 1.6 convert_bitcast_fusion
  548.1 15.0 %reduce-scatter.9.cloned.1.call-done = bf16[1,96,768]{2,1,0:T(8,128)(2,1)} async-done(((bf16[32,96,768]{2,1,0:T(8,128)(2,1)}), bf16[1,96,768]{2,1,0:T(8,128)(2,1)}) %reduce-scatter.9.cloned.1.call-update) | async-done | bytes 147472 | tf_op jit(solution)/shard_map/reduce_scatter | solution.py:212
  563.2 1.6 bitcast_convert_fusion
  564.8 109.5 %reduce-scatter.7.cloned.1.call-done = bf16[1,96,768]{2,1,0:T(8,128)(2,1)} async-done(((bf16[32,96,768]{2,1,0:T(8,128)(2,1)}), bf16[1,96,768]{2,1,0:T(8,128)(2,1)}) %reduce-scatter.7.cloned.1.call-update) | async-done | bytes 147472 | tf_op jit(solution)/shard_map/reduce_scatter | solution.py:212
  674.3 1.6 bitcast_convert_fusion.1
  676.0 114.4 %reduce-scatter.5.cloned.1.call-done = bf16[1,112,768]{2,1,0:T(8,128)(2,1)} async-done(((bf16[32,112,768]{2,1,0:T(8,128)(2,1)}), bf16[1,112,768]{2,1,0:T(8,128)(2,1)}) %reduce-scatter.5.cloned.1.call-update) | async-done | bytes 172048 | tf_op jit(solution)/shard_map/reduce_scatter | solution.py:212
  (155 shorter events, 26.8 us)
Async XLA Ops:
  7.2 82.1 %all-gather.9.cloned.1.call-start = ((), (), s32[]{:S(2)}) async-start(), calls=%async_computation.8 | async-start | bytes 5677056 | tf_op jit(solution)/shard_map/all_gather | solution.py:208
  9.8 166.4 %all-gather.11.cloned.1.call-start = ((), (), s32[]{:S(2)}) async-start(), calls=%async_computation.9 | async-start | bytes 4866048 | tf_op jit(solution)/shard_map/all_gather | solution.py:208
  10.6 221.3 %all-gather.13.cloned.1.call-start = ((), (), s32[]{:S(2)}) async-start(), calls=%async_computation.10 | async-start | bytes 4866048 | tf_op jit(solution)/shard_map/all_gather | solution.py:208
  11.3 285.8 %all-gather.15.cloned.1.call-start = ((), (), s32[]{:S(2)}) async-start(), calls=%async_computation.11 | async-start | bytes 4866048 | tf_op jit(solution)/shard_map/all_gather | solution.py:208
  13.4 7.2 copy-start.22
  13.4 7.1 copy-start.23
  14.6 10.1 %collective-permute-start = (bf16[512,768]{0,1:T(8,128)(2,1)}, bf16[512,768]{0,1:T(8,128)(2,1)S(1)}, u32[]{:S(2)}, u32[]{:S(2)}) collective-permute-start(bf16[512,768]{0,1:T(8,128)(2,1)} %bitcast.194), channel_id=1, source_target_pairs={{0,0},{1,1},{2,4},{3,5},{4,2},{5,3},{6,6},{7,7},{8,8},{9,9},{10,12... | collective-permute-start | bytes 2359304 | tf_op jit(solution)/shard_map/ppermute | solution.py:196
  17.6 25.9 %collective-permute-start.1 = (bf16[512,768]{0,1:T(8,128)(2,1)}, bf16[512,768]{0,1:T(8,128)(2,1)}, u32[]{:S(2)}, u32[]{:S(2)}) collective-permute-start(bf16[512,768]{0,1:T(8,128)(2,1)} %bitcast.195), channel_id=1, source_target_pairs={{0,1},{1,0},{2,5},{3,4},{4,3},{5,2},{6,7},{7,6},{8,9},{9,8},{10,13... | collective-permute-start | bytes 2359304 | tf_op jit(solution)/shard_map/ppermute | solution.py:196
  20.6 3.2 collective-permute-start.2
  24.7 80.8 %copy-start.16 = (f32[32,1024]{1,0:T(8,128)}, f32[32,1024]{1,0:T(8,128)S(1)}, u32[]{:S(2)}) copy-start(f32[32,1024]{1,0:T(8,128)S(1)} %get-tuple-element.114) | copy-start | bytes 393220
  24.7 80.8 %copy-start.18 = (f32[32,1024]{1,0:T(8,128)}, f32[32,1024]{1,0:T(8,128)S(1)}, u32[]{:S(2)}) copy-start(f32[32,1024]{1,0:T(8,128)S(1)} %get-tuple-element.115) | copy-start | bytes 393220
  93.8 2.4 copy-start
  96.9 1.8 copy-start.6
  105.5 2.8 copy-start.3
  108.3 2.2 copy-start.5
  110.5 19.4 %collective-permute-start.3 = (bf16[1536,1024]{1,0:T(8,128)(2,1)}, bf16[1536,1024]{1,0:T(8,128)(2,1)}, u32[]{:S(2)}, u32[]{:S(2)}) collective-permute-start(bf16[1536,1024]{1,0:T(8,128)(2,1)} %pad_maximum_fusion.2), channel_id=1, source_target_pairs={{0,4},{4,0},{1,5},{5,1},{2,6},{6,2},{3,7},{7,3},{8,12},{12,8},{9,1... | collective-permute-start | bytes 9437192 | tf_op jit(solution)/shard_map/ppermute | solution.py:269
  111.9 194.5 %collective-permute-start.6 = (bf16[512,768]{0,1:T(8,128)(2,1)}, bf16[512,768]{0,1:T(8,128)(2,1)}, u32[]{:S(2)}, u32[]{:S(2)}) collective-permute-start(bf16[512,768]{0,1:T(8,128)(2,1)} %bitcast.31), channel_id=1, source_target_pairs={{0,0},{1,1},{2,4},{3,5},{4,2},{5,3},{6,6},{7,7},{8,8},{9,9},{10,12... | collective-permute-start | bytes 2359304 | tf_op jit(solution)/shard_map/ppermute | solution.py:196
  120.5 185.9 %collective-permute-start.7 = (bf16[512,768]{0,1:T(8,128)(2,1)}, bf16[512,768]{0,1:T(8,128)(2,1)}, u32[]{:S(2)}, u32[]{:S(2)}) collective-permute-start(bf16[512,768]{0,1:T(8,128)(2,1)} %bitcast.32), channel_id=1, source_target_pairs={{0,1},{1,0},{2,5},{3,4},{4,3},{5,2},{6,7},{7,6},{8,9},{9,8},{10,13... | collective-permute-start | bytes 2359304 | tf_op jit(solution)/shard_map/ppermute | solution.py:196
  122.5 423.9 %reduce-scatter.11.cloned.1.call-start = ((), (), s32[]{:S(2)}) async-start(), calls=%async_computation.7 | async-start | bytes 4866048 | tf_op jit(solution)/shard_map/reduce_scatter | solution.py:212
  133.8 37.1 %copy-start.20 = (bf16[8,4,24,768]{3,2,1,0:T(8,128)(2,1)S(1)}, bf16[8,4,24,768]{3,2,1,0:T(8,128)(2,1)}, u32[]{:S(2)}) copy-start(bf16[8,4,24,768]{3,2,1,0:T(8,128)(2,1)} %copy.77) | copy-start | bytes 3538948
  306.0 5.5 copy-start.1
  306.4 5.1 copy-start.25
  320.3 242.9 %reduce-scatter.9.cloned.1.call-start = ((), (), s32[]{:S(2)}) async-start(), calls=%async_computation.6 | async-start | bytes 4866048 | tf_op jit(solution)/shard_map/reduce_scatter | solution.py:212
  349.6 324.8 %reduce-scatter.7.cloned.1.call-start = ((), (), s32[]{:S(2)}) async-start(), calls=%async_computation.5 | async-start | bytes 4866048 | tf_op jit(solution)/shard_map/reduce_scatter | solution.py:212
  349.6 9.2 %copy-start.2 = (f32[1024,768]{0,1:T(8,128)S(1)}, f32[1024,768]{0,1:T(8,128)}, u32[]{:S(2)}) copy-start(f32[1024,768]{0,1:T(8,128)} %copy-done.1) | copy-start | bytes 9437188
  369.7 1.3 copy-start.21
  369.7 3.9 slice-start
  370.9 2.6 copy-start.11
  370.9 3.5 copy-start.15
  371.0 4.1 slice-start.1
  381.8 408.6 %reduce-scatter.5.cloned.1.call-start = ((), (), s32[]{:S(2)}) async-start(), calls=%async_computation.4 | async-start | bytes 5677056 | tf_op jit(solution)/shard_map/reduce_scatter | solution.py:212
  452.7 7.2 copy-start.24
  456.6 7.5 collective-permute-start.8
  460.1 4.1 copy-start.7
  460.1 4.5 copy-start.8
  464.6 2.0 copy-start.12
  465.7 3.3 copy-start.13
  466.5 1.1 copy-start.17
  466.5 1.1 copy-start.19
  469.0 8.3 %copy-start.9 = (bf16[24,2,32,1024]{3,2,1,0:T(8,128)(2,1)}, bf16[24,2,32,1024]{3,2,1,0:T(8,128)(2,1)S(1)}, u32[]{:S(2)}) copy-start(bf16[24,2,32,1024]{3,2,1,0:T(8,128)(2,1)S(1)} %pad_maximum_fusion.4) | copy-start | bytes 9437188
  480.8 1.4 copy-start.4
  480.8 12.0 %copy-start.14 = (bf16[768,1024]{1,0:T(8,128)(2,1)S(1)}, bf16[768,1024]{1,0:T(8,128)(2,1)}, u32[]{:S(2)}) copy-start(bf16[768,1024]{1,0:T(8,128)(2,1)} %copy-done.13) | copy-start | bytes 4718596
  480.9 12.0 %copy-start.10 = (bf16[24,2,32,1024]{3,2,1,0:T(8,128)(2,1)S(1)}, bf16[24,2,32,1024]{3,2,1,0:T(8,128)(2,1)}, u32[]{:S(2)}) copy-start(bf16[24,2,32,1024]{3,2,1,0:T(8,128)(2,1)} %copy-done.9) | copy-start | bytes 9437188
  483.5 17.8 %collective-permute-start.4 = (bf16[512,768]{0,1:T(8,128)(2,1)}, bf16[512,768]{0,1:T(8,128)(2,1)}, u32[]{:S(2)}, u32[]{:S(2)}) collective-permute-start(bf16[512,768]{0,1:T(8,128)(2,1)} %get-tuple-element.103), channel_id=1, source_target_pairs={{0,0},{1,1},{4,2},{5,3},{2,4},{3,5},{6,6},{7,7},{8,8},{9,9},{12,10... | collective-permute-start | bytes 2359304 | tf_op jit(solution)/shard_map/ppermute | solution.py:202
  490.9 32.9 %collective-permute-start.5 = (bf16[512,768]{0,1:T(8,128)(2,1)}, bf16[512,768]{0,1:T(8,128)(2,1)}, u32[]{:S(2)}, u32[]{:S(2)}) collective-permute-start(bf16[512,768]{0,1:T(8,128)(2,1)} %get-tuple-element.102), channel_id=1, source_target_pairs={{1,0},{0,1},{5,2},{4,3},{3,4},{2,5},{7,6},{6,7},{9,8},{8,9},{13,10... | collective-permute-start | bytes 2359304 | tf_op jit(solution)/shard_map/ppermute | solution.py:202
  499.6 28.7 %collective-permute-start.9 = (bf16[512,768]{0,1:T(8,128)(2,1)S(1)}, bf16[512,768]{0,1:T(8,128)(2,1)}, u32[]{:S(2)}, u32[]{:S(2)}) collective-permute-start(bf16[512,768]{0,1:T(8,128)(2,1)S(1)} %get-tuple-element.99), channel_id=1, source_target_pairs={{0,0},{1,1},{4,2},{5,3},{2,4},{3,5},{6,6},{7,7},{8,8},{9,9},{12,10... | collective-permute-start | bytes 2359304 | tf_op jit(solution)/shard_map/ppermute | solution.py:202
  501.1 41.0 %collective-permute-start.10 = (bf16[512,768]{0,1:T(8,128)(2,1)S(1)}, bf16[512,768]{0,1:T(8,128)(2,1)}, u32[]{:S(2)}, u32[]{:S(2)}) collective-permute-start(bf16[512,768]{0,1:T(8,128)(2,1)S(1)} %get-tuple-element.98), channel_id=1, source_target_pairs={{1,0},{0,1},{5,2},{4,3},{3,4},{2,5},{7,6},{6,7},{9,8},{8,9},{13,10... | collective-permute-start | bytes 2359304 | tf_op jit(solution)/shard_map/ppermute | solution.py:202
Sparse Core Ops, SparseCore 0:
  11.5 77.7 all-gather.8
  92.2 75.2 all-gather.10
  170.3 61.4 all-gather.12
  234.6 62.4 all-gather.14
  320.4 105.8 reduce-scatter.10
  432.5 130.5 reduce-scatter.8
  568.6 105.6 reduce-scatter.6
  680.8 109.5 reduce-scatter.4

commit v2 on v1

v2 whole, which is shorter than its diff:
```python
import functools

import jax
import jax.numpy as jnp
from jax import lax
from jax.experimental import pallas as pl
from jax.experimental.pallas import tpu as pltpu
import numpy as np
from jax.sharding import Mesh, PartitionSpec as P

HEADS = 12
HEAD_DIM = 64
EPSILON = 1e-05
AUG = 16
PIECES = 4
COST = 16
MASK = 2.0**99
LOW = jnp.bfloat16
WIDE = jnp.float32
SWAP = [(0, 1), (1, 0)]


def dot(a, b, ca, cb):
    return lax.dot_general(a, b, (((ca,), (cb,)), ((), ())), preferred_element_type=WIDE)


def cost(flops=0, bytes_accessed=0, transcendentals=0, scale=COST):
    return pl.CostEstimate(
        flops=flops // scale, bytes_accessed=bytes_accessed // scale, transcendentals=transcendentals // scale
    )


def split3(x):
    high = x.astype(LOW)
    rest = x - high.astype(WIDE)
    middle = rest.astype(LOW)
    return [high, middle, (rest - middle.astype(WIDE)).astype(LOW)]


def put_rows(base, at, rows):
    index = lax.broadcasted_iota(jnp.int32, base.shape, 0)
    out = base.astype(WIDE)
    for i, row in enumerate(rows):
        out = jnp.where(index == at + i, row.astype(WIDE), out)
    return out.astype(LOW)


def ones_row(n):
    return jnp.ones((1, n), WIDE)


def forward_kernel(parts, *refs):
    q_ref, qa_ref = refs[:2]
    refs = refs[: 2 + 3 * parts] + refs[-3:]
    k_refs, v_refs, ka_refs = refs[2 : 2 + parts], refs[2 + parts : 2 + 2 * parts], refs[2 + 2 * parts : 2 + 3 * parts]
    o_ref, lse_ref, keys = refs[2 + 3 * parts :]
    at = 0
    values = []
    for k_ref, v_ref, ka_ref in zip(k_refs, v_refs, ka_refs):
        n = k_ref.shape[1]
        keys[at : at + n] = jnp.concatenate([k_ref[...], ka_ref[...]], axis=0).T
        values.append(v_ref[...])
        at += n
    queries = jnp.concatenate([q_ref[...], qa_ref[...]], axis=0)
    scores = dot(keys[...], queries, 1, 0)
    top = jnp.max(scores, axis=0, keepdims=True)
    terms = jnp.exp(scores - top)
    total = jnp.sum(terms, axis=0, keepdims=True)
    result = dot(jnp.concatenate(values, axis=1), terms.astype(LOW), 1, 0)
    o_ref[...] = (result / total).astype(LOW)
    lse_ref[...] = (top + jnp.log(total)).reshape(1, 1, -1)


def head_block(n, first):
    return pl.BlockSpec((HEAD_DIM, n), lambda h: (h + first, 0))


def whole_block(rows, n):
    return pl.BlockSpec((rows, n), lambda h: (0, 0))


def attend_forward(q, qa, kvs, kas, after, first, heads):
    parts, nq = len(kvs), q.shape[1]
    sizes = [kv.shape[1] for kv in kvs]
    nk = sum(sizes)
    return pl.pallas_call(
        functools.partial(forward_kernel, parts),
        grid=(heads,),
        in_specs=[head_block(nq, first), whole_block(AUG, nq)]
        + [head_block(n, first) for n in sizes]
        + [head_block(n, first + HEADS) for n in sizes]
        + [whole_block(AUG, n) for n in sizes]
        + [pl.BlockSpec(memory_space=pl.ANY)] * len(after),
        out_specs=[head_block(nq, 0), pl.BlockSpec((1, 1, nq), lambda h: (h, 0, 0))],
        out_shape=[
            jax.ShapeDtypeStruct((heads * HEAD_DIM, nq), LOW),
            jax.ShapeDtypeStruct((heads, 1, nq), WIDE),
        ],
        scratch_shapes=[pltpu.VMEM((nk, HEAD_DIM + AUG), LOW)],
        compiler_params=pltpu.CompilerParams(vmem_limit_bytes=56 << 20),
        cost_estimate=cost(
            flops=16 * heads * nq * nk * HEAD_DIM,
            bytes_accessed=4 * heads * HEAD_DIM * (nq + nk),
            transcendentals=heads * nq * nk,
        ),
        name="attend_forward",
    )(q, qa, *kvs, *kvs, *kas, *after)


def backward_kernel(parts, *refs):
    q_ref, g_ref, o_ref, lse_ref, qa_ref = refs[:5]
    refs = refs[: 5 + 3 * parts] + refs[-3 - parts :]
    k_refs, v_refs, ka_refs = refs[5 : 5 + parts], refs[5 + parts : 5 + 2 * parts], refs[5 + 2 * parts : 5 + 3 * parts]
    dq_ref = refs[5 + 3 * parts]
    dkv_refs = refs[6 + 3 * parts : 6 + 4 * parts]
    keys, values = refs[6 + 4 * parts :]
    nq = q_ref.shape[1]
    at = 0
    key_list = []
    for k_ref, v_ref, ka_ref in zip(k_refs, v_refs, ka_refs):
        n = k_ref.shape[1]
        keys[at : at + n] = jnp.concatenate(
            [k_ref[...], put_rows(ka_ref[...], 2, [ones_row(n)] * 3)], axis=0
        ).T
        values[at : at + n] = jnp.concatenate(
            [v_ref[...], put_rows(jnp.zeros((AUG, n), LOW), 0, [ones_row(n)] * 3)], axis=0
        ).T
        key_list.append(k_ref[...])
        at += n
    grads, queries = g_ref[...], q_ref[...]
    delta = jnp.sum(grads.astype(WIDE) * o_ref[...].astype(WIDE), axis=0, keepdims=True)
    query_aug = jnp.concatenate([queries, put_rows(qa_ref[...], 2, split3(-lse_ref[0]))], axis=0)
    grad_aug = jnp.concatenate([grads, put_rows(jnp.zeros((AUG, nq), LOW), 0, split3(-delta))], axis=0)
    probs = jnp.exp(dot(keys[...], query_aug, 1, 0))
    prob_grads = dot(values[...], grad_aug, 1, 0)
    low_probs = probs.astype(LOW)
    score_grads = (probs * prob_grads).astype(LOW)
    dq_ref[...] = dot(jnp.concatenate(key_list, axis=1), score_grads, 1, 0) * HEAD_DIM ** (-0.5)
    dv = dot(grads, low_probs, 1, 1)
    dk = dot(queries, score_grads, 1, 1)
    at = 0
    for dkv_ref in dkv_refs:
        n = dkv_ref.shape[2]
        dkv_ref[0] = dk[:, at : at + n].astype(dkv_ref.dtype)
        dkv_ref[1] = dv[:, at : at + n].astype(dkv_ref.dtype)
        at += n


def attend_backward(q, g, o, lse, qa, kvs, kas, types, after, first, heads):
    parts, nq = len(kvs), q.shape[1]
    sizes = [kv.shape[1] for kv in kvs]
    nk = sum(sizes)
    width = heads * HEAD_DIM
    out = pl.pallas_call(
        functools.partial(backward_kernel, parts),
        grid=(heads,),
        in_specs=[
            head_block(nq, first),
            head_block(nq, first),
            head_block(nq, 0),
            pl.BlockSpec((1, 1, nq), lambda h: (h, 0, 0)),
            whole_block(AUG, nq),
        ]
        + [head_block(n, first) for n in sizes]
        + [head_block(n, first + HEADS) for n in sizes]
        + [whole_block(AUG, n) for n in sizes]
        + [pl.BlockSpec(memory_space=pl.ANY)] * len(after),
        out_specs=[head_block(nq, 0)]
        + [pl.BlockSpec((2, HEAD_DIM, n), lambda h: (0, h, 0)) for n in sizes],
        out_shape=[jax.ShapeDtypeStruct((width, nq), WIDE)]
        + [jax.ShapeDtypeStruct((2, width, n), t) for n, t in zip(sizes, types)],
        scratch_shapes=[pltpu.VMEM((nk, HEAD_DIM + AUG), LOW)] * 2,
        compiler_params=pltpu.CompilerParams(vmem_limit_bytes=60 << 20),
        cost_estimate=cost(
            flops=30 * heads * nq * nk * HEAD_DIM,
            bytes_accessed=8 * width * (nq + nk),
            transcendentals=heads * nq * nk,
        ),
        name="attend_backward",
    )(q, g, o, lse, qa, *kvs, *kvs, *kas, *after)
    return out[0], out[1:]


def turn(values, cosine, sine):
    heads = values.reshape(-1, HEAD_DIM, values.shape[-1])
    half = HEAD_DIM // 2
    front, behind = heads[:, :half], heads[:, half:]
    turned = jnp.concatenate([front * cosine - behind * sine, behind * cosine + front * sine], axis=1)
    return turned.reshape(values.shape)


def project_kernel(kinds, w_ref, x_ref, cos_ref, sin_ref, o_ref):
    made = dot(w_ref[...], x_ref[...], 1, 1)
    for i, kind in enumerate(kinds):

        @pl.when(pl.program_id(0) == i)
        def _():
            if kind == "v":
                o_ref[...] = made.astype(LOW)
            else:
                low = turn(made, cos_ref[...], sin_ref[...]).astype(LOW)
                o_ref[...] = low * jnp.asarray(HEAD_DIM ** (-0.5), LOW) if kind == "q" else low


def project(qkv_t, x, cosine, sine, kinds, first):
    n, width = x.shape
    return pl.pallas_call(
        functools.partial(project_kernel, kinds),
        grid=(len(kinds),),
        in_specs=[
            pl.BlockSpec((width, width), lambda i: (i + first, 0)),
            pl.BlockSpec((n, width), lambda i: (0, 0)),
            whole_block(HEAD_DIM // 2, n),
            whole_block(HEAD_DIM // 2, n),
        ],
        out_specs=pl.BlockSpec((width, n), lambda i: (i, 0)),
        out_shape=jax.ShapeDtypeStruct((len(kinds) * width, n), LOW),
        compiler_params=pltpu.CompilerParams(vmem_limit_bytes=40 << 20),
        cost_estimate=cost(
            flops=2 * len(kinds) * width * width * n, bytes_accessed=6 * width * n, transcendentals=0
        ),
        name="project",
    )(qkv_t, x, cosine, sine)


def norm_forward(values, gain, shift):
    center = jnp.mean(values, axis=-1, keepdims=True)
    centered = values - center
    inverse = lax.rsqrt(jnp.mean(centered * centered, axis=-1, keepdims=True) + EPSILON)
    normed = centered * inverse
    return (normed * gain + shift, normed, inverse)


def norm_backward(grads, normed, inverse, gain):
    scaled = grads * gain
    first_mean = jnp.mean(scaled, axis=-1, keepdims=True)
    second_mean = jnp.mean(scaled * normed, axis=-1, keepdims=True)
    return inverse * (scaled - first_mean - normed * second_mean)


def middle_kernel(pieces, *refs):
    att_refs = refs[:pieces]
    x_ref, top_ref, vec_ref, out_w, gu_w, down_w = refs[pieces : pieces + 6]
    o_ref, low_ref, hid_ref, gug_ref, mix_ref, res_ref, proj_ref, att_ref, sums_ref = refs[pieces + 6 : pieces + 15]
    kept = refs[pieces + 15]
    gain_one, shift_one, gain_two, shift_two = (vec_ref[i : i + 1] for i in range(4))
    blocks, width = down_w.shape[0], down_w.shape[2]
    projected = dot(jnp.concatenate([r[...] for r in att_refs], axis=0), out_w[...], 0, 1)
    x_one, normed_one, inverse_one = norm_forward(x_ref[...].astype(WIDE) + projected, gain_one, shift_one)
    x_low = x_one.astype(LOW)
    low_ref[...] = x_low
    mixed = jnp.zeros_like(x_one)
    for j in range(blocks):
        both = dot(x_low, gu_w[j], 1, 0)
        gate, up = both[:, :width], both[:, width:]
        sigma = 0.5 * jnp.tanh(0.5 * gate) + 0.5
        activated = gate * sigma
        kept[j, :, :width] = up * (sigma + activated * (1.0 - sigma))
        kept[j, :, width:] = activated
        hidden = (activated * up).astype(LOW)
        hid_ref[j] = hidden
        mixed += dot(hidden, down_w[j], 1, 1)
    result, normed_two, inverse_two = norm_forward(x_one + mixed, gain_two, shift_two)
    o_ref[...] = result.astype(LOW)
    grad_top = top_ref[...].astype(WIDE)
    d_resid_two = norm_backward(grad_top, normed_two, inverse_two, gain_two)
    mix_grad = d_resid_two.astype(LOW)
    mix_ref[...] = mix_grad
    d_x_one = d_resid_two
    for j in range(blocks):
        hidden_grad = dot(mix_grad, down_w[j], 1, 0)
        gate_grad = (hidden_grad * kept[j, :, :width]).astype(LOW)
        up_grad = (hidden_grad * kept[j, :, width:]).astype(LOW)
        grads = jnp.concatenate([gate_grad, up_grad], axis=1)
        gug_ref[j] = grads
        d_x_one += dot(grads, gu_w[j], 1, 1)
    d_resid_one = norm_backward(d_x_one, normed_one, inverse_one, gain_one)
    res_ref[...] = d_resid_one
    proj_grad = d_resid_one.astype(LOW)
    proj_ref[...] = proj_grad
    att_ref[...] = dot(out_w[...], proj_grad, 0, 1).astype(LOW)
    sums = jnp.concatenate(
        [
            jnp.sum(v, axis=0, keepdims=True)
            for v in (d_x_one * normed_one, d_x_one, grad_top * normed_two, grad_top)
        ]
        + [jnp.zeros((4, d_x_one.shape[1]), WIDE)],
        axis=0,
    )

    @pl.when(pl.program_id(0) == 0)
    def _():
        sums_ref[...] = sums

    @pl.when(pl.program_id(0) > 0)
    def _():
        sums_ref[...] += sums


def middle(attended, x, grad_top, vectors, out_t, gu, down):
    n, width = x.shape
    blocks, _, units = down.shape
    step = min(n, 256)
    pieces = len(attended)

    def kept_block(shape):
        return pl.BlockSpec(shape, lambda i: (0,) * len(shape), pipeline_mode=pl.Buffered(1))

    rows = pl.BlockSpec((step, width), lambda i: (i, 0))
    return pl.pallas_call(
        functools.partial(middle_kernel, pieces),
        grid=(n // step,),
        in_specs=[pl.BlockSpec((a.shape[0], step), lambda i: (0, i)) for a in attended]
        + [rows, rows]
        + [kept_block(a.shape) for a in (vectors, out_t, gu, down)],
        out_specs=[
            rows,
            rows,
            pl.BlockSpec((blocks, step, units), lambda i: (0, i, 0)),
            pl.BlockSpec((blocks, step, 2 * units), lambda i: (0, i, 0)),
            rows,
            rows,
            rows,
            pl.BlockSpec((width, step), lambda i: (0, i)),
            pl.BlockSpec((8, width), lambda i: (0, 0)),
        ],
        out_shape=[
            jax.ShapeDtypeStruct((n, width), LOW),
            jax.ShapeDtypeStruct((n, width), LOW),
            jax.ShapeDtypeStruct((blocks, n, units), LOW),
            jax.ShapeDtypeStruct((blocks, n, 2 * units), LOW),
            jax.ShapeDtypeStruct((n, width), LOW),
            jax.ShapeDtypeStruct((n, width), WIDE),
            jax.ShapeDtypeStruct((n, width), LOW),
            jax.ShapeDtypeStruct((width, n), LOW),
            jax.ShapeDtypeStruct((8, width), WIDE),
        ],
        scratch_shapes=[pltpu.VMEM((blocks, step, 2 * units), WIDE)],
        compiler_params=pltpu.CompilerParams(vmem_limit_bytes=60 << 20),
        cost_estimate=cost(
            flops=2 * n * width * (2 * width + 6 * blocks * units), bytes_accessed=60 << 20, transcendentals=n * blocks * units
        ),
        name="middle",
    )(*attended, x, grad_top, vectors, out_t, gu, down)


def unturn_kernel(add, *refs):
    dq_ref, own_ref = refs[:2]
    cos_ref, sin_ref, x_ref, grad_ref, g_ref = refs[-5:]
    kind = pl.program_id(0)
    cosine, sine = cos_ref[...], -sin_ref[...]

    def emit(made):
        low = made.astype(LOW)
        grad_ref[0] = low
        g_ref[0] = dot(low, x_ref[...], 1, 0).astype(LOW)

    @pl.when(kind == 0)
    def _():
        emit(turn(dq_ref[...], cosine, sine))

    def total():
        return own_ref[0] + refs[2][0].astype(WIDE) if add else own_ref[0]

    @pl.when(kind == 1)
    def _():
        emit(turn(total(), cosine, sine))

    @pl.when(kind == 2)
    def _():
        emit(total())


def unturn(dq, own, others, cosine, sine, x):
    n, width = x.shape
    count = dq.shape[0]
    pair = pl.BlockSpec((1, count, n), lambda i: (jnp.maximum(i - 1, 0), 0, 0))
    table = whole_block(HEAD_DIM // 2, n)
    return pl.pallas_call(
        functools.partial(unturn_kernel, len(others)),
        grid=(3,),
        in_specs=[whole_block(count, n), pair] + [pair] * len(others) + [table, table, whole_block(n, width)],
        out_specs=[
            pl.BlockSpec((1, count, n), lambda i: (i, 0, 0)),
            pl.BlockSpec((1, count, width), lambda i: (i, 0, 0)),
        ],
        out_shape=[
            jax.ShapeDtypeStruct((3, count, n), LOW),
            jax.ShapeDtypeStruct((3, count, width), LOW),
        ],
        compiler_params=pltpu.CompilerParams(vmem_limit_bytes=30 << 20),
        cost_estimate=cost(flops=6 * n * width * count, bytes_accessed=9 << 20, transcendentals=0),
        name="unturn",
    )(dq, own, *others, cosine, sine, x)


def finish_kernel(groups, *refs):
    res_ref, w_ref = refs[groups : groups + 2]
    in_ref = refs[-1]
    grad = jnp.concatenate([r[kind] for kind in range(3) for r in refs[:groups]], axis=0)
    in_ref[...] = (res_ref[...] + dot(grad, w_ref[...], 0, 0)).astype(LOW)


def finish(grads, resid, qkv_t, after, part, n):
    width = resid.shape[1]
    step = min(n, 256)
    first = part * (n // step)
    rows = pl.BlockSpec((step, width), lambda i: (i + first, 0))
    return pl.pallas_call(
        functools.partial(finish_kernel, len(grads)),
        grid=(n // step,),
        in_specs=[pl.BlockSpec((3, a.shape[1], step), lambda i: (0, 0, i + first)) for a in grads]
        + [rows, pl.BlockSpec(qkv_t.shape, lambda i: (0, 0), pipeline_mode=pl.Buffered(1))]
        + [pl.BlockSpec(memory_space=pl.ANY)] * len(after),
        out_specs=pl.BlockSpec((step, width), lambda i: (i, 0)),
        out_shape=jax.ShapeDtypeStruct((n, width), LOW),
        compiler_params=pltpu.CompilerParams(vmem_limit_bytes=50 << 20),
        cost_estimate=cost(flops=6 * n * width * width, bytes_accessed=12 << 20, transcendentals=0),
        name="finish",
    )(*grads, resid, qkv_t, *after)


def beside_kernel(count, *refs):
    out = refs[-1]
    at = 0
    for ref in refs[:count]:
        n = ref.shape[1]
        out[:, at : at + n] = ref[...]
        at += n


def beside(arrays, after):
    whole = pl.BlockSpec(memory_space=pltpu.VMEM)
    total = sum(a.shape[1] for a in arrays)
    return pl.pallas_call(
        functools.partial(beside_kernel, len(arrays)),
        in_specs=[whole] * len(arrays) + [pl.BlockSpec(memory_space=pl.ANY)] * len(after),
        out_specs=whole,
        out_shape=jax.ShapeDtypeStruct((arrays[0].shape[0], total), arrays[0].dtype),
        name="beside",
    )(*arrays, *after)


def select_kernel(at, x_ref, *refs):
    outs = refs[-x_ref.shape[0] :]
    for k, out in enumerate(outs):
        out[...] = x_ref[at[k]]


def select(x, at, after):
    count = x.shape[0]
    whole = pl.BlockSpec(memory_space=pltpu.VMEM)
    return pl.pallas_call(
        select_kernel,
        in_specs=[pl.BlockSpec(memory_space=pltpu.SMEM), whole] + [pl.BlockSpec(memory_space=pl.ANY)] * len(after),
        out_specs=[whole] * count,
        out_shape=[jax.ShapeDtypeStruct(x.shape[1:], x.dtype)] * count,
        compiler_params=pltpu.CompilerParams(vmem_limit_bytes=10 << 20),
        cost_estimate=cost(flops=0, bytes_accessed=4 * x.size, transcendentals=0),
        name="select",
    )(at, x, *after)


def stack_kernel(count, *refs):
    out = refs[-1]
    at = 0
    for ref in refs[:count]:
        n = ref.shape[0]
        out[at : at + n] = ref[...]
        at += n


def stack(arrays, after=()):
    one = arrays[0]
    total = sum(a.shape[0] for a in arrays)
    whole = pl.BlockSpec(memory_space=pltpu.VMEM)
    return pl.pallas_call(
        functools.partial(stack_kernel, len(arrays)),
        in_specs=[whole] * len(arrays) + [pl.BlockSpec(memory_space=pl.ANY)] * len(after),
        out_specs=whole,
        out_shape=jax.ShapeDtypeStruct((total,) + one.shape[1:], one.dtype),
        compiler_params=pltpu.CompilerParams(vmem_limit_bytes=16 << 20),
        cost_estimate=cost(bytes_accessed=4 * one.size * len(arrays)),
        name="stack",
    )(*arrays, *after)


def arrange_kernel(cuts, place, mine, theirs, *refs):
    near, depth = mine.shape[:2]
    for half, src in enumerate((mine, theirs)):
        for r in range(near):
            spot = place[half * near + r]
            for k in range(depth):
                z = place[2 * near + k]
                for out, (start, size, z_first) in zip(refs[-len(cuts) :], cuts):
                    block = src[r, k, start : start + size]
                    if z_first:
                        out[z, spot] = block
                    else:
                        out[spot, z] = block


def arrange(mine, theirs, place, cuts, after):
    near, depth, _, width = mine.shape
    whole = pl.BlockSpec(memory_space=pltpu.VMEM)
    lead = {True: (depth, 2 * near), False: (2 * near, depth)}
    return pl.pallas_call(
        functools.partial(arrange_kernel, cuts),
        in_specs=[pl.BlockSpec(memory_space=pltpu.SMEM), whole, whole]
        + [pl.BlockSpec(memory_space=pl.ANY)] * len(after),
        out_specs=[whole] * len(cuts),
        out_shape=[
            jax.ShapeDtypeStruct(lead[z_first] + (size, width), mine.dtype) for _, size, z_first in cuts
        ],
        compiler_params=pltpu.CompilerParams(vmem_limit_bytes=30 << 20),
        cost_estimate=cost(flops=0, bytes_accessed=8 * mine.size, transcendentals=0),
        name="arrange",
    )(place, mine, theirs, *after)


def add_low(a, b):
    return (a.astype(WIDE) + b.astype(WIDE)).astype(LOW)


def join_core_kernel(axis, place, mine, got, *refs):
    outs = refs[-2:]
    for i in range(4):
        for t in range(mine.shape[1 - axis]):
            spot = (place[i], t) if axis == 0 else (t, place[i])
            outs[i // 2][i % 2, t] = add_low(mine[spot], got[spot])


def join_far_kernel(keep, got, *refs):
    for i, out in enumerate(refs[-2:]):
        out[...] = add_low(keep[i], got[i])


def join_near_kernel(place, keep, got, *refs):
    for k, out in enumerate(refs[-keep.shape[0] :]):
        out[...] = add_low(keep[place[k]], got[place[k]])


def join(kernel, arrays, shapes, after, scalars=()):
    whole = pl.BlockSpec(memory_space=pltpu.VMEM)
    return pl.pallas_call(
        kernel,
        in_specs=[pl.BlockSpec(memory_space=pltpu.SMEM)] * len(scalars)
        + [whole] * len(arrays)
        + [pl.BlockSpec(memory_space=pl.ANY)] * len(after),
        out_specs=[whole] * len(shapes),
        out_shape=[jax.ShapeDtypeStruct(shape, LOW) for shape in shapes],
        compiler_params=pltpu.CompilerParams(vmem_limit_bytes=24 << 20),
        cost_estimate=cost(bytes_accessed=8 * arrays[0].size),
        name="join",
    )(*scalars, *arrays, *after)


def side_kernel(pieces, core_ref, mix_ref, hid_ref, proj_ref, *refs):
    att_refs = refs[:pieces]
    norm_ref, mine, send, turned, result, side = refs[pieces:]
    j = pl.program_id(0)
    lines, count = mine.shape[2], mix_ref.shape[1] // (2 * mine.shape[1])
    extra = norm_ref.shape[2]
    few = lines - count - extra

    @pl.when(j == 0)
    def _():
        turned[...] = mix_ref[...].T
        side[...] = dot(proj_ref[...].T, jnp.concatenate([r[...] for r in att_refs], axis=0), 1, 1)

    result[...] = dot(turned[...], hid_ref[0], 1, 0)
    for p in range(mine.shape[1]):
        for rel, out in enumerate((mine, send)):
            dp = 2 * p + (core_ref[0] + rel) % 2
            rows = result[pl.ds(pl.multiple_of(dp * count, 8), count)]
            small = side[pl.ds(pl.multiple_of((dp * pl.num_programs(0) + j) * few, 8), few)]
            out[0, p, :count] = rows.astype(LOW)
            out[0, p, count:] = jnp.concatenate([small, norm_ref[dp, 0]], axis=0).astype(LOW)


def side_grads(core, mix_grad, hidden, proj_grad, attended, norms, lines):
    n, width = mix_grad.shape
    blocks, chips = hidden.shape[0], norms.shape[0] // 2
    whole = pl.BlockSpec((n, width), lambda j: (0, 0))
    out = pl.BlockSpec((1, chips, lines, width), lambda j: (j, 0, 0, 0))
    return pl.pallas_call(
        functools.partial(side_kernel, len(attended)),
        grid=(blocks,),
        in_specs=[
            pl.BlockSpec(memory_space=pltpu.SMEM),
            whole,
            pl.BlockSpec((1, n, width), lambda j: (j, 0, 0)),
            whole,
        ]
        + [whole_block(*a.shape) for a in attended]
        + [pl.BlockSpec((2 * chips, 1, norms.shape[2], width), lambda j: (0, j, 0, 0))],
        out_specs=[out] * 2,
        out_shape=[jax.ShapeDtypeStruct((blocks, chips, lines, width), LOW)] * 2,
        scratch_shapes=[
            pltpu.VMEM((width, n), LOW),
            pltpu.VMEM((width, width), WIDE),
            pltpu.VMEM((width, width), WIDE),
        ],
        compiler_params=pltpu.CompilerParams(vmem_limit_bytes=40 << 20),
        cost_estimate=cost(flops=10 * n * width * width, bytes_accessed=16 << 20),
        name="side_grads",
    )(core.reshape(1), mix_grad, hidden, proj_grad, *attended, norms)


def gate_up_kernel(x_ref, g_ref, *refs):
    out, turned = refs[-2:]

    @pl.when(pl.program_id(0) == 0)
    def _():
        turned[...] = x_ref[...].T

    out[0] = dot(turned[...], g_ref[0], 1, 0).astype(LOW)


def gate_up_grads(x, grads, after):
    n, width = x.shape
    blocks, _, both = grads.shape
    return pl.pallas_call(
        gate_up_kernel,
        grid=(blocks,),
        in_specs=[pl.BlockSpec((n, width), lambda j: (0, 0)), pl.BlockSpec((1, n, both), lambda j: (j, 0, 0))]
        + [pl.BlockSpec(memory_space=pl.ANY)] * len(after),
        out_specs=pl.BlockSpec((1, width, both), lambda j: (j, 0, 0)),
        out_shape=jax.ShapeDtypeStruct((blocks, width, both), LOW),
        scratch_shapes=[pltpu.VMEM((width, n), LOW)],
        compiler_params=pltpu.CompilerParams(vmem_limit_bytes=40 << 20),
        cost_estimate=cost(flops=2 * n * width * blocks * both, bytes_accessed=24 << 20, scale=1),
        name="gate_up_grads",
    )(x, grads, *after)


def local(
    tp, ways, tokens, segment_ids, positions, w_qkv, w_out, norm1_gain, norm1_shift, w_gate, w_up, w_down, norm2_gain, norm2_shift, out_grad
):
    rows, piece, width = tokens.shape
    chips, per_group = ways
    dp, near = 2 * chips, tp // per_group
    line = ("core", "zg", "zm")
    flat = ("zg", "zm")
    everyone = ("zg", "zm", "chip", "core")
    core = lax.axis_index("core")
    chip = lax.axis_index("chip")
    group = lax.axis_index("zg")
    z = group * near + lax.axis_index("zm")
    member = lax.axis_index("zm") * 2 + core
    own = rows * piece
    by_hand = chips == 4 and tp == 4

    def ring(step):
        pairs = []
        for c in range(2):
            for j in range(tp):
                row = c * rows + (j + step) % rows
                m = j // rows
                pairs.append((c * tp + j, (m % 2) * tp + row * near + m // 2))
        return pairs

    def bring(x, after=()):
        at = jnp.stack([(z + k) % rows for k in range(rows)]).astype(jnp.int32)
        return [lax.ppermute(a, line, ring(k)) for k, a in enumerate(select(x, at, after))]

    def give_back(parts):
        back = [lax.ppermute(part, line, [(b, a) for a, b in ring(k)]) for k, part in enumerate(parts)]
        return jnp.roll(jnp.stack(back), z, axis=0)

    def hop(x, first):
        pairs = []
        for p in range(4):
            for c in range(2):
                bit = 1 if (c == 0) == first else 2
                pairs.append((p * 2 + c, (p ^ bit) * 2 + c))
        return lax.ppermute(x, ("chip", "core"), pairs)

    def along(x, k):
        return lax.ppermute(x, flat, [(i, (i + k) % tp) for i in range(tp)])

    mask_one, mask_two = jnp.where(core == 0, 1, 2), jnp.where(core == 0, 2, 1)

    def spread_z(x, after=()):
        return stack([x[None]] + [along(x, k)[None] for k in range(1, tp)], after) if by_hand else x

    def spread_near(column, after=()):
        return stack([column, hop(column, True)], after) if by_hand else column

    def spread_far(pair, after=()):
        return stack([pair, hop(pair, False)], after) if by_hand else pair

    def spread_core(mine, cuts, after=()):
        if not by_hand:
            whole = lax.all_gather(mine, everyone, axis=0, tiled=False).reshape((tp, dp) + mine.shape)
            parts = [(whole[:, :, at : at + size], z_first) for at, size, z_first in cuts]
            return [a if z_first else a.swapaxes(0, 1) for a, z_first in parts]
        theirs = lax.ppermute(mine, "core", SWAP)
        place = [(chip ^ m) * 2 + core for m in (0, mask_one, mask_two, 3)]
        place += [(chip ^ m) * 2 + 1 - core for m in (0, mask_two, mask_one, 3)]
        place += [(z - k) % tp for k in range(tp)]
        mine, theirs = (a.reshape((chips, tp) + a.shape[1:]) for a in (mine, theirs))
        return arrange(mine, theirs, jnp.stack(place).astype(jnp.int32), cuts, after)

    pick = lambda a, i, axis: lax.dynamic_index_in_dim(a, i, axis, False)
    near_place = jnp.stack([chip, chip ^ mask_one, chip ^ mask_two, chip ^ 3]).astype(jnp.int32)
    line_place = jnp.stack([(z + k) % tp for k in range(tp)]).astype(jnp.int32)

    def collapse_core(mine, send, axis, after=()):
        got = lax.ppermute(send, "core", SWAP)
        shape = (2,) + mine.shape[: axis] + mine.shape[axis + 1 :]
        return join(functools.partial(join_core_kernel, axis), [mine, got], [shape] * 2, after, (near_place,))

    def collapse_far(keep, send, after=()):
        return join(join_far_kernel, [keep, hop(send, False)], [keep.shape[1:]] * 2, after)

    def collapse_near(keep, send, after=()):
        return join(join_near_kernel, [keep, hop(send, True)], [keep.shape[1:]] * tp, after, (line_place,))

    def collapse_z(parts):
        total = parts[0].astype(WIDE)
        for k in range(1, tp):
            total += along(parts[k], k).astype(WIDE)
        return total

    def collapse_all(x):
        return lax.psum_scatter(
            x.reshape((tp * dp,) + x.shape[2:]), everyone, scatter_dimension=0, tiled=False
        ).astype(WIDE)

    nq, no = w_qkv.shape[1], w_out.shape[1]
    units = w_gate.shape[1]
    blocks = tp * units // width
    merged = by_hand and units == width
    pad = -(no + 1) % 16
    norm_row = jnp.concatenate([norm1_gain, norm1_shift, norm2_gain, norm2_shift])
    norm_row = jnp.pad(norm_row, (0, width - 4 * no))[None]
    small = jnp.concatenate([w_out.T, norm_row, jnp.zeros((pad, width), LOW)])
    brought = bring(tokens)
    x = jnp.concatenate(brought)
    qkv_t = spread_near(spread_z(w_qkv.T, tuple(brought)))
    qkv_t = spread_far(qkv_t)
    qkv_t = spread_core(qkv_t, [(0, nq, False)])[0].reshape(3 * width, width)
    gu = beside([w_gate, w_up], tuple(brought))
    gu = lax.all_gather(gu, everyone, axis=0, tiled=False)
    gu = gu.reshape(blocks, tp // blocks, width, 2, units).transpose(0, 2, 3, 1, 4).reshape(blocks, width, -1)

    info = jnp.stack([segment_ids, positions])
    other = lax.ppermute(info, "core", SWAP)
    info = jnp.where(core == 0, jnp.stack([info, other], 1), jnp.stack([other, info], 1))
    info = info.reshape(2, 2 * rows, -1)
    info = lax.dynamic_index_in_dim(info, group, 1, False)
    second = (info[0] != info[0, 0]).reshape(-1, rows, piece)
    second = jnp.roll(second[:, ::-1], group + 1, axis=1).reshape(-1, own)
    places = info[1].reshape(-1, rows, piece)
    places = jnp.roll(places[:, ::-1], group + 1, axis=1).reshape(-1, own)
    own_second = lax.dynamic_index_in_dim(second, member, 0, False)
    own_places = lax.dynamic_index_in_dim(places, member, 0, False)

    def key_aug(is_second):
        return jnp.pad(
            jnp.stack([jnp.where(is_second, 0.0, -MASK), jnp.where(is_second, -MASK, 0.0)]), ((0, AUG - 2), (0, 0))
        ).astype(LOW)

    query_aug = jnp.pad(
        jnp.stack([own_second, ~own_second]).astype(WIDE), ((0, AUG - 2), (0, 0))
    ).astype(LOW)

    half = HEAD_DIM // 2
    frequency = 1000.0 ** (-(jnp.arange(half, dtype=WIDE) * 2.0) / HEAD_DIM)
    angles = own_places.astype(WIDE)[None] * frequency[:, None]
    cosine, sine = jnp.cos(angles), jnp.sin(angles)

    kv = project(qkv_t, x, cosine, sine, "kv", 1)
    members = 2 * near
    if members == 2:
        kvs = [kv, lax.ppermute(kv, "core", SWAP)]
        other_second = lax.dynamic_index_in_dim(second, 1 - member, 0, False)
        kas = [key_aug(own_second), key_aug(other_second)]
        types = [WIDE, LOW]
    else:
        kvs = [lax.all_gather(kv, ("zm", "core"), axis=1, tiled=True)]
        kas = [key_aug(second.reshape(-1))]
        types = [LOW]
    q = project(qkv_t, x, cosine, sine, "q", 0)
    spans = [(i * HEADS // PIECES, HEADS // PIECES) for i in range(PIECES)]
    late = stack([w_down.T, small] if merged else [small], (x,))
    attended, lses = [], []
    cuts = [(0, width // dp, True), (width // dp, small.shape[0], False)]
    for i, span in enumerate(spans):
        att, lse = attend_forward(q, query_aug, kvs, kas, (late,) if i else (), *span)
        attended.append(att)
        lses.append(lse)
        if i == 0:
            late = spread_z(late, (att,))
            top_parts = bring(out_grad, (att, late))
        if i == 1:
            late = spread_near(late, (att,))
        if i == 2:
            late = spread_far(late, (att,))
    late = spread_core(late, cuts if merged else [(0, small.shape[0], False)])
    grad_top = stack(top_parts, (attended[-1],))
    by_column = late[-1]
    down = late[0] if merged else spread_core(w_down.T, [(0, width // dp, True)])[0]
    down = down.reshape(blocks, tp // blocks, width, units).swapaxes(1, 2).reshape(blocks, width, -1)
    out_t = by_column[:, :, :no].reshape(width, width)
    vectors = by_column[:, :, no, : 4 * no].reshape(dp * tp, 4, no).swapaxes(0, 1).reshape(4, width)
    vectors = jnp.pad(vectors.astype(WIDE), ((0, 4), (0, 0)))

    output, x_low, hidden, gug, mix_grad, d_resid_one, proj_grad, att_grad, sums = middle(
        attended, x, grad_top, vectors, out_t, gu, down
    )
    output = give_back([output[k * piece : (k + 1) * piece] for k in range(rows)])

    def ungroup(g, parts):
        g = g.reshape(blocks, width, parts, tp // blocks, units).transpose(0, 3, 1, 2, 4)
        return g.reshape(tp, dp, width // dp, parts * units)

    norms = sums[:4].reshape(4, dp * tp, no).swapaxes(0, 1).reshape(dp, tp, 1, 4 * no)
    if merged:
        norms = jnp.pad(norms, ((0, 0), (0, 0), (0, pad), (0, width - 4 * no)))
        mine, send = side_grads(core, mix_grad, hidden, proj_grad, attended, norms, width // dp + no + pad + 1)
    else:
        norms = jnp.pad(norms.astype(LOW), ((0, 0), (0, 0), (0, pad), (0, width - 4 * no)))
        g_out = dot(proj_grad, jnp.concatenate(attended), 0, 1).astype(LOW)
        side = jnp.concatenate([g_out.reshape(dp, tp, no, width), norms], axis=2)
        side = collapse_all(side.swapaxes(0, 1))
        g_down = jnp.einsum("td,jtf->jdf", mix_grad, hidden, preferred_element_type=WIDE).astype(LOW)
        g_down = collapse_all(ungroup(g_down, 1))
        mine = mix_grad
    g_gu = ungroup(gate_up_grads(x_low, gug, (mine,)), 2)
    shared_gu = collapse_all(g_gu)
    held = (g_gu,)
    if merged:
        held = collapse_core(mine, send, 1, (g_gu,))

    grads, parts = [], []
    for i, ((start, count), att, lse) in enumerate(zip(spans, attended, lses)):
        after = tuple(held) + ((output,) if i + 1 == PIECES else ())
        dq, dkv = attend_backward(q, att_grad, att, lse, query_aug, kvs, kas, types, after, start, count)
        if merged and i == 0:
            held = collapse_far(*held, (dq,))
        if merged and i == 2:
            held = collapse_near(*held, (dq,))
        if members == 2:
            own_dkv, others = dkv[0], (lax.ppermute(dkv[1], "core", SWAP),)
        else:
            summed = lax.psum_scatter(dkv[0], ("zm", "core"), scatter_dimension=2, tiled=True)
            own_dkv, others = summed.astype(WIDE), ()
        grad, part = unturn(dq, own_dkv, others, cosine, sine, x)
        grads.append(grad)
        parts.append(part)
    if merged:
        total = collapse_z(held)
        g_down, side = total[: width // dp], total[width // dp :]
    g_qkv = jnp.concatenate(parts, axis=1).reshape(dp, tp, nq, width)
    if not by_hand:
        g_qkv = collapse_all(g_qkv.swapaxes(0, 1))
        in_grad = finish(grads, d_resid_one, qkv_t, (), 0, own)
        in_grad = give_back([in_grad[k * piece : (k + 1) * piece] for k in range(rows)])
    else:
        g_qkv = g_qkv.reshape(chips, 2, tp, nq, width)
        mine, send = pick(g_qkv, core, 1), pick(g_qkv, 1 - core, 1)
        in_grad = [finish(grads, d_resid_one, qkv_t, (send,) + ((total,) if merged else ()), 0, piece)]
        held = collapse_core(mine, send, 0, (in_grad[0],))
        for k in range(1, rows):
            in_grad.append(finish(grads, d_resid_one, qkv_t, (held[0],), k, piece))
        held = collapse_far(*held, (in_grad[-1],))
        g_qkv = collapse_z(collapse_near(*held))
        in_grad = give_back(in_grad)
    vector_grads = side[no, : 4 * no].reshape(4, no)
    return (
        output,
        in_grad,
        g_qkv.T,
        side[:no].T,
        vector_grads[0],
        vector_grads[1],
        shared_gu[:, :units],
        shared_gu[:, units:],
        g_down.T,
        vector_grads[2],
        vector_grads[3],
    )


def solution(mesh):
    dp, tp = mesh.shape["dp"], mesh.shape["tp"]

    def run(*arrays):
        rows = arrays[0].shape[0] // dp
        groups = 2 * rows
        grid = Mesh(
            mesh.devices.reshape(dp // 2, 2, groups, tp // groups), ("chip", "core", "zg", "zm")
        )
        d, t = ("chip", "core"), ("zg", "zm")
        both = d + t
        placed = (
            P(d, t, None),
            P(d, None),
            P(d, None),
            P(None, both),
            P(None, both),
            P(both),
            P(both),
            P(d, t),
            P(d, t),
            P(t, d),
            P(both),
            P(both),
            P(d, t, None),
        )
        return jax.shard_map(
            functools.partial(local, tp, (dp // 2, groups)),
            mesh=grid,
            in_specs=placed,
            out_specs=(
                P(d, t, None),
                P(d, t, None),
                P(None, both),
                P(None, both),
                P(both),
                P(both),
                P(d, t),
                P(d, t),
                P(t, d),
                P(both),
                P(both),
            ),
            check_vma=False,
        )(*arrays)

    return run
```

time: 811 us -> 548 us (0.68)
  waiting for transfers between devices: 435 us -> 137 us
  Pallas kernels: 108 us -> 238 us
  matrix products: 129 us -> 0 us
  starting transfers between devices: 28.8 us -> 81.5 us
  other arithmetic: 41.5 us -> 13.4 us
  local copies, waits for them, and re-layouts: 43.2 us -> 56.2 us
    reduce_scatter x4 -> x1, waiting for transfers between devices: 239 us -> 0.01 us  [collapse_all(): lax.psum_scatter(x.reshape((tp * dp,) + x.shape[2:]), everyone, scatter_d...]
    all_gather x4 -> x1, waiting for transfers between devices: 140 us -> 0.01 us  [local(): gu = lax.all_gather(gu, everyone, axis=0, tiled=False)]
    pallas_call x2 -> x38, Pallas kernels: 108 us -> 238 us  [the longest x4 77.8 us: attend_backward(): pl.pallas_call(functools.partial(backward_kernel, parts), grid=(heads,),...]
    dot_general x15 -> x0, matrix products: 129 us -> none  [the longest x6 30.2 us: dot(): lax.dot_general(a, b, (((ca,), (cb,)), ((), ())), preferred_element_type=...]
    ppermute x10 -> x37, waiting for transfers between devices: 54.2 us -> 135 us  [the longest x12 51.6 us: along(): return lax.ppermute(x, flat, [(i, (i + k) % tp) for i in range(tp)])]
    ppermute x10 -> x37, starting transfers between devices: 25.7 us -> 80.9 us  [the longest x12 43.2 us: along(): return lax.ppermute(x, flat, [(i, (i + k) % tp) for i in range(tp)])]
    unnamed x61 -> x163, local copies, waits for them, and re-layouts: 12.7 us -> 48.2 us
    reduce_sum x6 -> x0, other arithmetic: 8.5 us -> none  [the longest x1 5.04 us: local(): gain_two_grad = jnp.sum(grad_top * normed_two, axis=0)]
  transfers between devices with their start and end apart: 19 -> 40, of which waited for: 10 -> 17; matrix products, arithmetic and copies ran while one was open for 23% -> 3% of each run, Pallas kernels for 13% -> 29%
where the time goes in v2:
time: 548 us; the launch traced here: 542 us
  Pallas kernels  238 us (43%)
  waiting for transfers between devices  137 us (25%)
  starting transfers between devices  81.5 us (15%)
  local copies, waits for them, and re-layouts  56.2 us (10%)
  between operations  15.5 us (3%)
  other arithmetic  13.4 us (2%)
    pallas_call x4, Pallas kernels, attend_backward(): pl.pallas_call(functools.partial(backward_kernel, parts), grid=(heads,),...  77.8 us
    pallas_call x1, Pallas kernels, middle(): pl.pallas_call(functools.partial(middle_kernel, pieces), grid=(n // step,...  52.4 us
    ppermute x12, waiting for transfers between devices, along(): return lax.ppermute(x, flat, [(i, (i + k) % tp) for i in range(tp)])  51.6 us
    unnamed x163, local copies, waits for them, and re-layouts  48.2 us
    ppermute x12, starting transfers between devices, along(): return lax.ppermute(x, flat, [(i, (i + k) % tp) for i in range(tp)])  43.2 us
    pallas_call x4, Pallas kernels, attend_forward(): pl.pallas_call(functools.partial(forward_kernel, parts), grid=(heads,), i...  42.7 us
    ppermute x8, waiting for transfers between devices, hop(): return lax.ppermute(x, ('chip', 'core'), pairs)  39 us
    ppermute x4, waiting for transfers between devices, bring(): lax.ppermute(a, line, ring(k))  35.4 us
  transfers between devices with their start and end apart: 40, of which 17 were waited for; matrix products, arithmetic and copies ran while one was open for 3% of the time, Pallas kernels for 29%

profile of v2, /device:TPU:0, one launch (start us, length us, event | category | flops | bytes accessed | tf_op | source)
XLA Modules:
  0.0 541.8 jit_solution(15708492701589286015)
XLA Ops:
  7.3 1.4 copy-done.52
  10.2 3.1 collective-permute-start.4
  13.3 17.2 %collective-permute-done.4.refs_5_.refs_3_ = bf16[512,768]{1,0:T(8,128)(2,1)S(1)} collective-permute-done((bf16[512,768]{1,0:T(8,128)(2,1)S(1)}, bf16[512,768]{1,0:T(8,128)(2,1)S(1)}, u32[]{:S(2)}, u32[]{:S(2)}) %collective-permute-start.4) | collective-permute-done | bytes 786464 | tf_op jit(solution)/shard_map/ppermute | solution.py:665
  31.5 1.7 beside.1
  33.3 25.0 %collective-permute-start.1 = (bf16[72,768]{1,0:T(8,128)(2,1)S(1)}, bf16[72,768]{1,0:T(8,128)(2,1)S(1)}, u32[]{:S(2)}, u32[]{:S(2)}) collective-permute-start(bf16[72,768]{1,0:T(8,128)(2,1)S(1)} %bitcast.107), channel_id=1, source_target_pairs={{0,2},{1,3},{2,0},{3,1},{4,6},{5,7},{6,4},{7,5},{8,10},{9,11},{10,... | collective-permute-start | bytes 331784 | tf_op jit(solution)/shard_map/ppermute | solution.py:680
  58.3 3.8 collective-permute-start.2
  62.1 3.2 collective-permute-done.1
  67.7 1.6 collective-permute-start.5
  69.2 6.8 %collective-permute-done.5.refs_1_ = bf16[4,72,768]{2,1,0:T(8,128)(2,1)S(1)} collective-permute-done((bf16[4,72,768]{2,1,0:T(8,128)(2,1)S(1)}, bf16[4,72,768]{2,1,0:T(8,128)(2,1)S(1)}, u32[]{:S(2)}, u32[]{:S(2)}) %collective-permute-start.5) | collective-permute-done | bytes 442400 | tf_op jit(solution)/shard_map/ppermute | solution.py:677
  76.1 1.7 collective-permute-start.6
  77.8 15.6 %collective-permute-done.6.refs_1_ = bf16[8,72,768]{2,1,0:T(8,128)(2,1)S(1)} collective-permute-done((bf16[8,72,768]{2,1,0:T(8,128)(2,1)S(1)}, bf16[8,72,768]{2,1,0:T(8,128)(2,1)S(1)}, u32[]{:S(2)}, u32[]{:S(2)}) %collective-permute-start.6) | collective-permute-done | bytes 884768 | tf_op jit(solution)/shard_map/ppermute | solution.py:677
  94.4 2.7 collective-permute-done.8
  98.1 2.3 arrange.2
  100.5 3.5 project.3.refs_2_.refs_4_.refs_5_.refs_7_
  107.0 1.9 copy-done.3
  109.8 3.4 collective-permute-start.12
  115.3 2.0 copy-done.7
  117.3 1.6 project.2.refs_0_
  120.1 10.6 %attend_forward.4 = (bf16[192,1024]{1,0:T(8,128)(2,1)}, f32[3,1,1024]{2,1,0:T(1,128)}) custom-call(bf16[768,1024]{1,0:T(8,128)(2,1)} %copy-done.1, bf16[16,1024]{1,0:T(8,128)(2,1)} %convert_convert_fusion.refs_1_.refs_4_, bf16[1536,1024]{1,0:T(8,128)(2,1)} %copy-done, bf16[1536,1024]{1,0:T(8,128)(2,1)} %collective-permute-done.9.refs_3_.refs_5_.refs_6_.refs_8_, ...), custom_call_target="tpu_custom_call" | custom-call | flops 402653184 | bytes 147456 | tf_op jit(solution)/shard_map/attend_forward/pallas_call | solution.py:86
  130.7 19.6 %collective-permute-done.11 = bf16[128,768]{1,0:T(8,128)(2,1)S(1)} collective-permute-done((bf16[128,768]{1,0:T(8,128)(2,1)S(1)}, bf16[128,768]{1,0:T(8,128)(2,1)S(1)}, u32[]{:S(2)}, u32[]{:S(2)}) %collective-permute-start.11) | collective-permute-done | bytes 196640 | tf_op jit(solution)/shard_map/ppermute | solution.py:680
  151.4 1.6 collective-permute-start.13
  153.0 10.7 %attend_forward.5 = (bf16[192,1024]{1,0:T(8,128)(2,1)}, f32[3,1,1024]{2,1,0:T(1,128)}) custom-call(bf16[768,1024]{1,0:T(8,128)(2,1)} %copy-done.1, bf16[16,1024]{1,0:T(8,128)(2,1)} %convert_convert_fusion.refs_1_.refs_4_, bf16[1536,1024]{1,0:T(8,128)(2,1)} %copy-done, bf16[1536,1024]{1,0:T(8,128)(2,1)} %collective-permute-done.9.refs_3_.refs_5_.refs_6_.refs_8_, ...), custom_call_target="tpu_custom_call" | custom-call | flops 402653184 | bytes 147456 | tf_op jit(solution)/shard_map/attend_forward/pallas_call | solution.py:86
  165.9 1.5 collective-permute-start.14
  167.5 10.7 %attend_forward.6 = (bf16[192,1024]{1,0:T(8,128)(2,1)}, f32[3,1,1024]{2,1,0:T(1,128)}) custom-call(bf16[768,1024]{1,0:T(8,128)(2,1)} %copy-done.1, bf16[16,1024]{1,0:T(8,128)(2,1)} %convert_convert_fusion.refs_1_.refs_4_, bf16[1536,1024]{1,0:T(8,128)(2,1)} %copy-done, bf16[1536,1024]{1,0:T(8,128)(2,1)} %collective-permute-done.9.refs_3_.refs_5_.refs_6_.refs_8_, ...), custom_call_target="tpu_custom_call" | custom-call | flops 402653184 | bytes 147456 | tf_op jit(solution)/shard_map/attend_forward/pallas_call | solution.py:86
  178.2 8.3 %collective-permute-done.14.refs_1_ = bf16[8,128,768]{2,1,0:T(8,128)(2,1)S(1)} collective-permute-done((bf16[8,128,768]{2,1,0:T(8,128)(2,1)S(1)}, bf16[8,128,768]{2,1,0:T(8,128)(2,1)S(1)}, u32[]{:S(2)}, u32[]{:S(2)}) %collective-permute-start.14) | collective-permute-done | bytes 1572896 | tf_op jit(solution)/shard_map/ppermute | solution.py:677
  191.7 1.8 select.67
  193.5 1.8 collective-permute-start.15
  195.3 10.6 %attend_forward.7 = (bf16[192,1024]{1,0:T(8,128)(2,1)}, f32[3,1,1024]{2,1,0:T(1,128)}) custom-call(bf16[768,1024]{1,0:T(8,128)(2,1)} %copy-done.1, bf16[16,1024]{1,0:T(8,128)(2,1)} %convert_convert_fusion.refs_1_.refs_4_, bf16[1536,1024]{1,0:T(8,128)(2,1)} %copy-done, bf16[1536,1024]{1,0:T(8,128)(2,1)} %collective-permute-done.9.refs_3_.refs_5_.refs_6_.refs_8_, ...), custom_call_target="tpu_custom_call" | custom-call | flops 402653184 | bytes 147456 | tf_op jit(solution)/shard_map/attend_forward/pallas_call | solution.py:86
  206.0 18.2 %collective-permute-done.16.refs_1_ = bf16[512,768]{1,0:T(8,128)(2,1)S(1)} collective-permute-done((bf16[512,768]{1,0:T(8,128)(2,1)}, bf16[512,768]{1,0:T(8,128)(2,1)S(1)}, u32[]{:S(2)}, u32[]{:S(2)}) %collective-permute-start.16) | collective-permute-done | bytes 786464 | tf_op jit(solution)/shard_map/ppermute | solution.py:665
  227.6 2.3 arrange.3
  229.9 2.1 copy-done.41
  234.1 52.4 %middle.1 = (bf16[1024,768]{1,0:T(8,128)(2,1)}, bf16[1024,768]{1,0:T(8,128)(2,1)}, bf16[4,1024,768]{2,1,0:T(8,128)(2,1)}, bf16[4,1024,1536]{2,1,0:T(8,128)(2,1)}...) custom-call(bf16[192,1024]{1,0:T(8,128)(2,1)} %get-tuple-element.75., ...), custom_call_target="tpu_custom_call" | custom-call | flops 1962934272 | bytes 3932160 | tf_op jit(solution)/shard_map/middle/pallas_call | solution.py:310
  290.5 9.7 %side_grads.1 = (bf16[4,4,128,768]{3,2,1,0:T(8,128)(2,1)S(1)}, bf16[4,4,128,768]{3,2,1,0:T(8,128)(2,1)S(1)}) custom-call(s32[1]{0:T(128)} %bitcast.48.core_ref, bf16[1024,768]{1,0:T(8,128)(2,1)S(1)} %copy-done.56, bf16[4,1024,768]{2,1,0:T(8,128)(2,1)} %get-tuple-element.87.hid_ref, bf16[1024,768]{1,0:T(8,128)(2,1)S(1)} %copy-done.57, ...), custom_call_target="tpu_custom_call" | custom-call | flops 377487360 | bytes 1048576 | tf_op jit(solution)/shard_map/side_grads/pallas_call | solution.py:586
  300.2 1.6 copy-done.70
  301.8 14.0 %gate_up_grads.1 = bf16[4,768,1536]{2,1,0:T(8,128)(2,1)S(1)} custom-call(bf16[1024,768]{1,0:T(8,128)(2,1)S(1)} %copy-done.71, bf16[4,1024,1536]{2,1,0:T(8,128)(2,1)} %get-tuple-element.93.g_ref, bf16[4,4,128,768]{3,2,1,0:T(8,128)(2,1)S(1)} %get-tuple-element.90.refs_0_.mine), custom_call_target="tpu_custom_call" | custom-call | flops 9663676416 | bytes 25165824 | tf_op jit(solution)/shard_map/gate_up_grads/pallas_call | solution.py:623
  315.8 3.7 copy-done.8
  319.7 5.8 %collective-permute-done.20.got = bf16[4,4,128,768]{3,2,1,0:T(8,128)(2,1)S(1)} collective-permute-done((bf16[4,4,128,768]{3,2,1,0:T(8,128)(2,1)}, bf16[4,4,128,768]{3,2,1,0:T(8,128)(2,1)S(1)}, u32[]{:S(2)}, u32[]{:S(2)}) %collective-permute-start.20) | collective-permute-done | bytes 3145760 | tf_op jit(solution)/shard_map/ppermute | solution.py:710
  325.5 3.7 copy-done.9
  329.2 2.3 join.6
  334.1 7.2 %collective-permute-start.19 = (bf16[512,768]{1,0:T(8,128)(2,1)}, bf16[512,768]{1,0:T(8,128)(2,1)}, u32[]{:S(2)}, u32[]{:S(2)}) collective-permute-start(bf16[512,768]{1,0:T(8,128)(2,1)} %get-tuple-element.138), channel_id=1, source_target_pairs={{1,0},{0,1},{5,2},{4,3},{3,4},{2,5},{7,6},{6,7},{9,8},{8,9},{13,10... | collective-permute-start | bytes 2359304 | tf_op jit(solution)/shard_map/ppermute | solution.py:668
  341.4 7.4 %collective-permute-start.18 = (bf16[512,768]{1,0:T(8,128)(2,1)}, bf16[512,768]{1,0:T(8,128)(2,1)}, u32[]{:S(2)}, u32[]{:S(2)}) collective-permute-start(bf16[512,768]{1,0:T(8,128)(2,1)} %get-tuple-element.139), channel_id=1, source_target_pairs={{0,0},{1,1},{4,2},{5,3},{2,4},{3,5},{6,6},{7,7},{8,8},{9,9},{12,10... | collective-permute-start | bytes 2359304 | tf_op jit(solution)/shard_map/ppermute | solution.py:668
  348.8 19.5 %attend_backward.4 = (f32[192,1024]{1,0:T(8,128)}, f32[2,192,1024]{2,1,0:T(8,128)}, bf16[2,192,1024]{2,1,0:T(8,128)(2,1)}) custom-call(bf16[768,1024]{1,0:T(8,128)(2,1)} %copy-done.1, bf16[768,1024]{1,0:T(8,128)(2,1)} %get-tuple-element.84.refs_1_, bf16[192,1024]{1,0:T(8,128)(2,1)} %get-tuple-element.75.refs_4_.refs_0_.refs_2_, ...), custom_call_target="tpu_custom_call" | custom-call | flops 754974720 | bytes 294912 | tf_op jit(solution)/shard_map/attend_backward/pallas_call | solution.py:154
  374.6 4.4 fusion.4.refs_15_
  379.0 19.3 %attend_backward.6 = (f32[192,1024]{1,0:T(8,128)}, f32[2,192,1024]{2,1,0:T(8,128)}, bf16[2,192,1024]{2,1,0:T(8,128)(2,1)}) custom-call(bf16[768,1024]{1,0:T(8,128)(2,1)} %copy-done.1, bf16[768,1024]{1,0:T(8,128)(2,1)} %get-tuple-element.84.refs_1_, bf16[192,1024]{1,0:T(8,128)(2,1)} %get-tuple-element.77.refs_2_, f32[3,1,1024]{2,1,0:T(1,128)} %get-tuple-element.107.refs_3_, ...), custom_call_target="tpu_custom_call" | custom-call | flops 754974720 | bytes 294912 | tf_op jit(solution)/shard_map/attend_backward/pallas_call | solution.py:154
  398.9 19.7 %attend_backward.5 = (f32[192,1024]{1,0:T(8,128)}, f32[2,192,1024]{2,1,0:T(8,128)}, bf16[2,192,1024]{2,1,0:T(8,128)(2,1)}) custom-call(bf16[768,1024]{1,0:T(8,128)(2,1)} %copy-done.1, bf16[768,1024]{1,0:T(8,128)(2,1)} %get-tuple-element.84.refs_1_, bf16[192,1024]{1,0:T(8,128)(2,1)} %get-tuple-element.76.refs_2_.refs_1_, ...), custom_call_target="tpu_custom_call" | custom-call | flops 754974720 | bytes 294912 | tf_op jit(solution)/shard_map/attend_backward/pallas_call | solution.py:154
  422.1 19.4 %attend_backward.7 = (f32[192,1024]{1,0:T(8,128)}, f32[2,192,1024]{2,1,0:T(8,128)}, bf16[2,192,1024]{2,1,0:T(8,128)(2,1)}) custom-call(bf16[768,1024]{1,0:T(8,128)(2,1)} %copy-done.1, bf16[768,1024]{1,0:T(8,128)(2,1)} %get-tuple-element.84.refs_1_, bf16[192,1024]{1,0:T(8,128)(2,1)} %get-tuple-element.78.refs_2_.refs_3_, ...), custom_call_target="tpu_custom_call" | custom-call | flops 754974720 | bytes 294912 | tf_op jit(solution)/shard_map/attend_backward/pallas_call | solution.py:154
  444.6 3.2 unturn.4
  447.9 3.3 unturn.6
  452.2 3.5 unturn.5
  455.7 1.7 unturn.7
  460.2 3.1 collective-permute-start.29
  463.3 5.8 %collective-permute-done.27 = bf16[128,768]{1,0:T(8,128)(2,1)S(1)} collective-permute-done((bf16[128,768]{1,0:T(8,128)(2,1)S(1)}, bf16[128,768]{1,0:T(8,128)(2,1)S(1)}, u32[]{:S(2)}, u32[]{:S(2)}) %collective-permute-start.27) | collective-permute-done | bytes 196640 | tf_op jit(solution)/shard_map/ppermute | solution.py:680
  469.1 7.5 %collective-permute-done.28 = bf16[128,768]{1,0:T(8,128)(2,1)S(1)} collective-permute-done((bf16[128,768]{1,0:T(8,128)(2,1)S(1)}, bf16[128,768]{1,0:T(8,128)(2,1)S(1)}, u32[]{:S(2)}, u32[]{:S(2)}) %collective-permute-start.28) | collective-permute-done | bytes 196640 | tf_op jit(solution)/shard_map/ppermute | solution.py:680
  476.7 4.8 finish.2.refs_0_
  484.1 4.9 finish.3.refs_0_
  489.0 4.0 collective-permute-start.32
  493.7 2.0 collective-permute-done.33.got
  497.9 6.4 %collective-permute-done.34.got = bf16[4,72,768]{2,1,0:T(8,128)(2,1)S(1)} collective-permute-done((bf16[4,72,768]{2,1,0:T(8,128)(2,1)S(1)}, bf16[4,72,768]{2,1,0:T(8,128)(2,1)S(1)}, u32[]{:S(2)}, u32[]{:S(2)}) %collective-permute-start.34) | collective-permute-done | bytes 442400 | tf_op jit(solution)/shard_map/ppermute | solution.py:677
  504.9 3.9 collective-permute-start.35
  508.8 2.4 collective-permute-start.37
  511.2 3.0 collective-permute-done.32
  514.2 2.3 fusion.1
  516.5 5.1 collective-permute-done.35
  521.6 10.2 %collective-permute-done.36 = bf16[72,768]{1,0:T(8,128)(2,1)S(1)} collective-permute-done((bf16[72,768]{1,0:T(8,128)(2,1)S(1)}, bf16[72,768]{1,0:T(8,128)(2,1)S(1)}, u32[]{:S(2)}, u32[]{:S(2)}) %collective-permute-start.36) | collective-permute-done | bytes 110624 | tf_op jit(solution)/shard_map/ppermute | solution.py:680
  (274 shorter events, 60.7 us)
Async XLA Ops:
  7.2 226.9 %all-gather.3.cloned.1.call-start = ((), (), s32[]{:S(2)}) async-start(), calls=%async_computation.2 | async-start | bytes 9732096 | tf_op jit(solution)/shard_map/all_gather | solution.py:745
  9.4 23.9 %copy-start.69 = (bf16[768,72]{0,1:T(8,128)(2,1)S(1)}, bf16[768,72]{0,1:T(8,128)(2,1)}, u32[]{:S(2)}) copy-start(bf16[768,72]{0,1:T(8,128)(2,1)} %param.18) | copy-start | bytes 331780
  9.4 3.9 collective-permute-start.3
  10.2 20.3 %collective-permute-start.4 = (bf16[512,768]{1,0:T(8,128)(2,1)S(1)}, bf16[512,768]{1,0:T(8,128)(2,1)S(1)}, u32[]{:S(2)}, u32[]{:S(2)}) collective-permute-start(bf16[512,768]{1,0:T(8,128)(2,1)S(1)} %get-tuple-element.74), channel_id=1, source_target_pairs={{0,1},{1,0},{2,5},{3,4},{4,3},{5,2},{6,7},{7,6},{8,9},{9,8},{10,13... | collective-permute-start | bytes 2359304 | tf_op jit(solution)/shard_map/ppermute | solution.py:665
  13.3 17.2 %copy-start.22 = (bf16[512,768]{1,0:T(8,128)(2,1)}, bf16[512,768]{1,0:T(8,128)(2,1)S(1)}, u32[]{:S(2)}) copy-start(bf16[512,768]{1,0:T(8,128)(2,1)S(1)} %collective-permute-done.3.refs_4_.refs_2_) | copy-start | bytes 2359300
  33.2 499.4 %reduce-scatter.2.cloned.1.call-start = ((), (), s32[]{:S(2)}) async-start(), calls=%async_computation.1 | async-start | bytes 9732096 | tf_op jit(solution)/shard_map/reduce_scatter | solution.py:727
  33.3 32.0 %collective-permute-start.1 = (bf16[72,768]{1,0:T(8,128)(2,1)S(1)}, bf16[72,768]{1,0:T(8,128)(2,1)S(1)}, u32[]{:S(2)}, u32[]{:S(2)}) collective-permute-start(bf16[72,768]{1,0:T(8,128)(2,1)S(1)} %bitcast.107), channel_id=1, source_target_pairs={{0,2},{1,3},{2,0},{3,1},{4,6},{5,7},{6,4},{7,5},{8,10},{9,11},{10,... | collective-permute-start | bytes 331784 | tf_op jit(solution)/shard_map/ppermute | solution.py:680
  58.3 7.1 %collective-permute-start = (bf16[72,768]{1,0:T(8,128)(2,1)S(1)}, bf16[72,768]{1,0:T(8,128)(2,1)S(1)}, u32[]{:S(2)}, u32[]{:S(2)}) collective-permute-start(bf16[72,768]{1,0:T(8,128)(2,1)S(1)} %bitcast.108), channel_id=1, source_target_pairs={{0,1},{1,2},{2,3},{3,0},{4,5},{5,6},{6,7},{7,4},{8,9},{9,10},{10,1... | collective-permute-start | bytes 331784 | tf_op jit(solution)/shard_map/ppermute | solution.py:680
  58.3 7.1 %collective-permute-start.2 = (bf16[72,768]{1,0:T(8,128)(2,1)S(1)}, bf16[72,768]{1,0:T(8,128)(2,1)S(1)}, u32[]{:S(2)}, u32[]{:S(2)}) collective-permute-start(bf16[72,768]{1,0:T(8,128)(2,1)S(1)} %bitcast.109), channel_id=1, source_target_pairs={{0,3},{1,0},{2,1},{3,2},{4,7},{5,4},{6,5},{7,6},{8,11},{9,8},{10,9... | collective-permute-start | bytes 331784 | tf_op jit(solution)/shard_map/ppermute | solution.py:680
  67.7 8.4 %collective-permute-start.5 = (bf16[4,72,768]{2,1,0:T(8,128)(2,1)S(1)}, bf16[4,72,768]{2,1,0:T(8,128)(2,1)S(1)}, u32[]{:S(2)}, u32[]{:S(2)}) collective-permute-start(bf16[4,72,768]{2,1,0:T(8,128)(2,1)S(1)} %stack.199.refs_0_), channel_id=1, source_target_pairs={{0,8},{4,20},{8,0},{12,28},{16,24},{20,4},{24,16},{28,12},{1,9},{5... | collective-permute-start | bytes 1327112 | tf_op jit(solution)/shard_map/ppermute | solution.py:677
  76.1 17.6 %copy-start.74 = (s32[2,2048]{1,0:T(2,128)S(1)}, s32[2,2048]{1,0:T(2,128)}, u32[]{:S(2)}) copy-start(s32[2,2048]{1,0:T(2,128)} %param.17) | copy-start | bytes 49156
  76.1 17.6 %copy-start.75 = (s32[2,2048]{1,0:T(2,128)S(1)}, s32[2,2048]{1,0:T(2,128)}, u32[]{:S(2)}) copy-start(s32[2,2048]{1,0:T(2,128)} %param.16) | copy-start | bytes 49156
  76.1 21.8 %copy-start.24 = (bf16[512,768]{1,0:T(8,128)(2,1)S(1)}, bf16[512,768]{1,0:T(8,128)(2,1)}, u32[]{:S(2)}) copy-start(bf16[512,768]{1,0:T(8,128)(2,1)} %copy-done.22) | copy-start | bytes 2359300
  76.1 17.3 %collective-permute-start.6 = (bf16[8,72,768]{2,1,0:T(8,128)(2,1)S(1)}, bf16[8,72,768]{2,1,0:T(8,128)(2,1)S(1)}, u32[]{:S(2)}, u32[]{:S(2)}) collective-permute-start(bf16[8,72,768]{2,1,0:T(8,128)(2,1)S(1)} %stack.200.refs_0_), channel_id=1, source_target_pairs={{0,16},{4,12},{8,24},{12,4},{16,0},{20,28},{24,8},{28,20},{1,17},{... | collective-permute-start | bytes 2654216 | tf_op jit(solution)/shard_map/ppermute | solution.py:677
  93.6 4.4 copy-start.27
  93.6 4.5 collective-permute-start.7
  93.7 3.3 collective-permute-start.8
  104.0 15.0 %copy-start = (bf16[1536,1024]{1,0:T(8,128)(2,1)}, bf16[1536,1024]{1,0:T(8,128)(2,1)S(1)}, u32[]{:S(2)}) copy-start(bf16[1536,1024]{1,0:T(8,128)(2,1)S(1)} %project.3.refs_2_.refs_4_.refs_5_.refs_7_) | copy-start | bytes 9437188
  104.0 11.3 %copy-start.29 = (f32[32,1024]{1,0:T(8,128)S(1)}, f32[32,1024]{1,0:T(8,128)}, u32[]{:S(2)}) copy-start(f32[32,1024]{1,0:T(8,128)} %copy-done.28) | copy-start | bytes 393220
  104.0 16.1 %collective-permute-start.9 = (bf16[1536,1024]{1,0:T(8,128)(2,1)S(1)}, bf16[1536,1024]{1,0:T(8,128)(2,1)}, u32[]{:S(2)}, u32[]{:S(2)}) collective-permute-start(bf16[1536,1024]{1,0:T(8,128)(2,1)S(1)} %project.3.refs_2_.refs_4_.refs_5_.refs_7_), channel_id=1, source_target_pairs={{0,4},{4,0},{1,5},{5,1},{2,6},{6,2},{3,7},{7,3},{8,12},{12,8},{9,1... | collective-permute-start | bytes 9437192 | tf_op jit(solution)/shard_map/ppermute | solution.py:777
  109.8 5.5 %copy-start.4 = (bf16[1024,768]{1,0:T(8,128)(2,1)S(1)}, bf16[1024,768]{1,0:T(8,128)(2,1)}, u32[]{:S(2)}) copy-start(bf16[1024,768]{1,0:T(8,128)(2,1)} %copy-done.2) | copy-start | bytes 4718596
  109.8 20.9 %collective-permute-start.12 = (bf16[128,768]{1,0:T(8,128)(2,1)S(1)}, bf16[128,768]{1,0:T(8,128)(2,1)S(1)}, u32[]{:S(2)}, u32[]{:S(2)}) collective-permute-start(bf16[128,768]{1,0:T(8,128)(2,1)S(1)} %stack.202), channel_id=1, source_target_pairs={{0,3},{1,0},{2,1},{3,2},{4,7},{5,4},{6,5},{7,6},{8,11},{9,8},{10,9... | collective-permute-start | bytes 589832 | tf_op jit(solution)/shard_map/ppermute | solution.py:680
  113.2 37.2 %collective-permute-start.11 = (bf16[128,768]{1,0:T(8,128)(2,1)S(1)}, bf16[128,768]{1,0:T(8,128)(2,1)S(1)}, u32[]{:S(2)}, u32[]{:S(2)}) collective-permute-start(bf16[128,768]{1,0:T(8,128)(2,1)S(1)} %stack.202), channel_id=1, source_target_pairs={{0,2},{1,3},{2,0},{3,1},{4,6},{5,7},{6,4},{7,5},{8,10},{9,11},{10,... | collective-permute-start | bytes 589832 | tf_op jit(solution)/shard_map/ppermute | solution.py:680
  113.2 37.2 %collective-permute-start.10 = (bf16[128,768]{1,0:T(8,128)(2,1)S(1)}, bf16[128,768]{1,0:T(8,128)(2,1)S(1)}, u32[]{:S(2)}, u32[]{:S(2)}) collective-permute-start(bf16[128,768]{1,0:T(8,128)(2,1)S(1)} %stack.202), channel_id=1, source_target_pairs={{0,1},{1,2},{2,3},{3,0},{4,5},{5,6},{6,7},{7,4},{8,9},{9,10},{10,1... | collective-permute-start | bytes 589832 | tf_op jit(solution)/shard_map/ppermute | solution.py:680
  151.4 12.3 %collective-permute-start.13 = (bf16[4,128,768]{2,1,0:T(8,128)(2,1)S(1)}, bf16[4,128,768]{2,1,0:T(8,128)(2,1)S(1)}, u32[]{:S(2)}, u32[]{:S(2)}) collective-permute-start(bf16[4,128,768]{2,1,0:T(8,128)(2,1)S(1)} %stack.203.refs_8_.refs_0_.refs_1_), channel_id=1, source_target_pairs={{0,8},{4,20},{8,0},{12,28},{16,24},{20,4},{24,16},{28,12},{1,9},{5... | collective-permute-start | bytes 2359304 | tf_op jit(solution)/shard_map/ppermute | solution.py:677
  165.9 20.5 %collective-permute-start.14 = (bf16[8,128,768]{2,1,0:T(8,128)(2,1)S(1)}, bf16[8,128,768]{2,1,0:T(8,128)(2,1)S(1)}, u32[]{:S(2)}, u32[]{:S(2)}) collective-permute-start(bf16[8,128,768]{2,1,0:T(8,128)(2,1)S(1)} %stack.204.refs_8_.refs_0_), channel_id=1, source_target_pairs={{0,16},{4,12},{8,24},{12,4},{16,0},{20,28},{24,8},{28,20},{1,17},{... | collective-permute-start | bytes 4718600 | tf_op jit(solution)/shard_map/ppermute | solution.py:677
  189.0 6.3 %copy-start.10 = (bf16[16,128,768]{2,1,0:T(8,128)(2,1)}, bf16[16,128,768]{2,1,0:T(8,128)(2,1)S(1)}, u32[]{:S(2)}) copy-start(bf16[16,128,768]{2,1,0:T(8,128)(2,1)S(1)} %stack.205.refs_8_) | copy-start | bytes 9437188
  189.0 37.4 %collective-permute-start.17 = (bf16[16,128,768]{2,1,0:T(8,128)(2,1)S(1)}, bf16[16,128,768]{2,1,0:T(8,128)(2,1)}, u32[]{:S(2)}, u32[]{:S(2)}) collective-permute-start(bf16[16,128,768]{2,1,0:T(8,128)(2,1)S(1)} %stack.205.refs_8_), channel_id=1, source_target_pairs={{0,4},{4,0},{1,5},{5,1},{2,6},{6,2},{3,7},{7,3},{8,12},{12,8},{9,1... | collective-permute-start | bytes 9437192 | tf_op jit(solution)/shard_map/ppermute | solution.py:698
  193.5 12.4 %collective-permute-start.15 = (bf16[512,768]{1,0:T(8,128)(2,1)}, bf16[512,768]{1,0:T(8,128)(2,1)S(1)}, u32[]{:S(2)}, u32[]{:S(2)}) collective-permute-start(bf16[512,768]{1,0:T(8,128)(2,1)} %get-tuple-element.79), channel_id=1, source_target_pairs={{0,0},{1,1},{2,4},{3,5},{4,2},{5,3},{6,6},{7,7},{8,8},{9,9},{10,12... | collective-permute-start | bytes 2359304 | tf_op jit(solution)/shard_map/ppermute | solution.py:665
  195.3 28.8 %collective-permute-start.16 = (bf16[512,768]{1,0:T(8,128)(2,1)}, bf16[512,768]{1,0:T(8,128)(2,1)S(1)}, u32[]{:S(2)}, u32[]{:S(2)}) collective-permute-start(bf16[512,768]{1,0:T(8,128)(2,1)} %get-tuple-element.80), channel_id=1, source_target_pairs={{0,1},{1,0},{2,5},{3,4},{4,3},{5,2},{6,7},{7,6},{8,9},{9,8},{10,13... | collective-permute-start | bytes 2359304 | tf_op jit(solution)/shard_map/ppermute | solution.py:665
  234.1 53.5 %copy-start.19 = (bf16[192,1024]{1,0:T(8,128)(2,1)S(1)}, bf16[192,1024]{1,0:T(8,128)(2,1)}, u32[]{:S(2)}) copy-start(bf16[192,1024]{1,0:T(8,128)(2,1)} %get-tuple-element.75.refs_4_.refs_0_.refs_2_) | copy-start | bytes 1179652
  234.1 53.5 %copy-start.33 = (bf16[192,1024]{1,0:T(8,128)(2,1)S(1)}, bf16[192,1024]{1,0:T(8,128)(2,1)}, u32[]{:S(2)}) copy-start(bf16[192,1024]{1,0:T(8,128)(2,1)} %get-tuple-element.76.refs_2_.refs_1_) | copy-start | bytes 1179652
  234.1 53.5 %copy-start.35 = (bf16[192,1024]{1,0:T(8,128)(2,1)S(1)}, bf16[192,1024]{1,0:T(8,128)(2,1)}, u32[]{:S(2)}) copy-start(bf16[192,1024]{1,0:T(8,128)(2,1)} %get-tuple-element.78.refs_2_.refs_3_) | copy-start | bytes 1179652
  234.1 53.5 %copy-start.37 = (bf16[192,1024]{1,0:T(8,128)(2,1)S(1)}, bf16[192,1024]{1,0:T(8,128)(2,1)}, u32[]{:S(2)}) copy-start(bf16[192,1024]{1,0:T(8,128)(2,1)} %get-tuple-element.77.refs_2_) | copy-start | bytes 1179652
  290.5 11.3 %copy-start.71 = (bf16[1024,768]{1,0:T(8,128)(2,1)S(1)}, bf16[1024,768]{1,0:T(8,128)(2,1)}, u32[]{:S(2)}) copy-start(bf16[1024,768]{1,0:T(8,128)(2,1)} %get-tuple-element.92.x_ref) | copy-start | bytes 4718596
  301.8 14.0 %copy-start.44 = (bf16[4,4,128,768]{3,2,1,0:T(8,128)(2,1)}, bf16[4,4,128,768]{3,2,1,0:T(8,128)(2,1)S(1)}, u32[]{:S(2)}) copy-start(bf16[4,4,128,768]{3,2,1,0:T(8,128)(2,1)S(1)} %get-tuple-element.90.refs_0_.mine) | copy-start | bytes 9437188
  319.5 6.0 %copy-start.45 = (bf16[4,4,128,768]{3,2,1,0:T(8,128)(2,1)S(1)}, bf16[4,4,128,768]{3,2,1,0:T(8,128)(2,1)}, u32[]{:S(2)}) copy-start(bf16[4,4,128,768]{3,2,1,0:T(8,128)(2,1)} %copy-done.44) | copy-start | bytes 9437188
  319.5 5.9 %collective-permute-start.20 = (bf16[4,4,128,768]{3,2,1,0:T(8,128)(2,1)}, bf16[4,4,128,768]{3,2,1,0:T(8,128)(2,1)S(1)}, u32[]{:S(2)}, u32[]{:S(2)}) collective-permute-start(bf16[4,4,128,768]{3,2,1,0:T(8,128)(2,1)} %copy-done.70), channel_id=1, source_target_pairs={{0,4},{4,0},{1,5},{5,1},{2,6},{6,2},{3,7},{7,3},{8,12},{12,8},{9,1... | collective-permute-start | bytes 9437192 | tf_op jit(solution)/shard_map/ppermute | solution.py:710
  331.5 36.7 %collective-permute-start.22 = (bf16[2,4,128,768]{3,2,1,0:T(8,128)(2,1)}, bf16[2,4,128,768]{3,2,1,0:T(8,128)(2,1)S(1)}, u32[]{:S(2)}, u32[]{:S(2)}) collective-permute-start(bf16[2,4,128,768]{3,2,1,0:T(8,128)(2,1)} %get-tuple-element.95.refs_12_), channel_id=1, source_target_pairs={{0,16},{4,12},{8,24},{12,4},{16,0},{20,28},{24,8},{28,20},{1,17},{... | collective-permute-start | bytes 4718600 | tf_op jit(solution)/shard_map/ppermute | solution.py:677
  334.1 40.5 %collective-permute-start.19 = (bf16[512,768]{1,0:T(8,128)(2,1)}, bf16[512,768]{1,0:T(8,128)(2,1)}, u32[]{:S(2)}, u32[]{:S(2)}) collective-permute-start(bf16[512,768]{1,0:T(8,128)(2,1)} %get-tuple-element.138), channel_id=1, source_target_pairs={{1,0},{0,1},{5,2},{4,3},{3,4},{2,5},{7,6},{6,7},{9,8},{8,9},{13,10... | collective-permute-start | bytes 2359304 | tf_op jit(solution)/shard_map/ppermute | solution.py:668
  341.4 33.3 %collective-permute-start.18 = (bf16[512,768]{1,0:T(8,128)(2,1)}, bf16[512,768]{1,0:T(8,128)(2,1)}, u32[]{:S(2)}, u32[]{:S(2)}) collective-permute-start(bf16[512,768]{1,0:T(8,128)(2,1)} %get-tuple-element.139), channel_id=1, source_target_pairs={{0,0},{1,1},{4,2},{5,3},{2,4},{3,5},{6,6},{7,7},{8,8},{9,9},{12,10... | collective-permute-start | bytes 2359304 | tf_op jit(solution)/shard_map/ppermute | solution.py:668
  348.8 20.6 %copy-start.31 = (bf16[2,4,128,768]{3,2,1,0:T(8,128)(2,1)S(1)}, bf16[2,4,128,768]{3,2,1,0:T(8,128)(2,1)}, u32[]{:S(2)}) copy-start(bf16[2,4,128,768]{3,2,1,0:T(8,128)(2,1)} %copy-done.30) | copy-start | bytes 4718596
  373.2 5.8 %copy-start.42 = (bf16[4,128,768]{2,1,0:T(8,128)(2,1)}, bf16[4,128,768]{2,1,0:T(8,128)(2,1)S(1)}, u32[]{:S(2)}) copy-start(bf16[4,128,768]{2,1,0:T(8,128)(2,1)S(1)} %get-tuple-element.102.refs_12_) | copy-start | bytes 2359300
  373.2 45.4 %collective-permute-start.25 = (bf16[4,128,768]{2,1,0:T(8,128)(2,1)S(1)}, bf16[4,128,768]{2,1,0:T(8,128)(2,1)S(1)}, u32[]{:S(2)}, u32[]{:S(2)}) collective-permute-start(bf16[4,128,768]{2,1,0:T(8,128)(2,1)S(1)} %get-tuple-element.102.refs_12_), channel_id=1, source_target_pairs={{0,8},{4,20},{8,0},{12,28},{16,24},{20,4},{24,16},{28,12},{1,9},{5... | collective-permute-start | bytes 2359304 | tf_op jit(solution)/shard_map/ppermute | solution.py:677
  379.0 63.0 %collective-permute-start.21 = (bf16[2,192,1024]{2,1,0:T(8,128)(2,1)}, bf16[2,192,1024]{2,1,0:T(8,128)(2,1)}, u32[]{:S(2)}, u32[]{:S(2)}) collective-permute-start(bf16[2,192,1024]{2,1,0:T(8,128)(2,1)} %get-tuple-element.98), channel_id=1, source_target_pairs={{0,4},{4,0},{1,5},{5,1},{2,6},{6,2},{3,7},{7,3},{8,12},{12,8},{9,1... | collective-permute-start | bytes 2359304 | tf_op jit(solution)/shard_map/ppermute | solution.py:846
  398.3 49.5 %collective-permute-start.24 = (bf16[2,192,1024]{2,1,0:T(8,128)(2,1)}, bf16[2,192,1024]{2,1,0:T(8,128)(2,1)}, u32[]{:S(2)}, u32[]{:S(2)}) collective-permute-start(bf16[2,192,1024]{2,1,0:T(8,128)(2,1)} %get-tuple-element.110), channel_id=1, source_target_pairs={{0,4},{4,0},{1,5},{5,1},{2,6},{6,2},{3,7},{7,3},{8,12},{12,8},{9,1... | collective-permute-start | bytes 2359304 | tf_op jit(solution)/shard_map/ppermute | solution.py:846
  398.9 19.8 %copy-start.21 = (bf16[4,128,768]{2,1,0:T(8,128)(2,1)S(1)}, bf16[4,128,768]{2,1,0:T(8,128)(2,1)}, u32[]{:S(2)}) copy-start(bf16[4,128,768]{2,1,0:T(8,128)(2,1)} %copy-done.20) | copy-start | bytes 2359300
  398.9 19.8 %copy-start.43 = (f32[192,1024]{1,0:T(8,128)S(1)}, f32[192,1024]{1,0:T(8,128)}, u32[]{:S(2)}) copy-start(f32[192,1024]{1,0:T(8,128)} %get-tuple-element.108.refs_0_) | copy-start | bytes 2359300
  418.5 33.6 %collective-permute-start.23 = (bf16[2,192,1024]{2,1,0:T(8,128)(2,1)}, bf16[2,192,1024]{2,1,0:T(8,128)(2,1)}, u32[]{:S(2)}, u32[]{:S(2)}) collective-permute-start(bf16[2,192,1024]{2,1,0:T(8,128)(2,1)} %get-tuple-element.105), channel_id=1, source_target_pairs={{0,4},{4,0},{1,5},{5,1},{2,6},{6,2},{3,7},{7,3},{8,12},{12,8},{9,1... | collective-permute-start | bytes 2359304 | tf_op jit(solution)/shard_map/ppermute | solution.py:846
  422.1 19.9 %copy-start.5 = (bf16[1024,768]{1,0:T(8,128)(2,1)S(1)}, bf16[1024,768]{1,0:T(8,128)(2,1)}, u32[]{:S(2)}) copy-start(bf16[1024,768]{1,0:T(8,128)(2,1)} %copy-done.2) | copy-start | bytes 4718596
  441.5 14.2 %collective-permute-start.26 = (bf16[2,192,1024]{2,1,0:T(8,128)(2,1)}, bf16[2,192,1024]{2,1,0:T(8,128)(2,1)S(1)}, u32[]{:S(2)}, u32[]{:S(2)}) collective-permute-start(bf16[2,192,1024]{2,1,0:T(8,128)(2,1)} %get-tuple-element.119), channel_id=1, source_target_pairs={{0,4},{4,0},{1,5},{5,1},{2,6},{6,2},{3,7},{7,3},{8,12},{12,8},{9,1... | collective-permute-start | bytes 2359304 | tf_op jit(solution)/shard_map/ppermute | solution.py:846
  458.5 18.1 %copy-start.59 = (bf16[128,768]{1,0:T(8,128)(2,1)S(1)}, bf16[128,768]{1,0:T(8,128)(2,1)}, u32[]{:S(2)}) copy-start(bf16[128,768]{1,0:T(8,128)(2,1)} %copy-done.58) | copy-start | bytes 589828
  458.7 18.0 %copy-start.72 = (bf16[4,4,72,768]{3,2,1,0:T(8,128)(2,1)}, bf16[4,4,72,768]{3,2,1,0:T(8,128)(2,1)S(1)}, u32[]{:S(2)}) copy-start(bf16[4,4,72,768]{3,2,1,0:T(8,128)(2,1)S(1)} %get-tuple-element.137.refs_6_) | copy-start | bytes 5308420
  458.7 22.8 %collective-permute-start.31 = (bf16[4,4,72,768]{3,2,1,0:T(8,128)(2,1)S(1)}, bf16[4,4,72,768]{3,2,1,0:T(8,128)(2,1)S(1)}, u32[]{:S(2)}, u32[]{:S(2)}) collective-permute-start(bf16[4,4,72,768]{3,2,1,0:T(8,128)(2,1)S(1)} %get-tuple-element.137.refs_6_), channel_id=1, source_target_pairs={{0,4},{4,0},{1,5},{5,1},{2,6},{6,2},{3,7},{7,3},{8,12},{12,8},{9,1... | collective-permute-start | bytes 5308424 | tf_op jit(solution)/shard_map/ppermute | solution.py:710
  459.4 9.7 %collective-permute-start.27 = (bf16[128,768]{1,0:T(8,128)(2,1)S(1)}, bf16[128,768]{1,0:T(8,128)(2,1)S(1)}, u32[]{:S(2)}, u32[]{:S(2)}) collective-permute-start(bf16[128,768]{1,0:T(8,128)(2,1)S(1)} %copy-done.67), channel_id=1, source_target_pairs={{0,1},{1,2},{2,3},{3,0},{4,5},{5,6},{6,7},{7,4},{8,9},{9,10},{10,1... | collective-permute-start | bytes 589832 | tf_op jit(solution)/shard_map/ppermute | solution.py:680
  459.5 17.1 %collective-permute-start.28 = (bf16[128,768]{1,0:T(8,128)(2,1)S(1)}, bf16[128,768]{1,0:T(8,128)(2,1)S(1)}, u32[]{:S(2)}, u32[]{:S(2)}) collective-permute-start(bf16[128,768]{1,0:T(8,128)(2,1)S(1)} %copy-done.65), channel_id=1, source_target_pairs={{0,2},{1,3},{2,0},{3,1},{4,6},{5,7},{6,4},{7,5},{8,10},{9,11},{10,... | collective-permute-start | bytes 589832 | tf_op jit(solution)/shard_map/ppermute | solution.py:680
  460.2 16.4 %collective-permute-start.29 = (bf16[128,768]{1,0:T(8,128)(2,1)S(1)}, bf16[128,768]{1,0:T(8,128)(2,1)S(1)}, u32[]{:S(2)}, u32[]{:S(2)}) collective-permute-start(bf16[128,768]{1,0:T(8,128)(2,1)S(1)} %copy-done.63), channel_id=1, source_target_pairs={{0,3},{1,0},{2,1},{3,2},{4,7},{5,4},{6,5},{7,6},{8,11},{9,8},{10,9... | collective-permute-start | bytes 589832 | tf_op jit(solution)/shard_map/ppermute | solution.py:680
  482.5 13.1 %collective-permute-start.33 = (bf16[2,4,72,768]{3,2,1,0:T(8,128)(2,1)S(1)}, bf16[2,4,72,768]{3,2,1,0:T(8,128)(2,1)S(1)}, u32[]{:S(2)}, u32[]{:S(2)}) collective-permute-start(bf16[2,4,72,768]{3,2,1,0:T(8,128)(2,1)S(1)} %get-tuple-element.127), channel_id=1, source_target_pairs={{0,16},{4,12},{8,24},{12,4},{16,0},{20,28},{24,8},{28,20},{1,17},{... | collective-permute-start | bytes 2654216 | tf_op jit(solution)/shard_map/ppermute | solution.py:677
  483.4 27.8 %collective-permute-start.30 = (bf16[512,768]{1,0:T(8,128)(2,1)S(1)}, bf16[512,768]{1,0:T(8,128)(2,1)S(1)}, u32[]{:S(2)}, u32[]{:S(2)}) collective-permute-start(bf16[512,768]{1,0:T(8,128)(2,1)S(1)} %finish.2.refs_0_), channel_id=1, source_target_pairs={{0,0},{1,1},{4,2},{5,3},{2,4},{3,5},{6,6},{7,7},{8,8},{9,9},{12,10... | collective-permute-start | bytes 2359304 | tf_op jit(solution)/shard_map/ppermute | solution.py:668
  489.0 25.2 %collective-permute-start.32 = (bf16[512,768]{1,0:T(8,128)(2,1)S(1)}, bf16[512,768]{1,0:T(8,128)(2,1)S(1)}, u32[]{:S(2)}, u32[]{:S(2)}) collective-permute-start(bf16[512,768]{1,0:T(8,128)(2,1)S(1)} %finish.3.refs_0_), channel_id=1, source_target_pairs={{1,0},{0,1},{5,2},{4,3},{3,4},{2,5},{7,6},{6,7},{9,8},{8,9},{13,10... | collective-permute-start | bytes 2359304 | tf_op jit(solution)/shard_map/ppermute | solution.py:668
  495.8 8.4 %collective-permute-start.34 = (bf16[4,72,768]{2,1,0:T(8,128)(2,1)S(1)}, bf16[4,72,768]{2,1,0:T(8,128)(2,1)S(1)}, u32[]{:S(2)}, u32[]{:S(2)}) collective-permute-start(bf16[4,72,768]{2,1,0:T(8,128)(2,1)S(1)} %get-tuple-element.129), channel_id=1, source_target_pairs={{0,8},{4,20},{8,0},{12,28},{16,24},{20,4},{24,16},{28,12},{1,9},{5... | collective-permute-start | bytes 1327112 | tf_op jit(solution)/shard_map/ppermute | solution.py:677
  504.9 16.8 %collective-permute-start.35 = (bf16[72,768]{1,0:T(8,128)(2,1)S(1)}, bf16[72,768]{1,0:T(8,128)(2,1)S(1)}, u32[]{:S(2)}, u32[]{:S(2)}) collective-permute-start(bf16[72,768]{1,0:T(8,128)(2,1)S(1)} %get-tuple-element.131), channel_id=1, source_target_pairs={{0,1},{1,2},{2,3},{3,0},{4,5},{5,6},{6,7},{7,4},{8,9},{9,10},{10,1... | collective-permute-start | bytes 331784 | tf_op jit(solution)/shard_map/ppermute | solution.py:680
  508.8 23.1 %collective-permute-start.36 = (bf16[72,768]{1,0:T(8,128)(2,1)S(1)}, bf16[72,768]{1,0:T(8,128)(2,1)S(1)}, u32[]{:S(2)}, u32[]{:S(2)}) collective-permute-start(bf16[72,768]{1,0:T(8,128)(2,1)S(1)} %get-tuple-element.132), channel_id=1, source_target_pairs={{0,2},{1,3},{2,0},{3,1},{4,6},{5,7},{6,4},{7,5},{8,10},{9,11},{10,... | collective-permute-start | bytes 331784 | tf_op jit(solution)/shard_map/ppermute | solution.py:680
  508.8 23.1 %collective-permute-start.37 = (bf16[72,768]{1,0:T(8,128)(2,1)S(1)}, bf16[72,768]{1,0:T(8,128)(2,1)S(1)}, u32[]{:S(2)}, u32[]{:S(2)}) collective-permute-start(bf16[72,768]{1,0:T(8,128)(2,1)S(1)} %get-tuple-element.133), channel_id=1, source_target_pairs={{0,3},{1,0},{2,1},{3,2},{4,7},{5,4},{6,5},{7,6},{8,11},{9,8},{10,9... | collective-permute-start | bytes 331784 | tf_op jit(solution)/shard_map/ppermute | solution.py:680
  (56 other events, 108.4 us)
Sparse Core Ops, SparseCore 0:
  33.3 121.1 all-gather.2
  319.6 140.8 reduce-scatter.1

commit v3 on v2

--- a/solution.py
+++ b/solution.py
@@ -14,6 +14,7 @@
 AUG = 16
 PIECES = 4
 COST = 16
+CHUNK = 512
 MASK = 2.0**99
 LOW = jnp.bfloat16
 WIDE = jnp.float32
@@ -28,6 +29,10 @@
     return pl.CostEstimate(
         flops=flops // scale, bytes_accessed=bytes_accessed // scale, transcendentals=transcendentals // scale
     )
+
+
+def far(*arrays):
+    return [pltpu.with_memory_space_constraint(a, pltpu.HBM) for a in arrays]
 
 
 def split3(x):
@@ -97,14 +102,14 @@
             jax.ShapeDtypeStruct((heads, 1, nq), WIDE),
         ],
         scratch_shapes=[pltpu.VMEM((nk, HEAD_DIM + AUG), LOW)],
-        compiler_params=pltpu.CompilerParams(vmem_limit_bytes=56 << 20),
+        compiler_params=pltpu.CompilerParams(vmem_limit_bytes=28 << 20),
         cost_estimate=cost(
             flops=16 * heads * nq * nk * HEAD_DIM,
             bytes_accessed=4 * heads * HEAD_DIM * (nq + nk),
             transcendentals=heads * nq * nk,
         ),
         name="attend_forward",
-    )(q, qa, *kvs, *kvs, *kas, *after)
+    )(*far(q), qa, *far(*kvs), *far(*kvs), *kas, *after)
 
 
 def backward_kernel(parts, *refs):
@@ -116,7 +121,6 @@
     keys, values = refs[6 + 4 * parts :]
     nq = q_ref.shape[1]
     at = 0
-    key_list = []
     for k_ref, v_ref, ka_ref in zip(k_refs, v_refs, ka_refs):
         n = k_ref.shape[1]
         keys[at : at + n] = jnp.concatenate(
@@ -125,25 +129,27 @@
         values[at : at + n] = jnp.concatenate(
             [v_ref[...], put_rows(jnp.zeros((AUG, n), LOW), 0, [ones_row(n)] * 3)], axis=0
         ).T
-        key_list.append(k_ref[...])
         at += n
     grads, queries = g_ref[...], q_ref[...]
     delta = jnp.sum(grads.astype(WIDE) * o_ref[...].astype(WIDE), axis=0, keepdims=True)
     query_aug = jnp.concatenate([queries, put_rows(qa_ref[...], 2, split3(-lse_ref[0]))], axis=0)
     grad_aug = jnp.concatenate([grads, put_rows(jnp.zeros((AUG, nq), LOW), 0, split3(-delta))], axis=0)
-    probs = jnp.exp(dot(keys[...], query_aug, 1, 0))
-    prob_grads = dot(values[...], grad_aug, 1, 0)
-    low_probs = probs.astype(LOW)
-    score_grads = (probs * prob_grads).astype(LOW)
-    dq_ref[...] = dot(jnp.concatenate(key_list, axis=1), score_grads, 1, 0) * HEAD_DIM ** (-0.5)
-    dv = dot(grads, low_probs, 1, 1)
-    dk = dot(queries, score_grads, 1, 1)
     at = 0
-    for dkv_ref in dkv_refs:
-        n = dkv_ref.shape[2]
-        dkv_ref[0] = dk[:, at : at + n].astype(dkv_ref.dtype)
-        dkv_ref[1] = dv[:, at : at + n].astype(dkv_ref.dtype)
-        at += n
+    dq = jnp.zeros((HEAD_DIM, nq), WIDE)
+    for k_ref, dkv_ref in zip(k_refs, dkv_refs):
+        n = k_ref.shape[1]
+        step = min(n, CHUNK)
+        for start in range(0, n, step):
+            lines = slice(at, at + step)
+            spot = slice(start, start + step)
+            probs = jnp.exp(dot(keys[lines], query_aug, 1, 0))
+            prob_grads = dot(values[lines], grad_aug, 1, 0)
+            score_grads = (probs * prob_grads).astype(LOW)
+            dq += dot(k_ref[:, spot], score_grads, 1, 0)
+            dkv_ref[0, :, spot] = dot(score_grads, queries, 1, 1).T.astype(dkv_ref.dtype)
+            dkv_ref[1, :, spot] = dot(probs.astype(LOW), grads, 1, 1).T.astype(dkv_ref.dtype)
+            at += step
+    dq_ref[...] = dq * HEAD_DIM ** (-0.5)
 
 
 def attend_backward(q, g, o, lse, qa, kvs, kas, types, after, first, heads):
@@ -157,8 +163,8 @@
         in_specs=[
             head_block(nq, first),
             head_block(nq, first),
-            head_block(nq, 0),
-            pl.BlockSpec((1, 1, nq), lambda h: (h, 0, 0)),
+            head_block(nq, first),
+            pl.BlockSpec((1, 1, nq), lambda h: (h + first, 0, 0)),
             whole_block(AUG, nq),
         ]
         + [head_block(n, first) for n in sizes]
@@ -170,14 +176,14 @@
         out_shape=[jax.ShapeDtypeStruct((width, nq), WIDE)]
         + [jax.ShapeDtypeStruct((2, width, n), t) for n, t in zip(sizes, types)],
         scratch_shapes=[pltpu.VMEM((nk, HEAD_DIM + AUG), LOW)] * 2,
-        compiler_params=pltpu.CompilerParams(vmem_limit_bytes=60 << 20),
+        compiler_params=pltpu.CompilerParams(vmem_limit_bytes=24 << 20),
         cost_estimate=cost(
             flops=30 * heads * nq * nk * HEAD_DIM,
             bytes_accessed=8 * width * (nq + nk),
             transcendentals=heads * nq * nk,
         ),
         name="attend_backward",
-    )(q, g, o, lse, qa, *kvs, *kvs, *kas, *after)
+    )(*far(q, g, o), lse, qa, *far(*kvs), *far(*kvs), *kas, *after)
     return out[0], out[1:]
 
 
@@ -238,42 +244,68 @@
     return inverse * (scaled - first_mean - normed * second_mean)
 
 
-def middle_kernel(pieces, *refs):
-    att_refs = refs[:pieces]
-    x_ref, top_ref, vec_ref, out_w, gu_w, down_w = refs[pieces : pieces + 6]
-    o_ref, low_ref, hid_ref, gug_ref, mix_ref, res_ref, proj_ref, att_ref, sums_ref = refs[pieces + 6 : pieces + 15]
-    kept = refs[pieces + 15]
+def middle_kernel(parts, few, *refs):
+    att_in, x_ref, top_ref, pack = refs[:4]
+    low_ref, hid_ref, gug_ref, mix_ref, res_ref, proj_ref, att_ref, sums_ref = refs[-12 - parts : -4 - parts]
+    o_refs, kept, wide, out_w, vec_ref = refs[-4 - parts : -4], *refs[-4:]
+    blocks, width = pack.shape[0], pack.shape[3]
+    lines = width // pack.shape[1]
+    if few:
+
+        @pl.when(pl.program_id(0) == 0)
+        def _():
+            total = jnp.zeros((8, width), WIDE)
+            for j in range(blocks):
+                for i in range(pack.shape[1]):
+                    rows = pack[j, i, 3 * lines :].astype(WIDE)
+                    spot = (i * blocks + j) * few
+                    wide[spot : spot + few] = rows[:few]
+                    total += rows[few : few + 8]
+            out_w[...] = wide[...].astype(LOW)
+            vec_ref[...] = total
+
+    else:
+        out_w, vec_ref = refs[4:6]
     gain_one, shift_one, gain_two, shift_two = (vec_ref[i : i + 1] for i in range(4))
-    blocks, width = down_w.shape[0], down_w.shape[2]
-    projected = dot(jnp.concatenate([r[...] for r in att_refs], axis=0), out_w[...], 0, 1)
+
+    def weight(j, kind):
+        return pack[j, :, kind * lines : (kind + 1) * lines].reshape(width, width)
+
+    projected = dot(att_in[...], out_w[...], 0, 1)
     x_one, normed_one, inverse_one = norm_forward(x_ref[...].astype(WIDE) + projected, gain_one, shift_one)
     x_low = x_one.astype(LOW)
     low_ref[...] = x_low
     mixed = jnp.zeros_like(x_one)
     for j in range(blocks):
-        both = dot(x_low, gu_w[j], 1, 0)
-        gate, up = both[:, :width], both[:, width:]
+        gate = dot(x_low, weight(j, 0), 1, 0)
+        up = dot(x_low, weight(j, 1), 1, 0)
         sigma = 0.5 * jnp.tanh(0.5 * gate) + 0.5
         activated = gate * sigma
         kept[j, :, :width] = up * (sigma + activated * (1.0 - sigma))
         kept[j, :, width:] = activated
         hidden = (activated * up).astype(LOW)
         hid_ref[j] = hidden
-        mixed += dot(hidden, down_w[j], 1, 1)
+        mixed += dot(hidden, weight(j, 2), 1, 1)
     result, normed_two, inverse_two = norm_forward(x_one + mixed, gain_two, shift_two)
-    o_ref[...] = result.astype(LOW)
+    steps = pl.num_programs(0) // parts
+    for k, o_ref in enumerate(o_refs):
+
+        @pl.when(pl.program_id(0) // steps == k)
+        def _():
+            o_ref[...] = result.astype(LOW)
+
     grad_top = top_ref[...].astype(WIDE)
     d_resid_two = norm_backward(grad_top, normed_two, inverse_two, gain_two)
     mix_grad = d_resid_two.astype(LOW)
     mix_ref[...] = mix_grad
     d_x_one = d_resid_two
     for j in range(blocks):
-        hidden_grad = dot(mix_grad, down_w[j], 1, 0)
+        hidden_grad = dot(mix_grad, weight(j, 2), 1, 0)
         gate_grad = (hidden_grad * kept[j, :, :width]).astype(LOW)
         up_grad = (hidden_grad * kept[j, :, width:]).astype(LOW)
-        grads = jnp.concatenate([gate_grad, up_grad], axis=1)
-        gug_ref[j] = grads
-        d_x_one += dot(grads, gu_w[j], 1, 1)
+        gug_ref[j, :, :width] = gate_grad
+        gug_ref[j, :, width:] = up_grad
+        d_x_one += dot(gate_grad, weight(j, 0), 1, 1) + dot(up_grad, weight(j, 1), 1, 1)
     d_resid_one = norm_backward(d_x_one, normed_one, inverse_one, gain_one)
     res_ref[...] = d_resid_one
     proj_grad = d_resid_one.astype(LOW)
@@ -297,24 +329,26 @@
         sums_ref[...] += sums
 
 
-def middle(attended, x, grad_top, vectors, out_t, gu, down):
+def middle(attended, x, grad_top, pack, small, parts):
     n, width = x.shape
-    blocks, _, units = down.shape
-    step = min(n, 256)
-    pieces = len(attended)
+    blocks, units = pack.shape[0], width
+    step = min(n // parts, 256)
+    steps = n // step // parts
+    few = 0 if small else width // (blocks * pack.shape[1])
 
     def kept_block(shape):
         return pl.BlockSpec(shape, lambda i: (0,) * len(shape), pipeline_mode=pl.Buffered(1))
 
+    def part_block(k):
+        return pl.BlockSpec((step, width), lambda i: (jnp.clip(i - k * steps, 0, steps - 1), 0))
+
     rows = pl.BlockSpec((step, width), lambda i: (i, 0))
-    return pl.pallas_call(
-        functools.partial(middle_kernel, pieces),
+    out = pl.pallas_call(
+        functools.partial(middle_kernel, parts, few),
         grid=(n // step,),
-        in_specs=[pl.BlockSpec((a.shape[0], step), lambda i: (0, i)) for a in attended]
-        + [rows, rows]
-        + [kept_block(a.shape) for a in (vectors, out_t, gu, down)],
+        in_specs=[pl.BlockSpec((width, step), lambda i: (0, i)), rows, rows]
+        + [kept_block(a.shape) for a in (pack,) + small],
         out_specs=[
-            rows,
             rows,
             pl.BlockSpec((blocks, step, units), lambda i: (0, i, 0)),
             pl.BlockSpec((blocks, step, 2 * units), lambda i: (0, i, 0)),
@@ -323,30 +357,38 @@
             rows,
             pl.BlockSpec((width, step), lambda i: (0, i)),
             pl.BlockSpec((8, width), lambda i: (0, 0)),
+        ]
+        + [part_block(k) for k in range(parts)],
+        out_shape=[
+            pltpu.HBM((n, width), LOW),
+            pltpu.HBM((blocks, n, units), LOW),
+            pltpu.HBM((blocks, n, 2 * units), LOW),
+            pltpu.HBM((n, width), LOW),
+            pltpu.HBM((n, width), WIDE),
+            pltpu.HBM((n, width), LOW),
+            pltpu.HBM((width, n), LOW),
+            jax.ShapeDtypeStruct((8, width), WIDE),
+        ]
+        + [pltpu.HBM((n // parts, width), LOW)] * parts,
+        scratch_shapes=[
+            pltpu.VMEM((blocks, step, 2 * units), WIDE),
+            pltpu.VMEM((width, width), WIDE),
+            pltpu.VMEM((width, width), LOW),
+            pltpu.VMEM((8, width), WIDE),
         ],
-        out_shape=[
-            jax.ShapeDtypeStruct((n, width), LOW),
-            jax.ShapeDtypeStruct((n, width), LOW),
-            jax.ShapeDtypeStruct((blocks, n, units), LOW),
-            jax.ShapeDtypeStruct((blocks, n, 2 * units), LOW),
-            jax.ShapeDtypeStruct((n, width), LOW),
-            jax.ShapeDtypeStruct((n, width), WIDE),
-            jax.ShapeDtypeStruct((n, width), LOW),
-            jax.ShapeDtypeStruct((width, n), LOW),
-            jax.ShapeDtypeStruct((8, width), WIDE),
-        ],
-        scratch_shapes=[pltpu.VMEM((blocks, step, 2 * units), WIDE)],
         compiler_params=pltpu.CompilerParams(vmem_limit_bytes=60 << 20),
         cost_estimate=cost(
             flops=2 * n * width * (2 * width + 6 * blocks * units), bytes_accessed=60 << 20, transcendentals=n * blocks * units
         ),
         name="middle",
-    )(*attended, x, grad_top, vectors, out_t, gu, down)
+    )(*far(attended, x, grad_top, pack), *small)
+    return out[:8], out[8:]
 
 
 def unturn_kernel(add, *refs):
     dq_ref, own_ref = refs[:2]
-    cos_ref, sin_ref, x_ref, grad_ref, g_ref = refs[-5:]
+    cos_ref, sin_ref, x_ref = refs[2 + add : 5 + add]
+    grad_ref, g_ref = refs[-2:]
     kind = pl.program_id(0)
     cosine, sine = cos_ref[...], -sin_ref[...]
 
@@ -371,7 +413,7 @@
         emit(total())
 
 
-def unturn(dq, own, others, cosine, sine, x):
+def unturn(dq, own, others, cosine, sine, x, after):
     n, width = x.shape
     count = dq.shape[0]
     pair = pl.BlockSpec((1, count, n), lambda i: (jnp.maximum(i - 1, 0), 0, 0))
@@ -379,7 +421,8 @@
     return pl.pallas_call(
         functools.partial(unturn_kernel, len(others)),
         grid=(3,),
-        in_specs=[whole_block(count, n), pair] + [pair] * len(others) + [table, table, whole_block(n, width)],
+        in_specs=[whole_block(count, n), pair] + [pair] * len(others) + [table, table, whole_block(n, width)]
+        + [pl.BlockSpec(memory_space=pl.ANY)] * len(after),
         out_specs=[
             pl.BlockSpec((1, count, n), lambda i: (i, 0, 0)),
             pl.BlockSpec((1, count, width), lambda i: (i, 0, 0)),
@@ -391,7 +434,7 @@
         compiler_params=pltpu.CompilerParams(vmem_limit_bytes=30 << 20),
         cost_estimate=cost(flops=6 * n * width * count, bytes_accessed=9 << 20, transcendentals=0),
         name="unturn",
-    )(dq, own, *others, cosine, sine, x)
+    )(dq, own, *others, cosine, sine, x, *after)
 
 
 def finish_kernel(groups, *refs):
@@ -560,7 +603,7 @@
     norm_ref, mine, send, turned, result, side = refs[pieces:]
     j = pl.program_id(0)
     lines, count = mine.shape[2], mix_ref.shape[1] // (2 * mine.shape[1])
-    extra = norm_ref.shape[2]
+    extra = norm_ref.shape[0]
     few = lines - count - extra
 
     @pl.when(j == 0)
@@ -575,12 +618,12 @@
             rows = result[pl.ds(pl.multiple_of(dp * count, 8), count)]
             small = side[pl.ds(pl.multiple_of((dp * pl.num_programs(0) + j) * few, 8), few)]
             out[0, p, :count] = rows.astype(LOW)
-            out[0, p, count:] = jnp.concatenate([small, norm_ref[dp, 0]], axis=0).astype(LOW)
-
-
-def side_grads(core, mix_grad, hidden, proj_grad, attended, norms, lines):
+            out[0, p, count:] = jnp.concatenate([small, norm_ref[...]], axis=0).astype(LOW)
+
+
+def side_grads(core, mix_grad, hidden, proj_grad, attended, norms, lines, chips):
     n, width = mix_grad.shape
-    blocks, chips = hidden.shape[0], norms.shape[0] // 2
+    blocks = hidden.shape[0]
     whole = pl.BlockSpec((n, width), lambda j: (0, 0))
     out = pl.BlockSpec((1, chips, lines, width), lambda j: (j, 0, 0, 0))
     return pl.pallas_call(
@@ -593,7 +636,7 @@
             whole,
         ]
         + [whole_block(*a.shape) for a in attended]
-        + [pl.BlockSpec((2 * chips, 1, norms.shape[2], width), lambda j: (0, j, 0, 0))],
+        + [whole_block(8, width)],
         out_specs=[out] * 2,
         out_shape=[jax.ShapeDtypeStruct((blocks, chips, lines, width), LOW)] * 2,
         scratch_shapes=[
@@ -604,7 +647,7 @@
         compiler_params=pltpu.CompilerParams(vmem_limit_bytes=40 << 20),
         cost_estimate=cost(flops=10 * n * width * width, bytes_accessed=16 << 20),
         name="side_grads",
-    )(core.reshape(1), mix_grad, hidden, proj_grad, *attended, norms)
+    )(core.reshape(1), *far(mix_grad, hidden, proj_grad, *attended), norms)
 
 
 def gate_up_kernel(x_ref, g_ref, *refs):
@@ -614,24 +657,30 @@
     def _():
         turned[...] = x_ref[...].T
 
-    out[0] = dot(turned[...], g_ref[0], 1, 0).astype(LOW)
-
-
-def gate_up_grads(x, grads, after):
+    made = dot(turned[...], g_ref[0], 1, 0).astype(LOW)
+    out[...] = made.reshape(out.shape)
+
+
+def gate_up_grads(x, grads, first, count, given, after, ways):
     n, width = x.shape
     blocks, _, both = grads.shape
+    free = pl.BlockSpec(memory_space=pl.ANY)
     return pl.pallas_call(
         gate_up_kernel,
-        grid=(blocks,),
-        in_specs=[pl.BlockSpec((n, width), lambda j: (0, 0)), pl.BlockSpec((1, n, both), lambda j: (j, 0, 0))]
-        + [pl.BlockSpec(memory_space=pl.ANY)] * len(after),
-        out_specs=pl.BlockSpec((1, width, both), lambda j: (j, 0, 0)),
-        out_shape=jax.ShapeDtypeStruct((blocks, width, both), LOW),
+        grid=(count,),
+        in_specs=[
+            pl.BlockSpec((n, width), lambda j: (0, 0)),
+            pl.BlockSpec((1, n, both), lambda j: (j + first, 0, 0)),
+        ]
+        + [free] * (len(given) + len(after)),
+        out_specs=pl.BlockSpec((ways, 1, width // ways, both), lambda j: (0, j + first, 0, 0)),
+        out_shape=pltpu.HBM((ways, blocks, width // ways, both), LOW),
+        input_output_aliases={2: 0} if given else {},
         scratch_shapes=[pltpu.VMEM((width, n), LOW)],
         compiler_params=pltpu.CompilerParams(vmem_limit_bytes=40 << 20),
-        cost_estimate=cost(flops=2 * n * width * blocks * both, bytes_accessed=24 << 20, scale=1),
+        cost_estimate=cost(flops=2 * n * width * count * both, bytes_accessed=12 << 20, scale=1),
         name="gate_up_grads",
-    )(x, grads, *after)
+    )(*far(x, grads, *given), *after)
 
 
 def local(
@@ -664,9 +713,14 @@
         at = jnp.stack([(z + k) % rows for k in range(rows)]).astype(jnp.int32)
         return [lax.ppermute(a, line, ring(k)) for k, a in enumerate(select(x, at, after))]
 
+    def send_back(parts):
+        return [lax.ppermute(part, line, [(b, a) for a, b in ring(k)]) for k, part in enumerate(parts)]
+
+    def settle(back):
+        return jnp.roll(jnp.stack(back), z, axis=0)
+
     def give_back(parts):
-        back = [lax.ppermute(part, line, [(b, a) for a, b in ring(k)]) for k, part in enumerate(parts)]
-        return jnp.roll(jnp.stack(back), z, axis=0)
+        return settle(send_back(parts))
 
     def hop(x, first):
         pairs = []
@@ -702,6 +756,9 @@
         mine, theirs = (a.reshape((chips, tp) + a.shape[1:]) for a in (mine, theirs))
         return arrange(mine, theirs, jnp.stack(place).astype(jnp.int32), cuts, after)
 
+    def gather_all(x):
+        return lax.all_gather(x, everyone, axis=0, tiled=False).reshape((tp, dp) + x.shape)
+
     pick = lambda a, i, axis: lax.dynamic_index_in_dim(a, i, axis, False)
     near_place = jnp.stack([chip, chip ^ mask_one, chip ^ mask_two, chip ^ 3]).astype(jnp.int32)
     line_place = jnp.stack([(z + k) % tp for k in range(tp)]).astype(jnp.int32)
@@ -732,18 +789,26 @@
     units = w_gate.shape[1]
     blocks = tp * units // width
     merged = by_hand and units == width
-    pad = -(no + 1) % 16
-    norm_row = jnp.concatenate([norm1_gain, norm1_shift, norm2_gain, norm2_shift])
-    norm_row = jnp.pad(norm_row, (0, width - 4 * no))[None]
-    small = jnp.concatenate([w_out.T, norm_row, jnp.zeros((pad, width), LOW)])
+    me = (chip * 2 + core) * tp + z
+    mine_at = me * no
+    vector_rows = jnp.stack([norm1_gain, norm1_shift, norm2_gain, norm2_shift])
+    if merged:
+        placed = jnp.where(jnp.arange(width) // no == me, jnp.tile(vector_rows, (1, dp * tp)), 0)
+        small = jnp.concatenate([w_out.T, placed, jnp.zeros((4, width), LOW)])
     brought = bring(tokens)
     x = jnp.concatenate(brought)
-    qkv_t = spread_near(spread_z(w_qkv.T, tuple(brought)))
-    qkv_t = spread_far(qkv_t)
-    qkv_t = spread_core(qkv_t, [(0, nq, False)])[0].reshape(3 * width, width)
-    gu = beside([w_gate, w_up], tuple(brought))
-    gu = lax.all_gather(gu, everyone, axis=0, tiled=False)
-    gu = gu.reshape(blocks, tp // blocks, width, 2, units).transpose(0, 2, 3, 1, 4).reshape(blocks, width, -1)
+    column = spread_z(w_qkv.T, tuple(brought[:1]))
+    qkv_t = spread_core(spread_far(spread_near(column), tuple(brought[1:])), [(0, nq, False)])[0]
+    qkv_t = qkv_t.reshape(3 * width, width)
+    if merged:
+        pack = gather_all(stack([w_gate, w_up, w_down.T, small]))
+        small = ()
+    else:
+        regroup = lambda a: a.reshape(blocks, tp // blocks, width, units).swapaxes(1, 2).reshape(blocks, dp, -1, width)
+        pack = jnp.concatenate([regroup(gather_all(a)) for a in (w_gate, w_up, w_down.T)], axis=2)
+        out_t = gather_all(w_out.T).swapaxes(0, 1).reshape(width, width)
+        vectors = gather_all(vector_rows).swapaxes(0, 1).reshape(dp * tp, 4, no).swapaxes(0, 1)
+        small = (out_t, jnp.pad(vectors.reshape(4, width).astype(WIDE), ((0, 4), (0, 0))))
 
     info = jnp.stack([segment_ids, positions])
     other = lax.ppermute(info, "core", SWAP)
@@ -784,74 +849,63 @@
         types = [LOW]
     q = project(qkv_t, x, cosine, sine, "q", 0)
     spans = [(i * HEADS // PIECES, HEADS // PIECES) for i in range(PIECES)]
-    late = stack([w_down.T, small] if merged else [small], (x,))
-    attended, lses = [], []
-    cuts = [(0, width // dp, True), (width // dp, small.shape[0], False)]
-    for i, span in enumerate(spans):
-        att, lse = attend_forward(q, query_aug, kvs, kas, (late,) if i else (), *span)
-        attended.append(att)
-        lses.append(lse)
-        if i == 0:
-            late = spread_z(late, (att,))
-            top_parts = bring(out_grad, (att, late))
-        if i == 1:
-            late = spread_near(late, (att,))
-        if i == 2:
-            late = spread_far(late, (att,))
-    late = spread_core(late, cuts if merged else [(0, small.shape[0], False)])
-    grad_top = stack(top_parts, (attended[-1],))
-    by_column = late[-1]
-    down = late[0] if merged else spread_core(w_down.T, [(0, width // dp, True)])[0]
-    down = down.reshape(blocks, tp // blocks, width, units).swapaxes(1, 2).reshape(blocks, width, -1)
-    out_t = by_column[:, :, :no].reshape(width, width)
-    vectors = by_column[:, :, no, : 4 * no].reshape(dp * tp, 4, no).swapaxes(0, 1).reshape(4, width)
-    vectors = jnp.pad(vectors.astype(WIDE), ((0, 4), (0, 0)))
-
-    output, x_low, hidden, gug, mix_grad, d_resid_one, proj_grad, att_grad, sums = middle(
-        attended, x, grad_top, vectors, out_t, gu, down
+    top_parts = bring(out_grad, tuple(far(kv)))
+    attended, lse = attend_forward(q, query_aug, kvs, kas, (), 0, HEADS)
+    grad_top = stack(top_parts, tuple(far(attended)))
+
+    (x_low, hidden, gug, mix_grad, d_resid_one, proj_grad, att_grad, sums), output = middle(
+        attended, x, grad_top, pack, small, rows
     )
-    output = give_back([output[k * piece : (k + 1) * piece] for k in range(rows)])
-
-    def ungroup(g, parts):
-        g = g.reshape(blocks, width, parts, tp // blocks, units).transpose(0, 3, 1, 2, 4)
-        return g.reshape(tp, dp, width // dp, parts * units)
-
-    norms = sums[:4].reshape(4, dp * tp, no).swapaxes(0, 1).reshape(dp, tp, 1, 4 * no)
+    returned = send_back(output)
+    output = settle(returned)
+
+    def ungroup(g):
+        g = g.reshape(blocks, width, tp // blocks, units).swapaxes(1, 2)
+        return g.reshape(tp, dp, width // dp, units)
+
     if merged:
-        norms = jnp.pad(norms, ((0, 0), (0, 0), (0, pad), (0, width - 4 * no)))
-        mine, send = side_grads(core, mix_grad, hidden, proj_grad, attended, norms, width // dp + no + pad + 1)
+        mine, send = side_grads(core, mix_grad, hidden, proj_grad, [attended], sums, width // dp + no + 8, chips)
     else:
-        norms = jnp.pad(norms.astype(LOW), ((0, 0), (0, 0), (0, pad), (0, width - 4 * no)))
-        g_out = dot(proj_grad, jnp.concatenate(attended), 0, 1).astype(LOW)
-        side = jnp.concatenate([g_out.reshape(dp, tp, no, width), norms], axis=2)
-        side = collapse_all(side.swapaxes(0, 1))
+        g_out = dot(proj_grad, attended, 0, 1).astype(LOW).reshape(dp, tp, no, width)
+        spread_sums = jnp.broadcast_to(sums.astype(LOW), (dp, tp, 8, width))
+        side = collapse_all(jnp.concatenate([g_out, spread_sums], axis=2).swapaxes(0, 1))
         g_down = jnp.einsum("td,jtf->jdf", mix_grad, hidden, preferred_element_type=WIDE).astype(LOW)
-        g_down = collapse_all(ungroup(g_down, 1))
+        g_down = collapse_all(ungroup(g_down))
         mine = mix_grad
-    g_gu = ungroup(gate_up_grads(x_low, gug, (mine,)), 2)
-    shared_gu = collapse_all(g_gu)
-    held = (g_gu,)
+    split = blocks // 2
+    g_gu = gate_up_grads(x_low, gug, 0, split, (), (mine,), dp)
+    held = ()
     if merged:
-        held = collapse_core(mine, send, 1, (g_gu,))
-
-    grads, parts = [], []
-    for i, ((start, count), att, lse) in enumerate(zip(spans, attended, lses)):
-        after = tuple(held) + ((output,) if i + 1 == PIECES else ())
-        dq, dkv = attend_backward(q, att_grad, att, lse, query_aug, kvs, kas, types, after, start, count)
+        held = collapse_core(mine, send, 1, tuple(far(g_gu)))
+    g_gu = gate_up_grads(x_low, gug, split, blocks - split, (g_gu,), tuple(held), dp)
+    g_gu = g_gu.reshape(dp, blocks, width // dp, 2, tp // blocks, units).transpose(0, 1, 4, 2, 3, 5)
+    g_gu = g_gu.reshape(dp, tp, width // dp, 2 * units)
+    shared_gu = lax.psum_scatter(g_gu, ("chip", "core"), scatter_dimension=0, tiled=False)
+    shared_gu = lax.psum_scatter(shared_gu, flat, scatter_dimension=0, tiled=False).astype(WIDE)
+    spans = [(i * HEADS // PIECES, HEADS // PIECES) for i in range(PIECES)]
+
+    dqs, grads, parts = [], [], []
+    for i, (start, count) in enumerate(spans):
+        after = tuple(held) + (tuple(far(g_gu)) if i == 0 else ()) + (tuple(far(*returned)) if i == 1 else ())
+        dq, dkv = attend_backward(q, att_grad, attended, lse, query_aug, kvs, kas, types, after, start, count)
         if merged and i == 0:
             held = collapse_far(*held, (dq,))
+        if merged and i == 1:
+            held = collapse_near(*held, (dq,))
         if merged and i == 2:
-            held = collapse_near(*held, (dq,))
+            total = collapse_z(held)
+            held = (total,)
         if members == 2:
             own_dkv, others = dkv[0], (lax.ppermute(dkv[1], "core", SWAP),)
         else:
             summed = lax.psum_scatter(dkv[0], ("zm", "core"), scatter_dimension=2, tiled=True)
             own_dkv, others = summed.astype(WIDE), ()
-        grad, part = unturn(dq, own_dkv, others, cosine, sine, x)
+        dqs.append((dq, own_dkv, others))
+    for i, (dq, own_dkv, others) in enumerate(dqs):
+        grad, part = unturn(dq, own_dkv, others, cosine, sine, x, ())
         grads.append(grad)
         parts.append(part)
     if merged:
-        total = collapse_z(held)
         g_down, side = total[: width // dp], total[width // dp :]
     g_qkv = jnp.concatenate(parts, axis=1).reshape(dp, tp, nq, width)
     if not by_hand:
@@ -861,14 +915,14 @@
     else:
         g_qkv = g_qkv.reshape(chips, 2, tp, nq, width)
         mine, send = pick(g_qkv, core, 1), pick(g_qkv, 1 - core, 1)
-        in_grad = [finish(grads, d_resid_one, qkv_t, (send,) + ((total,) if merged else ()), 0, piece)]
+        in_grad = [finish(grads, d_resid_one, qkv_t, (send,), 0, piece)]
         held = collapse_core(mine, send, 0, (in_grad[0],))
         for k in range(1, rows):
             in_grad.append(finish(grads, d_resid_one, qkv_t, (held[0],), k, piece))
         held = collapse_far(*held, (in_grad[-1],))
         g_qkv = collapse_z(collapse_near(*held))
         in_grad = give_back(in_grad)
-    vector_grads = side[no, : 4 * no].reshape(4, no)
+    vector_grads = lax.dynamic_slice_in_dim(side[no : no + 4], mine_at, no, 1)
     return (
         output,
         in_grad,

time: 548 us -> 464 us (0.85)
  local copies, waits for them, and re-layouts: 56.2 us -> 24.1 us
  starting transfers between devices: 81.5 us -> 58.1 us
  Pallas kernels: 238 us -> 225 us
  waiting for transfers between devices: 137 us -> 124 us
    unnamed x163 -> x85, local copies, waits for them, and re-layouts: 48.2 us -> 18.5 us
    ppermute x12 -> x9, starting transfers between devices: 43.2 us -> 18.6 us  [along(): return lax.ppermute(x, flat, [(i, (i + k) % tp) for i in range(tp)])]
    ppermute x4, waiting for transfers between devices: 35.4 us -> 25.5 us  [bring(): lax.ppermute(a, line, ring(k))]
    ppermute x8 -> x6, waiting for transfers between devices: 39 us -> 29.9 us  [hop(): return lax.ppermute(x, ('chip', 'core'), pairs)]
    ppermute x2, starting transfers between devices: 0.19 us -> 7.22 us  [collapse_core(): got = lax.ppermute(send, 'core', SWAP)]
    pallas_call x4, Pallas kernels: 77.8 us -> 71.3 us  [attend_backward(): pl.pallas_call(functools.partial(backward_kernel, parts), grid=(heads,),...]
    ppermute x4, waiting for transfers between devices: 2.97 us -> 9.05 us  [send_back(): lax.ppermute(part, line, [(b, a) for a, b in ring(k)])]
    ppermute x2, waiting for transfers between devices: 5.78 us -> 0.01 us  [collapse_core(): got = lax.ppermute(send, 'core', SWAP)]
  transfers between devices with their start and end apart: 40 -> 35, of which waited for: 17 -> 12; matrix products, arithmetic and copies ran while one was open for 3% -> 3% of each run, Pallas kernels for 29% -> 33%
where the time goes in v3:
time: 464 us; the launch traced here: 458 us
  Pallas kernels  225 us (48%)
  waiting for transfers between devices  124 us (27%)
  starting transfers between devices  58.1 us (13%)
  local copies, waits for them, and re-layouts  24.1 us (5%)
  between operations  15 us (3%)
  other arithmetic  12 us (3%)
    pallas_call x4, Pallas kernels, attend_backward(): pl.pallas_call(functools.partial(backward_kernel, parts), grid=(heads,),...  71.3 us
    ppermute x9, waiting for transfers between devices, along(): return lax.ppermute(x, flat, [(i, (i + k) % tp) for i in range(tp)])  56.1 us
    pallas_call x1, Pallas kernels, middle(): pl.pallas_call(functools.partial(middle_kernel, parts, few), grid=(n // s...  52.4 us
    pallas_call x1, Pallas kernels, attend_forward(): pl.pallas_call(functools.partial(forward_kernel, parts), grid=(heads,), i...  38.7 us
    ppermute x6, waiting for transfers between devices, hop(): return lax.ppermute(x, ('chip', 'core'), pairs)  29.9 us
    ppermute x4, waiting for transfers between devices, bring(): lax.ppermute(a, line, ring(k))  25.5 us
    pallas_call x2, Pallas kernels, gate_up_grads(): pl.pallas_call(gate_up_kernel, grid=(count,), in_specs=[pl.BlockSpec((n,...  19.1 us
    ppermute x9, starting transfers between devices, along(): return lax.ppermute(x, flat, [(i, (i + k) % tp) for i in range(tp)])  18.6 us
  transfers between devices with their start and end apart: 35, of which 12 were waited for; matrix products, arithmetic and copies ran while one was open for 3% of the time, Pallas kernels for 33%

profile of v3, /device:TPU:0, one launch (start us, length us, event | category | flops | bytes accessed | tf_op | source)
XLA Modules:
  0.0 457.7 jit_solution(14977729722631186541)
XLA Ops:
  9.0 0.9 copy-done.28
  9.9 0.9 copy-done.29
  10.8 0.9 copy-done.30
  14.1 5.3 %collective-permute-start.1 = (bf16[72,768]{1,0:T(8,128)(2,1)S(1)}, bf16[72,768]{1,0:T(8,128)(2,1)S(1)}, u32[]{:S(2)}, u32[]{:S(2)}) collective-permute-start(bf16[72,768]{1,0:T(8,128)(2,1)S(1)} %bitcast.91), channel_id=1, source_target_pairs={{0,2},{1,3},{2,0},{3,1},{4,6},{5,7},{6,4},{7,5},{8,10},{9,11},{10,... | collective-permute-start | bytes 331784 | tf_op jit(solution)/shard_map/ppermute | solution.py:734
  19.4 1.6 collective-permute-start
  21.0 2.2 collective-permute-start.2
  23.3 33.3 %collective-permute-done.1 = bf16[72,768]{1,0:T(8,128)(2,1)S(1)} collective-permute-done((bf16[72,768]{1,0:T(8,128)(2,1)S(1)}, bf16[72,768]{1,0:T(8,128)(2,1)S(1)}, u32[]{:S(2)}, u32[]{:S(2)}) %collective-permute-start.1) | collective-permute-done | bytes 110624 | tf_op jit(solution)/shard_map/ppermute | solution.py:734
  56.6 1.6 collective-permute-start.4
  58.2 16.6 %collective-permute-done.4.refs_1_ = bf16[4,72,768]{2,1,0:T(8,128)(2,1)S(1)} collective-permute-done((bf16[4,72,768]{2,1,0:T(8,128)(2,1)S(1)}, bf16[4,72,768]{2,1,0:T(8,128)(2,1)S(1)}, u32[]{:S(2)}, u32[]{:S(2)}) %collective-permute-start.4) | collective-permute-done | bytes 442400 | tf_op jit(solution)/shard_map/ppermute | solution.py:731
  74.8 1.6 collective-permute-start.5
  76.4 1.8 collective-permute-start.6
  78.2 25.4 %collective-permute-done.6.refs_2_ = bf16[512,768]{1,0:T(8,128)(2,1)S(1)} collective-permute-done((bf16[512,768]{1,0:T(8,128)(2,1)S(1)}, bf16[512,768]{1,0:T(8,128)(2,1)S(1)}, u32[]{:S(2)}, u32[]{:S(2)}) %collective-permute-start.6) | collective-permute-done | bytes 786464 | tf_op jit(solution)/shard_map/ppermute | solution.py:714
  107.6 2.4 collective-permute-done.7
  109.9 1.7 arrange.1
  111.7 3.5 project.3.refs_2_.refs_4_.refs_0_.refs_5_.refs_7_
  117.1 1.4 copy-done.24
  119.9 2.0 collective-permute-start.11
  122.0 2.0 copy-done.5
  124.0 1.6 project.2.refs_0_
  125.6 1.1 copy-done.7
  126.7 38.7 %attend_forward.1 = (bf16[768,1024]{1,0:T(8,128)(2,1)S(1)}, f32[12,1,1024]{2,1,0:T(1,128)S(1)}) custom-call(bf16[768,1024]{1,0:T(8,128)(2,1)} %copy-done.7, bf16[16,1024]{1,0:T(8,128)(2,1)S(1)} %convert_convert_fusion.refs_1_.refs_4_, bf16[1536,1024]{1,0:T(8,128)(2,1)} %copy-done, bf16[1536,1024]{1,0:T(8,128)(2,1)} %collective-permute-done.9.refs_3_.refs_5_.refs_6_.refs_8_, ...), custom_call_target="tpu_custom_call" | custom-call | flops 1610612736 | bytes 589824 | tf_op jit(solution)/shard_map/attend_forward/pallas_call | solution.py:91
  165.4 1.2 copy-done.6
  166.7 1.2 copy-done.8
  167.9 52.4 %middle.1 = (bf16[1024,768]{1,0:T(8,128)(2,1)}, bf16[4,1024,768]{2,1,0:T(8,128)(2,1)}, bf16[4,1024,1536]{2,1,0:T(8,128)(2,1)}, bf16[1024,768]{1,0:T(8,128)(2,1)}...) custom-call(bf16[768,1024]{1,0:T(8,128)(2,1)} %copy-done.6, ...), custom_call_target="tpu_custom_call" | custom-call | flops 1962934272 | bytes 3932160 | tf_op jit(solution)/shard_map/middle/pallas_call | solution.py:346
  221.0 11.4 %side_grads.1 = (bf16[4,4,128,768]{3,2,1,0:T(8,128)(2,1)S(1)}, bf16[4,4,128,768]{3,2,1,0:T(8,128)(2,1)S(1)}) custom-call(s32[1]{0:T(128)} %bitcast.43.core_ref, bf16[1024,768]{1,0:T(8,128)(2,1)} %get-tuple-element.75.mix_ref, bf16[4,1024,768]{2,1,0:T(8,128)(2,1)} %get-tuple-element.76.hid_ref, bf16[1024,768]{1,0:T(8,128)(2,1)} %get-tuple-element.77.proj_ref, ...), custom_call_target="tpu_custom_call" | custom-call | flops 377487360 | bytes 1048576 | tf_op jit(solution)/shard_map/side_grads/pallas_call | solution.py:629
  232.4 7.2 %collective-permute-start.14 = (bf16[4,4,128,768]{3,2,1,0:T(8,128)(2,1)S(1)}, bf16[4,4,128,768]{3,2,1,0:T(8,128)(2,1)S(1)}, u32[]{:S(2)}, u32[]{:S(2)}) collective-permute-start(bf16[4,4,128,768]{3,2,1,0:T(8,128)(2,1)S(1)} %get-tuple-element.80), channel_id=1, source_target_pairs={{0,4},{4,0},{1,5},{5,1},{2,6},{6,2},{3,7},{7,3},{8,12},{12,8},{9,1... | collective-permute-start | bytes 9437192 | tf_op jit(solution)/shard_map/ppermute | solution.py:767
  239.6 9.5 %gate_up_grads.2.refs_0_ = bf16[8,4,96,1536]{3,2,1,0:T(8,128)(2,1)} custom-call(bf16[1024,768]{1,0:T(8,128)(2,1)} %get-tuple-element.81.x_ref, bf16[4,1024,1536]{2,1,0:T(8,128)(2,1)} %get-tuple-element.82.g_ref, bf16[4,4,128,768]{3,2,1,0:T(8,128)(2,1)S(1)} %get-tuple-element.79.refs_0_.mine), custom_call_target="tpu_custom_call" | custom-call | flops 4831838208 | bytes 12582912 | tf_op jit(solution)/shard_map/gate_up_grads/pallas_call | solution.py:668
  249.1 1.3 join.6
  250.4 9.6 %gate_up_grads.3.refs_13_ = bf16[8,4,96,1536]{3,2,1,0:T(8,128)(2,1)} custom-call(bf16[1024,768]{1,0:T(8,128)(2,1)} %get-tuple-element.81.x_ref, bf16[4,1024,1536]{2,1,0:T(8,128)(2,1)} %get-tuple-element.82.g_ref, bf16[8,4,96,1536]{3,2,1,0:T(8,128)(2,1)} %gate_up_grads.2.refs_0_, ...), custom_call_target="tpu_custom_call", output_to_operand_aliasing={{}: (2, {})} | custom-call | flops 4831838208 | bytes 12582912 | tf_op jit(solution)/shard_map/gate_up_grads/pallas_call | solution.py:668
  260.0 1.5 collective-permute-start.16
  261.5 7.4 %collective-permute-start.12 = (bf16[512,768]{1,0:T(8,128)(2,1)}, bf16[512,768]{1,0:T(8,128)(2,1)}, u32[]{:S(2)}, u32[]{:S(2)}) collective-permute-start(bf16[512,768]{1,0:T(8,128)(2,1)} %get-tuple-element.71), channel_id=1, source_target_pairs={{0,0},{1,1},{4,2},{5,3},{2,4},{3,5},{6,6},{7,7},{8,8},{9,9},{12,10... | collective-permute-start | bytes 2359304 | tf_op jit(solution)/shard_map/ppermute | solution.py:717
  269.0 8.1 %collective-permute-start.13 = (bf16[512,768]{1,0:T(8,128)(2,1)}, bf16[512,768]{1,0:T(8,128)(2,1)}, u32[]{:S(2)}, u32[]{:S(2)}) collective-permute-start(bf16[512,768]{1,0:T(8,128)(2,1)} %get-tuple-element.72), channel_id=1, source_target_pairs={{1,0},{0,1},{5,2},{4,3},{3,4},{2,5},{7,6},{6,7},{9,8},{8,9},{13,10... | collective-permute-start | bytes 2359304 | tf_op jit(solution)/shard_map/ppermute | solution.py:717
  277.0 18.0 %attend_backward.4 = (f32[192,1024]{1,0:T(8,128)S(1)}, f32[2,192,1024]{2,1,0:T(8,128)S(1)}, bf16[2,192,1024]{2,1,0:T(8,128)(2,1)S(1)}) custom-call(bf16[768,1024]{1,0:T(8,128)(2,1)} %copy-done.7, bf16[768,1024]{1,0:T(8,128)(2,1)} %get-tuple-element.73.refs_1_, bf16[768,1024]{1,0:T(8,128)(2,1)} %copy-done.6, f32[12,1,1024]{2,1,0:T(1,128)S(1)} %get-tuple-element.74.refs_3_, ...), custom_call_target="tpu_custom_call" | custom-call | flops 754974720 | bytes 294912 | tf_op jit(solution)/shard_map/attend_backward/pallas_call | solution.py:160
  295.1 1.1 copy-done.25
  297.4 1.4 collective-permute-start.18
  298.9 3.6 collective-permute-done.13.refs_14_
  302.5 17.6 %attend_backward.5 = (f32[192,1024]{1,0:T(8,128)S(1)}, f32[2,192,1024]{2,1,0:T(8,128)S(1)}, bf16[2,192,1024]{2,1,0:T(8,128)(2,1)S(1)}) custom-call(bf16[768,1024]{1,0:T(8,128)(2,1)} %copy-done.7, bf16[768,1024]{1,0:T(8,128)(2,1)} %get-tuple-element.73.refs_1_, bf16[768,1024]{1,0:T(8,128)(2,1)} %copy-done.6, f32[12,1,1024]{2,1,0:T(1,128)S(1)} %get-tuple-element.74.refs_3_, ...), custom_call_target="tpu_custom_call" | custom-call | flops 754974720 | bytes 294912 | tf_op jit(solution)/shard_map/attend_backward/pallas_call | solution.py:160
  320.1 6.1 %collective-permute-done.18.got = bf16[4,128,768]{2,1,0:T(8,128)(2,1)S(1)} collective-permute-done((bf16[4,128,768]{2,1,0:T(8,128)(2,1)S(1)}, bf16[4,128,768]{2,1,0:T(8,128)(2,1)S(1)}, u32[]{:S(2)}, u32[]{:S(2)}) %collective-permute-start.18) | collective-permute-done | bytes 786464 | tf_op jit(solution)/shard_map/ppermute | solution.py:731
  327.1 3.7 collective-permute-start.22
  331.3 17.8 %attend_backward.6 = (f32[192,1024]{1,0:T(8,128)S(1)}, f32[2,192,1024]{2,1,0:T(8,128)S(1)}, bf16[2,192,1024]{2,1,0:T(8,128)(2,1)S(1)}) custom-call(bf16[768,1024]{1,0:T(8,128)(2,1)} %copy-done.7, bf16[768,1024]{1,0:T(8,128)(2,1)} %get-tuple-element.73.refs_1_, bf16[768,1024]{1,0:T(8,128)(2,1)} %copy-done.6, f32[12,1,1024]{2,1,0:T(1,128)S(1)} %get-tuple-element.74.refs_3_, ...), custom_call_target="tpu_custom_call" | custom-call | flops 754974720 | bytes 294912 | tf_op jit(solution)/shard_map/attend_backward/pallas_call | solution.py:160
  349.4 17.8 %attend_backward.7 = (f32[192,1024]{1,0:T(8,128)S(1)}, f32[2,192,1024]{2,1,0:T(8,128)S(1)}, bf16[2,192,1024]{2,1,0:T(8,128)(2,1)S(1)}) custom-call(bf16[768,1024]{1,0:T(8,128)(2,1)} %copy-done.7, bf16[768,1024]{1,0:T(8,128)(2,1)} %get-tuple-element.73.refs_1_, bf16[768,1024]{1,0:T(8,128)(2,1)} %copy-done.6, f32[12,1,1024]{2,1,0:T(1,128)S(1)} %get-tuple-element.74.refs_3_, ...), custom_call_target="tpu_custom_call" | custom-call | flops 754974720 | bytes 294912 | tf_op jit(solution)/shard_map/attend_backward/pallas_call | solution.py:160
  367.9 1.6 unturn.4
  369.5 1.9 unturn.5
  371.5 1.0 copy-done.9
  372.5 1.6 unturn.6
  374.1 1.0 copy-done.12
  375.1 1.6 unturn.7
  377.8 1.5 dynamic-slice_bitcast_fusion
  379.4 1.3 copy-done.10
  380.6 4.8 %finish.2.refs_0_ = bf16[512,768]{1,0:T(8,128)(2,1)S(1)} custom-call(bf16[3,192,1024]{2,1,0:T(8,128)(2,1)S(1)} %get-tuple-element.88.refs_0_, bf16[3,192,1024]{2,1,0:T(8,128)(2,1)S(1)} %copy-done.10, bf16[3,192,1024]{2,1,0:T(8,128)(2,1)} %copy-done.12, bf16[3,192,1024]{2,1,0:T(8,128)(2,1)} %copy-done.13, f32[1024,768]{1,0:T(8,128)} %get-tuple-element.107.refs_4_, ...), custom_call_target="tpu_custom_call" | custom-call | flops 113246208 | bytes 786432 | tf_op jit(solution)/shard_map/finish/pallas_call | solution.py:452
  385.5 3.1 join.9
  388.6 0.9 copy-done.14
  390.0 4.0 fusion.4
  394.7 4.9 %finish.3.refs_0_ = bf16[512,768]{1,0:T(8,128)(2,1)S(1)} custom-call(bf16[3,192,1024]{2,1,0:T(8,128)(2,1)S(1)} %get-tuple-element.88.refs_0_, bf16[3,192,1024]{2,1,0:T(8,128)(2,1)S(1)} %copy-done.11, bf16[3,192,1024]{2,1,0:T(8,128)(2,1)} %copy-done.12, bf16[3,192,1024]{2,1,0:T(8,128)(2,1)} %copy-done.13, f32[1024,768]{1,0:T(8,128)} %get-tuple-element.107.refs_4_, ...), custom_call_target="tpu_custom_call" | custom-call | flops 113246208 | bytes 786432 | tf_op jit(solution)/shard_map/finish/pallas_call | solution.py:452
  401.1 1.6 collective-permute-done.27.got
  402.9 1.5 collective-permute-start.28
  405.7 5.6 %collective-permute-done.28.got = bf16[4,72,768]{2,1,0:T(8,128)(2,1)S(1)} collective-permute-done((bf16[4,72,768]{2,1,0:T(8,128)(2,1)S(1)}, bf16[4,72,768]{2,1,0:T(8,128)(2,1)S(1)}, u32[]{:S(2)}, u32[]{:S(2)}) %collective-permute-start.28) | collective-permute-done | bytes 442400 | tf_op jit(solution)/shard_map/ppermute | solution.py:731
  412.6 4.5 collective-permute-start.30
  417.6 5.5 %collective-permute-done.26 = bf16[512,768]{1,0:T(8,128)(2,1)S(1)} collective-permute-done((bf16[512,768]{1,0:T(8,128)(2,1)S(1)}, bf16[512,768]{1,0:T(8,128)(2,1)S(1)}, u32[]{:S(2)}, u32[]{:S(2)}) %collective-permute-start.26) | collective-permute-done | bytes 786464 | tf_op jit(solution)/shard_map/ppermute | solution.py:717
  423.0 2.3 fusion.1
  425.4 11.7 %collective-permute-done.29 = bf16[72,768]{1,0:T(8,128)(2,1)S(1)} collective-permute-done((bf16[72,768]{1,0:T(8,128)(2,1)S(1)}, bf16[72,768]{1,0:T(8,128)(2,1)S(1)}, u32[]{:S(2)}, u32[]{:S(2)}) %collective-permute-start.29) | collective-permute-done | bytes 110624 | tf_op jit(solution)/shard_map/ppermute | solution.py:734
  437.1 11.1 %collective-permute-done.30 = bf16[72,768]{1,0:T(8,128)(2,1)S(1)} collective-permute-done((bf16[72,768]{1,0:T(8,128)(2,1)S(1)}, bf16[72,768]{1,0:T(8,128)(2,1)S(1)}, u32[]{:S(2)}, u32[]{:S(2)}) %collective-permute-start.30) | collective-permute-done | bytes 110624 | tf_op jit(solution)/shard_map/ppermute | solution.py:734
  448.9 1.0 bitcast_convert_fusion
  449.9 0.9 fusion.23
  (173 shorter events, 23.5 us)
Async XLA Ops:
  7.2 5.6 %copy-start.27 = (bf16[2,512,768]{2,1,0:T(8,128)(2,1)S(1)}, bf16[2,512,768]{2,1,0:T(8,128)(2,1)}, u32[]{:S(2)}) copy-start(bf16[2,512,768]{2,1,0:T(8,128)(2,1)} %x_ref.2) | copy-start | bytes 4718596
  7.2 160.7 %all-gather.3.cloned.1.call-start = ((), (), s32[]{:S(2)}) async-start(), calls=%async_computation.4 | async-start | bytes 16220160 | tf_op jit(solution)/shard_map/all_gather | solution.py:760
  11.8 2.4 copy-start.31
  12.6 366.7 %reduce-scatter.3.cloned.1.call-start = ((), (), s32[]{:S(2)}) async-start(), calls=%async_computation.2 | async-start | bytes 10616832 | tf_op jit(solution)/shard_map/reduce_scatter | solution.py:883
  13.4 43.2 %collective-permute-start.3 = (bf16[512,768]{1,0:T(8,128)(2,1)S(1)}, bf16[512,768]{1,0:T(8,128)(2,1)S(1)}, u32[]{:S(2)}, u32[]{:S(2)}) collective-permute-start(bf16[512,768]{1,0:T(8,128)(2,1)S(1)} %get-tuple-element.66), channel_id=1, source_target_pairs={{0,0},{1,1},{2,4},{3,5},{4,2},{5,3},{6,6},{7,7},{8,8},{9,9},{10,12... | collective-permute-start | bytes 2359304 | tf_op jit(solution)/shard_map/ppermute | solution.py:714
  14.1 42.4 %collective-permute-start.1 = (bf16[72,768]{1,0:T(8,128)(2,1)S(1)}, bf16[72,768]{1,0:T(8,128)(2,1)S(1)}, u32[]{:S(2)}, u32[]{:S(2)}) collective-permute-start(bf16[72,768]{1,0:T(8,128)(2,1)S(1)} %bitcast.91), channel_id=1, source_target_pairs={{0,2},{1,3},{2,0},{3,1},{4,6},{5,7},{6,4},{7,5},{8,10},{9,11},{10,... | collective-permute-start | bytes 331784 | tf_op jit(solution)/shard_map/ppermute | solution.py:734
  19.4 37.1 %collective-permute-start = (bf16[72,768]{1,0:T(8,128)(2,1)S(1)}, bf16[72,768]{1,0:T(8,128)(2,1)S(1)}, u32[]{:S(2)}, u32[]{:S(2)}) collective-permute-start(bf16[72,768]{1,0:T(8,128)(2,1)S(1)} %bitcast.92), channel_id=1, source_target_pairs={{0,1},{1,2},{2,3},{3,0},{4,5},{5,6},{6,7},{7,4},{8,9},{9,10},{10,1... | collective-permute-start | bytes 331784 | tf_op jit(solution)/shard_map/ppermute | solution.py:734
  21.0 35.5 %collective-permute-start.2 = (bf16[72,768]{1,0:T(8,128)(2,1)S(1)}, bf16[72,768]{1,0:T(8,128)(2,1)S(1)}, u32[]{:S(2)}, u32[]{:S(2)}) collective-permute-start(bf16[72,768]{1,0:T(8,128)(2,1)S(1)} %bitcast.93), channel_id=1, source_target_pairs={{0,3},{1,0},{2,1},{3,2},{4,7},{5,4},{6,5},{7,6},{8,11},{9,8},{10,9... | collective-permute-start | bytes 331784 | tf_op jit(solution)/shard_map/ppermute | solution.py:734
  56.6 18.1 %collective-permute-start.4 = (bf16[4,72,768]{2,1,0:T(8,128)(2,1)S(1)}, bf16[4,72,768]{2,1,0:T(8,128)(2,1)S(1)}, u32[]{:S(2)}, u32[]{:S(2)}) collective-permute-start(bf16[4,72,768]{2,1,0:T(8,128)(2,1)S(1)} %stack.203.refs_0_), channel_id=1, source_target_pairs={{0,8},{4,20},{8,0},{12,28},{16,24},{20,4},{24,16},{28,12},{1,9},{5... | collective-permute-start | bytes 1327112 | tf_op jit(solution)/shard_map/ppermute | solution.py:731
  74.8 28.9 %collective-permute-start.5 = (bf16[8,72,768]{2,1,0:T(8,128)(2,1)S(1)}, bf16[8,72,768]{2,1,0:T(8,128)(2,1)S(1)}, u32[]{:S(2)}, u32[]{:S(2)}) collective-permute-start(bf16[8,72,768]{2,1,0:T(8,128)(2,1)S(1)} %stack.204.refs_0_), channel_id=1, source_target_pairs={{0,16},{4,12},{8,24},{12,4},{16,0},{20,28},{24,8},{28,20},{1,17},{... | collective-permute-start | bytes 2654216 | tf_op jit(solution)/shard_map/ppermute | solution.py:731
  76.4 28.2 %copy-start.39 = (s32[2,2048]{1,0:T(2,128)S(1)}, s32[2,2048]{1,0:T(2,128)}, u32[]{:S(2)}) copy-start(s32[2,2048]{1,0:T(2,128)} %param.17) | copy-start | bytes 49156
  76.4 28.2 %copy-start.40 = (s32[2,2048]{1,0:T(2,128)S(1)}, s32[2,2048]{1,0:T(2,128)}, u32[]{:S(2)}) copy-start(s32[2,2048]{1,0:T(2,128)} %param.16) | copy-start | bytes 49156
  76.4 27.3 %collective-permute-start.6 = (bf16[512,768]{1,0:T(8,128)(2,1)S(1)}, bf16[512,768]{1,0:T(8,128)(2,1)S(1)}, u32[]{:S(2)}, u32[]{:S(2)}) collective-permute-start(bf16[512,768]{1,0:T(8,128)(2,1)S(1)} %get-tuple-element.67), channel_id=1, source_target_pairs={{0,1},{1,0},{2,5},{3,4},{4,3},{5,2},{6,7},{7,6},{8,9},{9,8},{10,13... | collective-permute-start | bytes 2359304 | tf_op jit(solution)/shard_map/ppermute | solution.py:714
  104.5 5.4 %collective-permute-start.7 = (bf16[16,72,768]{2,1,0:T(8,128)(2,1)S(1)}, bf16[16,72,768]{2,1,0:T(8,128)(2,1)}, u32[]{:S(2)}, u32[]{:S(2)}) collective-permute-start(bf16[16,72,768]{2,1,0:T(8,128)(2,1)S(1)} %stack.205), channel_id=1, source_target_pairs={{0,4},{4,0},{1,5},{5,1},{2,6},{6,2},{3,7},{7,3},{8,12},{12,8},{9,1... | collective-permute-start | bytes 5308424 | tf_op jit(solution)/shard_map/ppermute | solution.py:752
  104.6 1.5 collective-permute-start.8
  107.6 4.1 copy-start.1
  111.7 3.5 copy-start.4
  115.2 1.9 copy-start
  115.2 11.6 %collective-permute-start.9 = (bf16[1536,1024]{1,0:T(8,128)(2,1)S(1)}, bf16[1536,1024]{1,0:T(8,128)(2,1)}, u32[]{:S(2)}, u32[]{:S(2)}) collective-permute-start(bf16[1536,1024]{1,0:T(8,128)(2,1)S(1)} %project.3.refs_2_.refs_4_.refs_0_.refs_5_.refs_7_), channel_id=1, source_target_pairs={{0,4},{4,0},{1,5},{5,1},{2,6},{6,2},{3,7},{7,3},{8,12},{12,8},{9,1... | collective-permute-start | bytes 9437192 | tf_op jit(solution)/shard_map/ppermute | solution.py:842
  117.1 1.4 copy-start.24
  118.5 3.5 copy-start.2
  119.2 47.4 %collective-permute-start.10 = (bf16[512,768]{1,0:T(8,128)(2,1)S(1)}, bf16[512,768]{1,0:T(8,128)(2,1)S(1)}, u32[]{:S(2)}, u32[]{:S(2)}) collective-permute-start(bf16[512,768]{1,0:T(8,128)(2,1)S(1)} %get-tuple-element.69), channel_id=1, source_target_pairs={{0,0},{1,1},{2,4},{3,5},{4,2},{5,3},{6,6},{7,7},{8,8},{9,9},{10,12... | collective-permute-start | bytes 2359304 | tf_op jit(solution)/shard_map/ppermute | solution.py:714
  119.9 46.7 %collective-permute-start.11 = (bf16[512,768]{1,0:T(8,128)(2,1)S(1)}, bf16[512,768]{1,0:T(8,128)(2,1)S(1)}, u32[]{:S(2)}, u32[]{:S(2)}) collective-permute-start(bf16[512,768]{1,0:T(8,128)(2,1)S(1)} %get-tuple-element.70), channel_id=1, source_target_pairs={{0,1},{1,0},{2,5},{3,4},{4,3},{5,2},{6,7},{7,6},{8,9},{9,8},{10,13... | collective-permute-start | bytes 2359304 | tf_op jit(solution)/shard_map/ppermute | solution.py:714
  122.0 2.0 copy-start.5
  165.4 1.2 copy-start.6
  166.7 1.2 copy-start.8
  232.4 16.8 %collective-permute-start.14 = (bf16[4,4,128,768]{3,2,1,0:T(8,128)(2,1)S(1)}, bf16[4,4,128,768]{3,2,1,0:T(8,128)(2,1)S(1)}, u32[]{:S(2)}, u32[]{:S(2)}) collective-permute-start(bf16[4,4,128,768]{3,2,1,0:T(8,128)(2,1)S(1)} %get-tuple-element.80), channel_id=1, source_target_pairs={{0,4},{4,0},{1,5},{5,1},{2,6},{6,2},{3,7},{7,3},{8,12},{12,8},{9,1... | collective-permute-start | bytes 9437192 | tf_op jit(solution)/shard_map/ppermute | solution.py:767
  239.6 9.5 %copy-start.33 = (s32[4]{0:T(128)}, s32[4]{0:T(128)S(1)}, u32[]{:S(2)}) copy-start(s32[4]{0:T(128)S(1)} %pad_add_fusion.3.place) | copy-start | bytes 52
  260.0 188.9 %reduce-scatter.5.cloned.1.call-start = ((), (), s32[]{:S(2)}) async-start(), calls=%async_computation.3 | async-start | bytes 1474560 | tf_op jit(solution)/shard_map/reduce_scatter | solution.py:884
  260.0 36.2 %collective-permute-start.16 = (bf16[2,4,128,768]{3,2,1,0:T(8,128)(2,1)S(1)}, bf16[2,4,128,768]{3,2,1,0:T(8,128)(2,1)S(1)}, u32[]{:S(2)}, u32[]{:S(2)}) collective-permute-start(bf16[2,4,128,768]{3,2,1,0:T(8,128)(2,1)S(1)} %get-tuple-element.84.refs_2_.refs_12_), channel_id=1, source_target_pairs={{0,16},{4,12},{8,24},{12,4},{16,0},{20,28},{24,8},{28,20},{1,17},{... | collective-permute-start | bytes 4718600 | tf_op jit(solution)/shard_map/ppermute | solution.py:731
  261.5 37.4 %collective-permute-start.12 = (bf16[512,768]{1,0:T(8,128)(2,1)}, bf16[512,768]{1,0:T(8,128)(2,1)}, u32[]{:S(2)}, u32[]{:S(2)}) collective-permute-start(bf16[512,768]{1,0:T(8,128)(2,1)} %get-tuple-element.71), channel_id=1, source_target_pairs={{0,0},{1,1},{4,2},{5,3},{2,4},{3,5},{6,6},{7,7},{8,8},{9,9},{12,10... | collective-permute-start | bytes 2359304 | tf_op jit(solution)/shard_map/ppermute | solution.py:717
  269.0 33.5 %collective-permute-start.13 = (bf16[512,768]{1,0:T(8,128)(2,1)}, bf16[512,768]{1,0:T(8,128)(2,1)}, u32[]{:S(2)}, u32[]{:S(2)}) collective-permute-start(bf16[512,768]{1,0:T(8,128)(2,1)} %get-tuple-element.72), channel_id=1, source_target_pairs={{1,0},{0,1},{5,2},{4,3},{3,4},{2,5},{7,6},{6,7},{9,8},{8,9},{13,10... | collective-permute-start | bytes 2359304 | tf_op jit(solution)/shard_map/ppermute | solution.py:717
  296.2 1.2 copy-start.37
  297.4 28.8 %collective-permute-start.18 = (bf16[4,128,768]{2,1,0:T(8,128)(2,1)S(1)}, bf16[4,128,768]{2,1,0:T(8,128)(2,1)S(1)}, u32[]{:S(2)}, u32[]{:S(2)}) collective-permute-start(bf16[4,128,768]{2,1,0:T(8,128)(2,1)S(1)} %get-tuple-element.90.refs_12_), channel_id=1, source_target_pairs={{0,8},{4,20},{8,0},{12,28},{16,24},{20,4},{24,16},{28,12},{1,9},{5... | collective-permute-start | bytes 2359304 | tf_op jit(solution)/shard_map/ppermute | solution.py:731
  298.9 27.3 %copy-start.35 = (s32[4]{0:T(128)}, s32[4]{0:T(128)S(1)}, u32[]{:S(2)}) copy-start(s32[4]{0:T(128)S(1)} %pad_add_fusion.4.place) | copy-start | bytes 52
  320.1 10.8 %copy-start.38 = (bf16[2,192,1024]{2,1,0:T(8,128)(2,1)S(1)}, bf16[2,192,1024]{2,1,0:T(8,128)(2,1)}, u32[]{:S(2)}) copy-start(bf16[2,192,1024]{2,1,0:T(8,128)(2,1)} %copy-done.37) | copy-start | bytes 2359300
  327.0 22.2 %collective-permute-start.20 = (bf16[128,768]{1,0:T(8,128)(2,1)S(1)}, bf16[128,768]{1,0:T(8,128)(2,1)S(1)}, u32[]{:S(2)}, u32[]{:S(2)}) collective-permute-start(bf16[128,768]{1,0:T(8,128)(2,1)S(1)} %get-tuple-element.96.refs_12_), channel_id=1, source_target_pairs={{0,1},{1,2},{2,3},{3,0},{4,5},{5,6},{6,7},{7,4},{8,9},{9,10},{10,1... | collective-permute-start | bytes 589832 | tf_op jit(solution)/shard_map/ppermute | solution.py:734
  327.0 22.2 %collective-permute-start.21 = (bf16[128,768]{1,0:T(8,128)(2,1)S(1)}, bf16[128,768]{1,0:T(8,128)(2,1)S(1)}, u32[]{:S(2)}, u32[]{:S(2)}) collective-permute-start(bf16[128,768]{1,0:T(8,128)(2,1)S(1)} %get-tuple-element.97.refs_13_), channel_id=1, source_target_pairs={{0,2},{1,3},{2,0},{3,1},{4,6},{5,7},{6,4},{7,5},{8,10},{9,11},{10,... | collective-permute-start | bytes 589832 | tf_op jit(solution)/shard_map/ppermute | solution.py:734
  327.1 22.2 %collective-permute-start.22 = (bf16[128,768]{1,0:T(8,128)(2,1)S(1)}, bf16[128,768]{1,0:T(8,128)(2,1)S(1)}, u32[]{:S(2)}, u32[]{:S(2)}) collective-permute-start(bf16[128,768]{1,0:T(8,128)(2,1)S(1)} %get-tuple-element.98.refs_14_), channel_id=1, source_target_pairs={{0,3},{1,0},{2,1},{3,2},{4,7},{5,4},{6,5},{7,6},{8,11},{9,8},{10,9... | collective-permute-start | bytes 589832 | tf_op jit(solution)/shard_map/ppermute | solution.py:734
  330.8 37.0 %collective-permute-start.15 = (bf16[2,192,1024]{2,1,0:T(8,128)(2,1)S(1)}, bf16[2,192,1024]{2,1,0:T(8,128)(2,1)S(1)}, u32[]{:S(2)}, u32[]{:S(2)}) collective-permute-start(bf16[2,192,1024]{2,1,0:T(8,128)(2,1)S(1)} %copy-done.38), channel_id=1, source_target_pairs={{0,4},{4,0},{1,5},{5,1},{2,6},{6,2},{3,7},{7,3},{8,12},{12,8},{9,1... | collective-permute-start | bytes 2359304 | tf_op jit(solution)/shard_map/ppermute | solution.py:899
  330.8 38.7 %collective-permute-start.17 = (bf16[2,192,1024]{2,1,0:T(8,128)(2,1)S(1)}, bf16[2,192,1024]{2,1,0:T(8,128)(2,1)S(1)}, u32[]{:S(2)}, u32[]{:S(2)}) collective-permute-start(bf16[2,192,1024]{2,1,0:T(8,128)(2,1)S(1)} %get-tuple-element.93), channel_id=1, source_target_pairs={{0,4},{4,0},{1,5},{5,1},{2,6},{6,2},{3,7},{7,3},{8,12},{12,8},{9,1... | collective-permute-start | bytes 2359304 | tf_op jit(solution)/shard_map/ppermute | solution.py:899
  349.2 23.3 %collective-permute-start.19 = (bf16[2,192,1024]{2,1,0:T(8,128)(2,1)S(1)}, bf16[2,192,1024]{2,1,0:T(8,128)(2,1)S(1)}, u32[]{:S(2)}, u32[]{:S(2)}) collective-permute-start(bf16[2,192,1024]{2,1,0:T(8,128)(2,1)S(1)} %get-tuple-element.101), channel_id=1, source_target_pairs={{0,4},{4,0},{1,5},{5,1},{2,6},{6,2},{3,7},{7,3},{8,12},{12,8},{9,1... | collective-permute-start | bytes 2359304 | tf_op jit(solution)/shard_map/ppermute | solution.py:899
  349.4 17.9 %copy-start.16 = (f32[128,768]{1,0:T(8,128)}, f32[128,768]{1,0:T(8,128)S(1)}, u32[]{:S(2)}) copy-start(f32[128,768]{1,0:T(8,128)S(1)} %convert_add_fusion.refs_11_) | copy-start | bytes 1179652
  349.4 18.5 %copy-start.3 = (bf16[1024,768]{1,0:T(8,128)(2,1)S(1)}, bf16[1024,768]{1,0:T(8,128)(2,1)}, u32[]{:S(2)}) copy-start(bf16[1024,768]{1,0:T(8,128)(2,1)} %copy-done.1) | copy-start | bytes 4718596
  349.4 18.5 %copy-start.19 = (f32[192,1024]{1,0:T(8,128)S(1)}, f32[192,1024]{1,0:T(8,128)}, u32[]{:S(2)}) copy-start(f32[192,1024]{1,0:T(8,128)} %copy-done.18) | copy-start | bytes 2359300
  349.4 18.5 %copy-start.26 = (f32[2,192,1024]{2,1,0:T(8,128)S(1)}, f32[2,192,1024]{2,1,0:T(8,128)}, u32[]{:S(2)}) copy-start(f32[2,192,1024]{2,1,0:T(8,128)} %copy-done.25) | copy-start | bytes 4718596
  367.3 7.9 %collective-permute-start.23 = (bf16[2,192,1024]{2,1,0:T(8,128)(2,1)S(1)}, bf16[2,192,1024]{2,1,0:T(8,128)(2,1)S(1)}, u32[]{:S(2)}, u32[]{:S(2)}) collective-permute-start(bf16[2,192,1024]{2,1,0:T(8,128)(2,1)S(1)} %get-tuple-element.105), channel_id=1, source_target_pairs={{0,4},{4,0},{1,5},{5,1},{2,6},{6,2},{3,7},{7,3},{8,12},{12,8},{9,1... | collective-permute-start | bytes 2359304 | tf_op jit(solution)/shard_map/ppermute | solution.py:899
  379.3 6.2 %collective-permute-start.25 = (bf16[4,4,72,768]{3,2,1,0:T(8,128)(2,1)}, bf16[4,4,72,768]{3,2,1,0:T(8,128)(2,1)}, u32[]{:S(2)}, u32[]{:S(2)}) collective-permute-start(bf16[4,4,72,768]{3,2,1,0:T(8,128)(2,1)} %get-tuple-element.123.refs_6_), channel_id=1, source_target_pairs={{0,4},{4,0},{1,5},{5,1},{2,6},{6,2},{3,7},{7,3},{8,12},{12,8},{9,1... | collective-permute-start | bytes 5308424 | tf_op jit(solution)/shard_map/ppermute | solution.py:767
  379.4 1.3 copy-start.10
  380.6 4.9 %copy-start.34 = (s32[4]{0:T(128)S(1)}, s32[4]{0:T(128)}, u32[]{:S(2)}) copy-start(s32[4]{0:T(128)} %copy-done.33) | copy-start | bytes 52
  385.5 3.1 copy-start.22
  389.5 13.3 %collective-permute-start.27 = (bf16[2,4,72,768]{3,2,1,0:T(8,128)(2,1)}, bf16[2,4,72,768]{3,2,1,0:T(8,128)(2,1)S(1)}, u32[]{:S(2)}, u32[]{:S(2)}) collective-permute-start(bf16[2,4,72,768]{3,2,1,0:T(8,128)(2,1)} %get-tuple-element.113), channel_id=1, source_target_pairs={{0,16},{4,12},{8,24},{12,4},{16,0},{20,28},{24,8},{28,20},{1,17},{... | collective-permute-start | bytes 2654216 | tf_op jit(solution)/shard_map/ppermute | solution.py:731
  389.9 4.1 copy-start.23
  389.9 4.8 %copy-start.11 = (bf16[3,192,1024]{2,1,0:T(8,128)(2,1)S(1)}, bf16[3,192,1024]{2,1,0:T(8,128)(2,1)}, u32[]{:S(2)}) copy-start(bf16[3,192,1024]{2,1,0:T(8,128)(2,1)} %copy-done.9) | copy-start | bytes 3538948
  389.9 4.8 %copy-start.15 = (bf16[2,4,72,768]{3,2,1,0:T(8,128)(2,1)S(1)}, bf16[2,4,72,768]{3,2,1,0:T(8,128)(2,1)}, u32[]{:S(2)}) copy-start(bf16[2,4,72,768]{3,2,1,0:T(8,128)(2,1)} %copy-done.14) | copy-start | bytes 2654212
  394.0 23.6 %collective-permute-start.24 = (bf16[512,768]{1,0:T(8,128)(2,1)S(1)}, bf16[512,768]{1,0:T(8,128)(2,1)S(1)}, u32[]{:S(2)}, u32[]{:S(2)}) collective-permute-start(bf16[512,768]{1,0:T(8,128)(2,1)S(1)} %copy-done.23), channel_id=1, source_target_pairs={{0,0},{1,1},{4,2},{5,3},{2,4},{3,5},{6,6},{7,7},{8,8},{9,9},{12,10... | collective-permute-start | bytes 2359304 | tf_op jit(solution)/shard_map/ppermute | solution.py:717
  394.7 5.7 %slice-start = ((f32[128,768]{1,0:T(8,128)}), f32[4,768]{1,0:T(4,128)S(1)}, s32[]{:S(2)}) async-start(f32[128,768]{1,0:T(8,128)} %copy-done.16), calls=%async_computation.5 | async-start | bytes 24576 | tf_op jit(solution)/shard_map/slice | solution.py:925
  394.7 5.8 %copy-start.17 = (f32[128,768]{1,0:T(8,128)S(1)}, f32[128,768]{1,0:T(8,128)}, u32[]{:S(2)}) copy-start(f32[128,768]{1,0:T(8,128)} %copy-done.16) | copy-start | bytes 1179652
  399.7 23.4 %collective-permute-start.26 = (bf16[512,768]{1,0:T(8,128)(2,1)S(1)}, bf16[512,768]{1,0:T(8,128)(2,1)S(1)}, u32[]{:S(2)}, u32[]{:S(2)}) collective-permute-start(bf16[512,768]{1,0:T(8,128)(2,1)S(1)} %finish.3.refs_0_), channel_id=1, source_target_pairs={{1,0},{0,1},{5,2},{4,3},{3,4},{2,5},{7,6},{6,7},{9,8},{8,9},{13,10... | collective-permute-start | bytes 2359304 | tf_op jit(solution)/shard_map/ppermute | solution.py:717
  401.1 10.2 %copy-start.36 = (s32[4]{0:T(128)S(1)}, s32[4]{0:T(128)}, u32[]{:S(2)}) copy-start(s32[4]{0:T(128)} %copy-done.35) | copy-start | bytes 52
  402.9 8.4 %collective-permute-start.28 = (bf16[4,72,768]{2,1,0:T(8,128)(2,1)S(1)}, bf16[4,72,768]{2,1,0:T(8,128)(2,1)S(1)}, u32[]{:S(2)}, u32[]{:S(2)}) collective-permute-start(bf16[4,72,768]{2,1,0:T(8,128)(2,1)S(1)} %get-tuple-element.115), channel_id=1, source_target_pairs={{0,8},{4,20},{8,0},{12,28},{16,24},{20,4},{24,16},{28,12},{1,9},{5... | collective-permute-start | bytes 1327112 | tf_op jit(solution)/shard_map/ppermute | solution.py:731
  412.0 25.1 %collective-permute-start.29 = (bf16[72,768]{1,0:T(8,128)(2,1)S(1)}, bf16[72,768]{1,0:T(8,128)(2,1)S(1)}, u32[]{:S(2)}, u32[]{:S(2)}) collective-permute-start(bf16[72,768]{1,0:T(8,128)(2,1)S(1)} %get-tuple-element.117), channel_id=1, source_target_pairs={{0,1},{1,2},{2,3},{3,0},{4,5},{5,6},{6,7},{7,4},{8,9},{9,10},{10,1... | collective-permute-start | bytes 331784 | tf_op jit(solution)/shard_map/ppermute | solution.py:734
  412.6 35.5 %collective-permute-start.30 = (bf16[72,768]{1,0:T(8,128)(2,1)S(1)}, bf16[72,768]{1,0:T(8,128)(2,1)S(1)}, u32[]{:S(2)}, u32[]{:S(2)}) collective-permute-start(bf16[72,768]{1,0:T(8,128)(2,1)S(1)} %get-tuple-element.118), channel_id=1, source_target_pairs={{0,2},{1,3},{2,0},{3,1},{4,6},{5,7},{6,4},{7,5},{8,10},{9,11},{10,... | collective-permute-start | bytes 331784 | tf_op jit(solution)/shard_map/ppermute | solution.py:734
  417.1 31.0 %collective-permute-start.31 = (bf16[72,768]{1,0:T(8,128)(2,1)S(1)}, bf16[72,768]{1,0:T(8,128)(2,1)S(1)}, u32[]{:S(2)}, u32[]{:S(2)}) collective-permute-start(bf16[72,768]{1,0:T(8,128)(2,1)S(1)} %get-tuple-element.119), channel_id=1, source_target_pairs={{0,3},{1,0},{2,1},{3,2},{4,7},{5,4},{6,5},{7,6},{8,11},{9,8},{10,9... | collective-permute-start | bytes 331784 | tf_op jit(solution)/shard_map/ppermute | solution.py:734
  (13 other events, 12.7 us)
Sparse Core Ops, SparseCore 0:
  12.7 151.5 all-gather.2
  260.1 90.7 reduce-scatter.2
  379.5 31.8 reduce-scatter.4

commit v4 on v3

--- a/solution.py
+++ b/solution.py
@@ -257,7 +257,7 @@
             total = jnp.zeros((8, width), WIDE)
             for j in range(blocks):
                 for i in range(pack.shape[1]):
-                    rows = pack[j, i, 3 * lines :].astype(WIDE)
+                    rows = refs[4][j, i].astype(WIDE)
                     spot = (i * blocks + j) * few
                     wide[spot : spot + few] = rows[:few]
                     total += rows[few : few + 8]
@@ -334,7 +334,7 @@
     blocks, units = pack.shape[0], width
     step = min(n // parts, 256)
     steps = n // step // parts
-    few = 0 if small else width // (blocks * pack.shape[1])
+    few = 0 if len(small) == 2 else width // (blocks * pack.shape[1])
 
     def kept_block(shape):
         return pl.BlockSpec(shape, lambda i: (0,) * len(shape), pipeline_mode=pl.Buffered(1))
@@ -504,6 +504,31 @@
     )(at, x, *after)
 
 
+def settle_kernel(count, at, *refs):
+    out = refs[-1]
+    for r in range(count):
+        for k in range(count):
+
+            @pl.when(at[r] == k)
+            def _():
+                out[r] = refs[k][...]
+
+
+def settle_late(back, at, after):
+    whole = pl.BlockSpec(memory_space=pltpu.VMEM)
+    return pl.pallas_call(
+        functools.partial(settle_kernel, len(back)),
+        in_specs=[pl.BlockSpec(memory_space=pltpu.SMEM)]
+        + [whole] * len(back)
+        + [pl.BlockSpec(memory_space=pl.ANY)] * len(after),
+        out_specs=whole,
+        out_shape=jax.ShapeDtypeStruct((len(back),) + back[0].shape, back[0].dtype),
+        compiler_params=pltpu.CompilerParams(vmem_limit_bytes=10 << 20),
+        cost_estimate=cost(bytes_accessed=4 * len(back) * back[0].size),
+        name="settle",
+    )(at, *back, *after)
+
+
 def stack_kernel(count, *refs):
     out = refs[-1]
     at = 0
@@ -713,14 +738,14 @@
         at = jnp.stack([(z + k) % rows for k in range(rows)]).astype(jnp.int32)
         return [lax.ppermute(a, line, ring(k)) for k, a in enumerate(select(x, at, after))]
 
-    def send_back(parts):
-        return [lax.ppermute(part, line, [(b, a) for a, b in ring(k)]) for k, part in enumerate(parts)]
+    def send_back(parts, first):
+        return [lax.ppermute(part, line, [(b, a) for a, b in ring(first + k)]) for k, part in enumerate(parts)]
 
     def settle(back):
         return jnp.roll(jnp.stack(back), z, axis=0)
 
     def give_back(parts):
-        return settle(send_back(parts))
+        return settle(send_back(parts, 0))
 
     def hop(x, first):
         pairs = []
@@ -797,12 +822,15 @@
         small = jnp.concatenate([w_out.T, placed, jnp.zeros((4, width), LOW)])
     brought = bring(tokens)
     x = jnp.concatenate(brought)
-    column = spread_z(w_qkv.T, tuple(brought[:1]))
-    qkv_t = spread_core(spread_far(spread_near(column), tuple(brought[1:])), [(0, nq, False)])[0]
+    first = jnp.concatenate([small, w_qkv.T]) if merged else w_qkv.T
+    extra = first.shape[0] - nq
+    column = spread_z(first, tuple(brought[:1]))
+    cuts = [(extra, nq, False)] + ([(0, extra, True)] if merged else [])
+    qkv_t, *small = spread_core(spread_far(spread_near(column), tuple(brought[1:])), cuts)
     qkv_t = qkv_t.reshape(3 * width, width)
     if merged:
-        pack = gather_all(stack([w_gate, w_up, w_down.T, small]))
-        small = ()
+        pack = gather_all(stack([w_gate, w_up, w_down.T], (brought[0],)))
+        small = tuple(far(*small))
     else:
         regroup = lambda a: a.reshape(blocks, tp // blocks, width, units).swapaxes(1, 2).reshape(blocks, dp, -1, width)
         pack = jnp.concatenate([regroup(gather_all(a)) for a in (w_gate, w_up, w_down.T)], axis=2)
@@ -856,8 +884,7 @@
     (x_low, hidden, gug, mix_grad, d_resid_one, proj_grad, att_grad, sums), output = middle(
         attended, x, grad_top, pack, small, rows
     )
-    returned = send_back(output)
-    output = settle(returned)
+    returned = send_back(output[:1], 0)
 
     def ungroup(g):
         g = g.reshape(blocks, width, tp // blocks, units).swapaxes(1, 2)
@@ -886,8 +913,10 @@
 
     dqs, grads, parts = [], [], []
     for i, (start, count) in enumerate(spans):
-        after = tuple(held) + (tuple(far(g_gu)) if i == 0 else ()) + (tuple(far(*returned)) if i == 1 else ())
+        after = tuple(held) + (tuple(far(g_gu)) if i == 0 else ()) + (tuple(far(*returned[i - 1 : i])) if i in (1, 2) else ())
         dq, dkv = attend_backward(q, att_grad, attended, lse, query_aug, kvs, kas, types, after, start, count)
+        if i == 0:
+            returned += send_back([stack([part], (dq,)) for part in output[1:]], 1)
         if merged and i == 0:
             held = collapse_far(*held, (dq,))
         if merged and i == 1:
@@ -911,7 +940,8 @@
     if not by_hand:
         g_qkv = collapse_all(g_qkv.swapaxes(0, 1))
         in_grad = finish(grads, d_resid_one, qkv_t, (), 0, own)
-        in_grad = give_back([in_grad[k * piece : (k + 1) * piece] for k in range(rows)])
+        sent = [in_grad[k * piece : (k + 1) * piece] for k in range(rows)]
+        in_grad = give_back(sent)
     else:
         g_qkv = g_qkv.reshape(chips, 2, tp, nq, width)
         mine, send = pick(g_qkv, core, 1), pick(g_qkv, 1 - core, 1)
@@ -921,10 +951,12 @@
             in_grad.append(finish(grads, d_resid_one, qkv_t, (held[0],), k, piece))
         held = collapse_far(*held, (in_grad[-1],))
         g_qkv = collapse_z(collapse_near(*held))
+        sent = in_grad
         in_grad = give_back(in_grad)
     vector_grads = lax.dynamic_slice_in_dim(side[no : no + 4], mine_at, no, 1)
+    order = jnp.stack([(r - z) % rows for r in range(rows)]).astype(jnp.int32)
     return (
-        output,
+        settle_late(returned, order, tuple(far(sent[-1]))),
         in_grad,
         g_qkv.T,
         side[:no].T,

time: 464 us -> 464 us (level)
  waiting for transfers between devices: 124 us -> 89.7 us
  starting transfers between devices: 58.1 us -> 87.1 us
  Pallas kernels: 225 us -> 231 us
  other arithmetic: 12 us -> 6.28 us
  local copies, waits for them, and re-layouts: 24.1 us -> 28.9 us
    ppermute x9, waiting for transfers between devices: 56.1 us -> 29.6 us  [along(): return lax.ppermute(x, flat, [(i, (i + k) % tp) for i in range(tp)])]
    ppermute x9, starting transfers between devices: 18.6 us -> 42.7 us  [along(): return lax.ppermute(x, flat, [(i, (i + k) % tp) for i in range(tp)])]
    ppermute x6, waiting for transfers between devices: 29.9 us -> 14.9 us  [hop(): return lax.ppermute(x, ('chip', 'core'), pairs)]
    ppermute x4, waiting for transfers between devices: 25.5 us -> 31.8 us  [bring(): lax.ppermute(a, line, ring(k))]
    unnamed x85 -> x107, local copies, waits for them, and re-layouts: 18.5 us -> 23 us
  transfers between devices with their start and end apart: 35 -> 35, of which waited for: 12 -> 12; matrix products, arithmetic and copies ran while one was open for 3% -> 2% of each run, Pallas kernels for 33% -> 34%
where the time goes in v4:
time: 464 us; the launch traced here: 458 us
  Pallas kernels  231 us (50%)
  waiting for transfers between devices  89.7 us (19%)
  starting transfers between devices  87.1 us (19%)
  local copies, waits for them, and re-layouts  28.9 us (6%)
  between operations  15.1 us (3%)
  other arithmetic  6.28 us (1%)
    pallas_call x4, Pallas kernels, attend_backward(): pl.pallas_call(functools.partial(backward_kernel, parts), grid=(heads,),...  71 us
    pallas_call x1, Pallas kernels, middle(): pl.pallas_call(functools.partial(middle_kernel, parts, few), grid=(n // s...  52.2 us
    ppermute x9, starting transfers between devices, along(): return lax.ppermute(x, flat, [(i, (i + k) % tp) for i in range(tp)])  42.7 us
    pallas_call x1, Pallas kernels, attend_forward(): pl.pallas_call(functools.partial(forward_kernel, parts), grid=(heads,), i...  38.9 us
    ppermute x4, waiting for transfers between devices, bring(): lax.ppermute(a, line, ring(k))  31.8 us
    ppermute x9, waiting for transfers between devices, along(): return lax.ppermute(x, flat, [(i, (i + k) % tp) for i in range(tp)])  29.6 us
    unnamed x107, local copies, waits for them, and re-layouts  23 us
    pallas_call x2, Pallas kernels, gate_up_grads(): pl.pallas_call(gate_up_kernel, grid=(count,), in_specs=[pl.BlockSpec((n,...  18.9 us
  transfers between devices with their start and end apart: 35, of which 12 were waited for; matrix products, arithmetic and copies ran while one was open for 2% of the time, Pallas kernels for 34%

profile of v4, /device:TPU:0, one launch (start us, length us, event | category | flops | bytes accessed | tf_op | source)
XLA Modules:
  0.0 458.2 jit_solution(13970329812575157135)
XLA Ops:
  7.3 1.4 copy-done.32
  11.4 23.2 %collective-permute-start.1 = (bf16[104,768]{1,0:T(8,128)(2,1)S(1)}, bf16[104,768]{1,0:T(8,128)(2,1)S(1)}, u32[]{:S(2)}, u32[]{:S(2)}) collective-permute-start(bf16[104,768]{1,0:T(8,128)(2,1)S(1)} %get-tuple-element.129), channel_id=1, source_target_pairs={{0,2},{1,3},{2,0},{3,1},{4,6},{5,7},{6,4},{7,5},{8,10},{9,11},{10,... | collective-permute-start | bytes 479240 | tf_op jit(solution)/shard_map/ppermute | solution.py:759
  34.6 4.3 collective-permute-start
  39.0 7.7 %collective-permute-done = bf16[104,768]{1,0:T(8,128)(2,1)S(1)} collective-permute-done((bf16[104,768]{1,0:T(8,128)(2,1)S(1)}, bf16[104,768]{1,0:T(8,128)(2,1)S(1)}, u32[]{:S(2)}, u32[]{:S(2)}) %collective-permute-start) | collective-permute-done | bytes 159776 | tf_op jit(solution)/shard_map/ppermute | solution.py:759
  46.7 2.2 collective-permute-done.2
  49.0 1.6 collective-permute-start.4
  50.6 8.9 %collective-permute-done.4.refs_1_ = bf16[4,104,768]{2,1,0:T(8,128)(2,1)S(1)} collective-permute-done((bf16[4,104,768]{2,1,0:T(8,128)(2,1)S(1)}, bf16[4,104,768]{2,1,0:T(8,128)(2,1)S(1)}, u32[]{:S(2)}, u32[]{:S(2)}) %collective-permute-start.4) | collective-permute-done | bytes 639008 | tf_op jit(solution)/shard_map/ppermute | solution.py:756
  59.5 1.7 collective-permute-start.5
  61.2 7.0 %collective-permute-start.6 = (bf16[512,768]{1,0:T(8,128)(2,1)S(1)}, bf16[512,768]{1,0:T(8,128)(2,1)S(1)}, u32[]{:S(2)}, u32[]{:S(2)}) collective-permute-start(bf16[512,768]{1,0:T(8,128)(2,1)S(1)} %get-tuple-element.68), channel_id=1, source_target_pairs={{0,1},{1,0},{2,5},{3,4},{4,3},{5,2},{6,7},{7,6},{8,9},{9,8},{10,13... | collective-permute-start | bytes 2359304 | tf_op jit(solution)/shard_map/ppermute | solution.py:739
  68.3 31.8 %collective-permute-done.6.refs_2_ = bf16[512,768]{1,0:T(8,128)(2,1)S(1)} collective-permute-done((bf16[512,768]{1,0:T(8,128)(2,1)S(1)}, bf16[512,768]{1,0:T(8,128)(2,1)S(1)}, u32[]{:S(2)}, u32[]{:S(2)}) %collective-permute-start.6) | collective-permute-done | bytes 786464 | tf_op jit(solution)/shard_map/ppermute | solution.py:739
  101.7 3.8 collective-permute-done.8
  107.0 2.6 arrange.1
  109.6 1.2 copy-done.31
  110.8 3.5 project.3.refs_2_.refs_4_.refs_0_.refs_5_.refs_7_
  116.5 1.4 copy-done.28
  119.3 1.4 collective-permute-start.11
  120.8 2.0 copy-done.7
  122.8 1.6 project.2.refs_0_
  124.4 1.1 copy-done.5
  125.5 38.9 %attend_forward.1 = (bf16[768,1024]{1,0:T(8,128)(2,1)S(1)}, f32[12,1,1024]{2,1,0:T(1,128)S(1)}) custom-call(bf16[768,1024]{1,0:T(8,128)(2,1)} %copy-done.5, bf16[16,1024]{1,0:T(8,128)(2,1)S(1)} %convert_convert_fusion.refs_1_.refs_4_, bf16[1536,1024]{1,0:T(8,128)(2,1)} %copy-done, bf16[1536,1024]{1,0:T(8,128)(2,1)} %collective-permute-done.9.refs_3_.refs_5_.refs_6_.refs_8_, ...), custom_call_target="tpu_custom_call" | custom-call | flops 1610612736 | bytes 589824 | tf_op jit(solution)/shard_map/attend_forward/pallas_call | solution.py:91
  164.4 1.2 copy-done.4
  165.7 1.1 copy-done.11
  166.8 52.2 %middle.1 = (bf16[1024,768]{1,0:T(8,128)(2,1)}, bf16[4,1024,768]{2,1,0:T(8,128)(2,1)}, bf16[4,1024,1536]{2,1,0:T(8,128)(2,1)}, bf16[1024,768]{1,0:T(8,128)(2,1)}...) custom-call(bf16[768,1024]{1,0:T(8,128)(2,1)} %copy-done.4, ...), custom_call_target="tpu_custom_call" | custom-call | flops 1962934272 | bytes 3932160 | tf_op jit(solution)/shard_map/middle/pallas_call | solution.py:346
  219.8 11.4 %side_grads.1 = (bf16[4,4,128,768]{3,2,1,0:T(8,128)(2,1)S(1)}, bf16[4,4,128,768]{3,2,1,0:T(8,128)(2,1)S(1)}) custom-call(s32[1]{0:T(128)} %bitcast.43.core_ref, bf16[1024,768]{1,0:T(8,128)(2,1)} %get-tuple-element.78.mix_ref, bf16[4,1024,768]{2,1,0:T(8,128)(2,1)} %get-tuple-element.79.hid_ref, bf16[1024,768]{1,0:T(8,128)(2,1)} %get-tuple-element.80.proj_ref, ...), custom_call_target="tpu_custom_call" | custom-call | flops 377487360 | bytes 1048576 | tf_op jit(solution)/shard_map/side_grads/pallas_call | solution.py:654
  231.2 5.6 %collective-permute-start.13 = (bf16[4,4,128,768]{3,2,1,0:T(8,128)(2,1)S(1)}, bf16[4,4,128,768]{3,2,1,0:T(8,128)(2,1)S(1)}, u32[]{:S(2)}, u32[]{:S(2)}) collective-permute-start(bf16[4,4,128,768]{3,2,1,0:T(8,128)(2,1)S(1)} %get-tuple-element.83), channel_id=1, source_target_pairs={{0,4},{4,0},{1,5},{5,1},{2,6},{6,2},{3,7},{7,3},{8,12},{12,8},{9,1... | collective-permute-start | bytes 9437192 | tf_op jit(solution)/shard_map/ppermute | solution.py:792
  236.9 9.5 %gate_up_grads.2.refs_0_ = bf16[8,4,96,1536]{3,2,1,0:T(8,128)(2,1)} custom-call(bf16[1024,768]{1,0:T(8,128)(2,1)} %get-tuple-element.84.x_ref, bf16[4,1024,1536]{2,1,0:T(8,128)(2,1)} %get-tuple-element.85.g_ref, bf16[4,4,128,768]{3,2,1,0:T(8,128)(2,1)S(1)} %get-tuple-element.82.refs_0_.mine), custom_call_target="tpu_custom_call" | custom-call | flops 4831838208 | bytes 12582912 | tf_op jit(solution)/shard_map/gate_up_grads/pallas_call | solution.py:693
  246.4 2.4 join.6
  248.7 9.5 %gate_up_grads.3.refs_13_ = bf16[8,4,96,1536]{3,2,1,0:T(8,128)(2,1)} custom-call(bf16[1024,768]{1,0:T(8,128)(2,1)} %get-tuple-element.84.x_ref, bf16[4,1024,1536]{2,1,0:T(8,128)(2,1)} %get-tuple-element.85.g_ref, bf16[8,4,96,1536]{3,2,1,0:T(8,128)(2,1)} %gate_up_grads.2.refs_0_, ...), custom_call_target="tpu_custom_call", output_to_operand_aliasing={{}: (2, {})} | custom-call | flops 4831838208 | bytes 12582912 | tf_op jit(solution)/shard_map/gate_up_grads/pallas_call | solution.py:693
  258.3 1.5 collective-permute-start.16
  259.8 7.4 %collective-permute-start.12 = (bf16[512,768]{1,0:T(8,128)(2,1)}, bf16[512,768]{1,0:T(8,128)(2,1)}, u32[]{:S(2)}, u32[]{:S(2)}) collective-permute-start(bf16[512,768]{1,0:T(8,128)(2,1)} %get-tuple-element.74), channel_id=1, source_target_pairs={{0,0},{1,1},{4,2},{5,3},{2,4},{3,5},{6,6},{7,7},{8,8},{9,9},{12,10... | collective-permute-start | bytes 2359304 | tf_op jit(solution)/shard_map/ppermute | solution.py:742
  267.2 17.7 %attend_backward.4 = (f32[192,1024]{1,0:T(8,128)S(1)}, f32[2,192,1024]{2,1,0:T(8,128)S(1)}, bf16[2,192,1024]{2,1,0:T(8,128)(2,1)S(1)}) custom-call(bf16[768,1024]{1,0:T(8,128)(2,1)} %copy-done.5, bf16[768,1024]{1,0:T(8,128)(2,1)} %get-tuple-element.76.refs_1_, bf16[768,1024]{1,0:T(8,128)(2,1)} %copy-done.4, f32[12,1,1024]{2,1,0:T(1,128)S(1)} %get-tuple-element.77.refs_3_, ...), custom_call_target="tpu_custom_call" | custom-call | flops 754974720 | bytes 294912 | tf_op jit(solution)/shard_map/attend_backward/pallas_call | solution.py:160
  285.0 1.2 copy-done.29
  287.1 1.2 join.7
  288.3 1.5 collective-permute-start.18
  290.7 8.3 %collective-permute-start.14 = (bf16[512,768]{1,0:T(8,128)(2,1)}, bf16[512,768]{1,0:T(8,128)(2,1)S(1)}, u32[]{:S(2)}, u32[]{:S(2)}) collective-permute-start(bf16[512,768]{1,0:T(8,128)(2,1)} %stack.206), channel_id=1, source_target_pairs={{1,0},{0,1},{5,2},{4,3},{3,4},{2,5},{7,6},{6,7},{9,8},{8,9},{13,10... | collective-permute-start | bytes 2359304 | tf_op jit(solution)/shard_map/ppermute | solution.py:742
  299.0 17.6 %attend_backward.5 = (f32[192,1024]{1,0:T(8,128)S(1)}, f32[2,192,1024]{2,1,0:T(8,128)S(1)}, bf16[2,192,1024]{2,1,0:T(8,128)(2,1)S(1)}) custom-call(bf16[768,1024]{1,0:T(8,128)(2,1)} %copy-done.5, bf16[768,1024]{1,0:T(8,128)(2,1)} %get-tuple-element.76.refs_1_, bf16[768,1024]{1,0:T(8,128)(2,1)} %copy-done.4, f32[12,1,1024]{2,1,0:T(1,128)S(1)} %get-tuple-element.77.refs_3_, ...), custom_call_target="tpu_custom_call" | custom-call | flops 754974720 | bytes 294912 | tf_op jit(solution)/shard_map/attend_backward/pallas_call | solution.py:160
  317.2 1.3 join.8
  318.5 8.5 %collective-permute-start.20 = (bf16[128,768]{1,0:T(8,128)(2,1)S(1)}, bf16[128,768]{1,0:T(8,128)(2,1)S(1)}, u32[]{:S(2)}, u32[]{:S(2)}) collective-permute-start(bf16[128,768]{1,0:T(8,128)(2,1)S(1)} %get-tuple-element.99.refs_12_), channel_id=1, source_target_pairs={{0,1},{1,2},{2,3},{3,0},{4,5},{5,6},{6,7},{7,4},{8,9},{9,10},{10,1... | collective-permute-start | bytes 589832 | tf_op jit(solution)/shard_map/ppermute | solution.py:759
  327.1 2.4 collective-permute-start.22
  330.4 17.8 %attend_backward.6 = (f32[192,1024]{1,0:T(8,128)S(1)}, f32[2,192,1024]{2,1,0:T(8,128)S(1)}, bf16[2,192,1024]{2,1,0:T(8,128)(2,1)S(1)}) custom-call(bf16[768,1024]{1,0:T(8,128)(2,1)} %copy-done.5, bf16[768,1024]{1,0:T(8,128)(2,1)} %get-tuple-element.76.refs_1_, bf16[768,1024]{1,0:T(8,128)(2,1)} %copy-done.4, f32[12,1,1024]{2,1,0:T(1,128)S(1)} %get-tuple-element.77.refs_3_, ...), custom_call_target="tpu_custom_call" | custom-call | flops 754974720 | bytes 294912 | tf_op jit(solution)/shard_map/attend_backward/pallas_call | solution.py:160
  348.9 17.8 %attend_backward.7 = (f32[192,1024]{1,0:T(8,128)S(1)}, f32[2,192,1024]{2,1,0:T(8,128)S(1)}, bf16[2,192,1024]{2,1,0:T(8,128)(2,1)S(1)}) custom-call(bf16[768,1024]{1,0:T(8,128)(2,1)} %copy-done.5, bf16[768,1024]{1,0:T(8,128)(2,1)} %get-tuple-element.76.refs_1_, bf16[768,1024]{1,0:T(8,128)(2,1)} %copy-done.4, f32[12,1,1024]{2,1,0:T(1,128)S(1)} %get-tuple-element.77.refs_3_, ...), custom_call_target="tpu_custom_call" | custom-call | flops 754974720 | bytes 294912 | tf_op jit(solution)/shard_map/attend_backward/pallas_call | solution.py:160
  366.9 1.6 unturn.4
  369.5 1.9 unturn.5
  372.5 1.6 unturn.6
  374.1 1.0 copy-done.17
  375.1 1.6 unturn.7
  377.8 1.5 dynamic-slice_bitcast_fusion
  380.6 1.3 copy-done.15
  381.8 4.8 %finish.2.refs_0_ = bf16[512,768]{1,0:T(8,128)(2,1)S(1)} custom-call(bf16[3,192,1024]{2,1,0:T(8,128)(2,1)S(1)} %copy-done.13, bf16[3,192,1024]{2,1,0:T(8,128)(2,1)S(1)} %copy-done.15, bf16[3,192,1024]{2,1,0:T(8,128)(2,1)} %copy-done.17, bf16[3,192,1024]{2,1,0:T(8,128)(2,1)} %copy-done.18, f32[1024,768]{1,0:T(8,128)} %get-tuple-element.110.refs_4_, ...), custom_call_target="tpu_custom_call" | custom-call | flops 113246208 | bytes 786432 | tf_op jit(solution)/shard_map/finish/pallas_call | solution.py:452
  386.7 3.0 join.9
  391.5 1.8 collective-permute-start.25
  393.2 1.3 copy-done.16
  394.5 1.2 copy-done.20
  395.7 4.9 %finish.3.refs_2_.refs_0_ = bf16[512,768]{1,0:T(8,128)(2,1)S(1)} custom-call(bf16[3,192,1024]{2,1,0:T(8,128)(2,1)S(1)} %copy-done.13, bf16[3,192,1024]{2,1,0:T(8,128)(2,1)S(1)} %copy-done.16, bf16[3,192,1024]{2,1,0:T(8,128)(2,1)} %copy-done.17, bf16[3,192,1024]{2,1,0:T(8,128)(2,1)} %copy-done.18, f32[1024,768]{1,0:T(8,128)} %get-tuple-element.110.refs_4_, ...), custom_call_target="tpu_custom_call" | custom-call | flops 113246208 | bytes 786432 | tf_op jit(solution)/shard_map/finish/pallas_call | solution.py:452
  401.5 2.4 collective-permute-done.27.got
  404.1 1.5 collective-permute-start.28
  406.9 2.4 settle.1
  409.3 3.2 collective-permute-done.28.got
  413.2 2.6 collective-permute-start.30
  415.7 1.7 collective-permute-start.31
  417.4 9.4 %collective-permute-done.26 = bf16[512,768]{1,0:T(8,128)(2,1)S(1)} collective-permute-done((bf16[512,768]{1,0:T(8,128)(2,1)S(1)}, bf16[512,768]{1,0:T(8,128)(2,1)S(1)}, u32[]{:S(2)}, u32[]{:S(2)}) %collective-permute-start.26) | collective-permute-done | bytes 786464 | tf_op jit(solution)/shard_map/ppermute | solution.py:742
  426.8 2.2 fusion.2
  429.1 8.4 %collective-permute-done.29 = bf16[72,768]{1,0:T(8,128)(2,1)S(1)} collective-permute-done((bf16[72,768]{1,0:T(8,128)(2,1)S(1)}, bf16[72,768]{1,0:T(8,128)(2,1)S(1)}, u32[]{:S(2)}, u32[]{:S(2)}) %collective-permute-start.29) | collective-permute-done | bytes 110624 | tf_op jit(solution)/shard_map/ppermute | solution.py:759
  437.5 11.1 %collective-permute-done.30 = bf16[72,768]{1,0:T(8,128)(2,1)S(1)} collective-permute-done((bf16[72,768]{1,0:T(8,128)(2,1)S(1)}, bf16[72,768]{1,0:T(8,128)(2,1)S(1)}, u32[]{:S(2)}, u32[]{:S(2)}) %collective-permute-start.30) | collective-permute-done | bytes 110624 | tf_op jit(solution)/shard_map/ppermute | solution.py:759
  (197 shorter events, 26.4 us)
Async XLA Ops:
  7.2 159.7 %all-gather.3.cloned.1.call-start = ((), (), s32[]{:S(2)}) async-start(), calls=%async_computation.4 | async-start | bytes 14598144 | tf_op jit(solution)/shard_map/all_gather | solution.py:785
  8.7 2.4 copy-start.48
  8.7 2.4 copy-start.49
  8.7 2.4 copy-start.50
  8.8 2.4 copy-start.51
  8.8 2.5 copy-start.44
  8.8 2.5 copy-start.45
  9.5 0.7 collective-permute-start.3
  11.0 368.8 %reduce-scatter.3.cloned.1.call-start = ((), (), s32[]{:S(2)}) async-start(), calls=%async_computation.2 | async-start | bytes 10616832 | tf_op jit(solution)/shard_map/reduce_scatter | solution.py:910
  11.4 27.6 %collective-permute-start.1 = (bf16[104,768]{1,0:T(8,128)(2,1)S(1)}, bf16[104,768]{1,0:T(8,128)(2,1)S(1)}, u32[]{:S(2)}, u32[]{:S(2)}) collective-permute-start(bf16[104,768]{1,0:T(8,128)(2,1)S(1)} %get-tuple-element.129), channel_id=1, source_target_pairs={{0,2},{1,3},{2,0},{3,1},{4,6},{5,7},{6,4},{7,5},{8,10},{9,11},{10,... | collective-permute-start | bytes 479240 | tf_op jit(solution)/shard_map/ppermute | solution.py:759
  34.6 12.1 %collective-permute-start = (bf16[104,768]{1,0:T(8,128)(2,1)S(1)}, bf16[104,768]{1,0:T(8,128)(2,1)S(1)}, u32[]{:S(2)}, u32[]{:S(2)}) collective-permute-start(bf16[104,768]{1,0:T(8,128)(2,1)S(1)} %get-tuple-element.129), channel_id=1, source_target_pairs={{0,1},{1,2},{2,3},{3,0},{4,5},{5,6},{6,7},{7,4},{8,9},{9,10},{10,1... | collective-permute-start | bytes 479240 | tf_op jit(solution)/shard_map/ppermute | solution.py:759
  38.8 10.1 %collective-permute-start.2 = (bf16[104,768]{1,0:T(8,128)(2,1)S(1)}, bf16[104,768]{1,0:T(8,128)(2,1)S(1)}, u32[]{:S(2)}, u32[]{:S(2)}) collective-permute-start(bf16[104,768]{1,0:T(8,128)(2,1)S(1)} %get-tuple-element.129), channel_id=1, source_target_pairs={{0,3},{1,0},{2,1},{3,2},{4,7},{5,4},{6,5},{7,6},{8,11},{9,8},{10,9... | collective-permute-start | bytes 479240 | tf_op jit(solution)/shard_map/ppermute | solution.py:759
  49.0 10.5 %collective-permute-start.4 = (bf16[4,104,768]{2,1,0:T(8,128)(2,1)S(1)}, bf16[4,104,768]{2,1,0:T(8,128)(2,1)S(1)}, u32[]{:S(2)}, u32[]{:S(2)}) collective-permute-start(bf16[4,104,768]{2,1,0:T(8,128)(2,1)S(1)} %stack.201.refs_0_), channel_id=1, source_target_pairs={{0,8},{4,20},{8,0},{12,28},{16,24},{20,4},{24,16},{28,12},{1,9},{5... | collective-permute-start | bytes 1916936 | tf_op jit(solution)/shard_map/ppermute | solution.py:756
  59.5 40.6 %collective-permute-start.5 = (bf16[8,104,768]{2,1,0:T(8,128)(2,1)S(1)}, bf16[8,104,768]{2,1,0:T(8,128)(2,1)S(1)}, u32[]{:S(2)}, u32[]{:S(2)}) collective-permute-start(bf16[8,104,768]{2,1,0:T(8,128)(2,1)S(1)} %stack.202.refs_0_), channel_id=1, source_target_pairs={{0,16},{4,12},{8,24},{12,4},{16,0},{20,28},{24,8},{28,20},{1,17},{... | collective-permute-start | bytes 3833864 | tf_op jit(solution)/shard_map/ppermute | solution.py:756
  61.2 39.7 %copy-start.46 = (s32[2,2048]{1,0:T(2,128)S(1)}, s32[2,2048]{1,0:T(2,128)}, u32[]{:S(2)}) copy-start(s32[2,2048]{1,0:T(2,128)} %param.15) | copy-start | bytes 49156
  61.2 39.7 %copy-start.47 = (s32[2,2048]{1,0:T(2,128)S(1)}, s32[2,2048]{1,0:T(2,128)}, u32[]{:S(2)}) copy-start(s32[2,2048]{1,0:T(2,128)} %param.14) | copy-start | bytes 49156
  61.2 38.8 %collective-permute-start.6 = (bf16[512,768]{1,0:T(8,128)(2,1)S(1)}, bf16[512,768]{1,0:T(8,128)(2,1)S(1)}, u32[]{:S(2)}, u32[]{:S(2)}) collective-permute-start(bf16[512,768]{1,0:T(8,128)(2,1)S(1)} %get-tuple-element.68), channel_id=1, source_target_pairs={{0,1},{1,0},{2,5},{3,4},{4,3},{5,2},{6,7},{7,6},{8,9},{9,8},{10,13... | collective-permute-start | bytes 2359304 | tf_op jit(solution)/shard_map/ppermute | solution.py:739
  101.0 6.0 %collective-permute-start.7 = (bf16[16,104,768]{2,1,0:T(8,128)(2,1)S(1)}, bf16[16,104,768]{2,1,0:T(8,128)(2,1)}, u32[]{:S(2)}, u32[]{:S(2)}) collective-permute-start(bf16[16,104,768]{2,1,0:T(8,128)(2,1)S(1)} %stack.203), channel_id=1, source_target_pairs={{0,4},{4,0},{1,5},{5,1},{2,6},{6,2},{3,7},{7,3},{8,12},{12,8},{9,1... | collective-permute-start | bytes 7667720 | tf_op jit(solution)/shard_map/ppermute | solution.py:777
  101.0 4.5 collective-permute-start.8
  106.4 4.4 copy-start.9
  107.0 3.9 copy-start.1
  110.8 3.5 copy-start.6
  114.3 2.2 copy-start
  114.3 11.2 %collective-permute-start.9 = (bf16[1536,1024]{1,0:T(8,128)(2,1)S(1)}, bf16[1536,1024]{1,0:T(8,128)(2,1)}, u32[]{:S(2)}, u32[]{:S(2)}) collective-permute-start(bf16[1536,1024]{1,0:T(8,128)(2,1)S(1)} %project.3.refs_2_.refs_4_.refs_0_.refs_5_.refs_7_), channel_id=1, source_target_pairs={{0,4},{4,0},{1,5},{5,1},{2,6},{6,2},{3,7},{7,3},{8,12},{12,8},{9,1... | collective-permute-start | bytes 9437192 | tf_op jit(solution)/shard_map/ppermute | solution.py:870
  117.9 2.9 copy-start.2
  117.9 2.9 copy-start.10
  118.6 47.0 %collective-permute-start.10 = (bf16[512,768]{1,0:T(8,128)(2,1)S(1)}, bf16[512,768]{1,0:T(8,128)(2,1)S(1)}, u32[]{:S(2)}, u32[]{:S(2)}) collective-permute-start(bf16[512,768]{1,0:T(8,128)(2,1)S(1)} %get-tuple-element.71), channel_id=1, source_target_pairs={{0,0},{1,1},{2,4},{3,5},{4,2},{5,3},{6,6},{7,7},{8,8},{9,9},{10,12... | collective-permute-start | bytes 2359304 | tf_op jit(solution)/shard_map/ppermute | solution.py:739
  119.3 46.3 %collective-permute-start.11 = (bf16[512,768]{1,0:T(8,128)(2,1)S(1)}, bf16[512,768]{1,0:T(8,128)(2,1)S(1)}, u32[]{:S(2)}, u32[]{:S(2)}) collective-permute-start(bf16[512,768]{1,0:T(8,128)(2,1)S(1)} %get-tuple-element.72), channel_id=1, source_target_pairs={{0,1},{1,0},{2,5},{3,4},{4,3},{5,2},{6,7},{7,6},{8,9},{9,8},{10,13... | collective-permute-start | bytes 2359304 | tf_op jit(solution)/shard_map/ppermute | solution.py:739
  120.8 2.0 copy-start.7
  231.2 15.2 %collective-permute-start.13 = (bf16[4,4,128,768]{3,2,1,0:T(8,128)(2,1)S(1)}, bf16[4,4,128,768]{3,2,1,0:T(8,128)(2,1)S(1)}, u32[]{:S(2)}, u32[]{:S(2)}) collective-permute-start(bf16[4,4,128,768]{3,2,1,0:T(8,128)(2,1)S(1)} %get-tuple-element.83), channel_id=1, source_target_pairs={{0,4},{4,0},{1,5},{5,1},{2,6},{6,2},{3,7},{7,3},{8,12},{12,8},{9,1... | collective-permute-start | bytes 9437192 | tf_op jit(solution)/shard_map/ppermute | solution.py:792
  236.9 9.5 %copy-start.38 = (s32[4]{0:T(128)}, s32[4]{0:T(128)S(1)}, u32[]{:S(2)}) copy-start(s32[4]{0:T(128)S(1)} %pad_add_fusion.4.place) | copy-start | bytes 52
  258.2 191.1 %reduce-scatter.5.cloned.1.call-start = ((), (), s32[]{:S(2)}) async-start(), calls=%async_computation.3 | async-start | bytes 1474560 | tf_op jit(solution)/shard_map/reduce_scatter | solution.py:911
  258.3 28.8 %collective-permute-start.16 = (bf16[2,4,128,768]{3,2,1,0:T(8,128)(2,1)}, bf16[2,4,128,768]{3,2,1,0:T(8,128)(2,1)S(1)}, u32[]{:S(2)}, u32[]{:S(2)}) collective-permute-start(bf16[2,4,128,768]{3,2,1,0:T(8,128)(2,1)} %get-tuple-element.87.refs_2_.refs_12_), channel_id=1, source_target_pairs={{0,16},{4,12},{8,24},{12,4},{16,0},{20,28},{24,8},{28,20},{1,17},{... | collective-permute-start | bytes 4718600 | tf_op jit(solution)/shard_map/ppermute | solution.py:756
  259.8 39.2 %collective-permute-start.12 = (bf16[512,768]{1,0:T(8,128)(2,1)}, bf16[512,768]{1,0:T(8,128)(2,1)}, u32[]{:S(2)}, u32[]{:S(2)}) collective-permute-start(bf16[512,768]{1,0:T(8,128)(2,1)} %get-tuple-element.74), channel_id=1, source_target_pairs={{0,0},{1,1},{4,2},{5,3},{2,4},{3,5},{6,6},{7,7},{8,8},{9,9},{12,10... | collective-permute-start | bytes 2359304 | tf_op jit(solution)/shard_map/ppermute | solution.py:742
  287.1 2.7 copy-start.33
  288.3 28.9 %collective-permute-start.18 = (bf16[4,128,768]{2,1,0:T(8,128)(2,1)}, bf16[4,128,768]{2,1,0:T(8,128)(2,1)}, u32[]{:S(2)}, u32[]{:S(2)}) collective-permute-start(bf16[4,128,768]{2,1,0:T(8,128)(2,1)} %get-tuple-element.93.refs_12_), channel_id=1, source_target_pairs={{0,8},{4,20},{8,0},{12,28},{16,24},{20,4},{24,16},{28,12},{1,9},{5... | collective-permute-start | bytes 2359304 | tf_op jit(solution)/shard_map/ppermute | solution.py:756
  290.7 38.8 %collective-permute-start.14 = (bf16[512,768]{1,0:T(8,128)(2,1)}, bf16[512,768]{1,0:T(8,128)(2,1)S(1)}, u32[]{:S(2)}, u32[]{:S(2)}) collective-permute-start(bf16[512,768]{1,0:T(8,128)(2,1)} %stack.206), channel_id=1, source_target_pairs={{1,0},{0,1},{5,2},{4,3},{3,4},{2,5},{7,6},{6,7},{9,8},{8,9},{13,10... | collective-permute-start | bytes 2359304 | tf_op jit(solution)/shard_map/ppermute | solution.py:742
  299.0 18.2 %copy-start.40 = (s32[4]{0:T(128)}, s32[4]{0:T(128)S(1)}, u32[]{:S(2)}) copy-start(s32[4]{0:T(128)S(1)} %pad_add_fusion.5.place) | copy-start | bytes 52
  316.7 12.9 %copy-start.43 = (bf16[2,192,1024]{2,1,0:T(8,128)(2,1)S(1)}, bf16[2,192,1024]{2,1,0:T(8,128)(2,1)}, u32[]{:S(2)}) copy-start(bf16[2,192,1024]{2,1,0:T(8,128)(2,1)} %copy-done.42) | copy-start | bytes 2359300
  318.5 29.7 %collective-permute-start.20 = (bf16[128,768]{1,0:T(8,128)(2,1)S(1)}, bf16[128,768]{1,0:T(8,128)(2,1)S(1)}, u32[]{:S(2)}, u32[]{:S(2)}) collective-permute-start(bf16[128,768]{1,0:T(8,128)(2,1)S(1)} %get-tuple-element.99.refs_12_), channel_id=1, source_target_pairs={{0,1},{1,2},{2,3},{3,0},{4,5},{5,6},{6,7},{7,4},{8,9},{9,10},{10,1... | collective-permute-start | bytes 589832 | tf_op jit(solution)/shard_map/ppermute | solution.py:759
  327.1 21.7 %collective-permute-start.21 = (bf16[128,768]{1,0:T(8,128)(2,1)S(1)}, bf16[128,768]{1,0:T(8,128)(2,1)S(1)}, u32[]{:S(2)}, u32[]{:S(2)}) collective-permute-start(bf16[128,768]{1,0:T(8,128)(2,1)S(1)} %get-tuple-element.100.refs_13_), channel_id=1, source_target_pairs={{0,2},{1,3},{2,0},{3,1},{4,6},{5,7},{6,4},{7,5},{8,10},{9,11},{10,... | collective-permute-start | bytes 589832 | tf_op jit(solution)/shard_map/ppermute | solution.py:759
  327.1 21.7 %collective-permute-start.22 = (bf16[128,768]{1,0:T(8,128)(2,1)S(1)}, bf16[128,768]{1,0:T(8,128)(2,1)S(1)}, u32[]{:S(2)}, u32[]{:S(2)}) collective-permute-start(bf16[128,768]{1,0:T(8,128)(2,1)S(1)} %get-tuple-element.101.refs_14_), channel_id=1, source_target_pairs={{0,3},{1,0},{2,1},{3,2},{4,7},{5,4},{6,5},{7,6},{8,11},{9,8},{10,9... | collective-permute-start | bytes 589832 | tf_op jit(solution)/shard_map/ppermute | solution.py:759
  329.5 37.3 %collective-permute-start.15 = (bf16[2,192,1024]{2,1,0:T(8,128)(2,1)S(1)}, bf16[2,192,1024]{2,1,0:T(8,128)(2,1)S(1)}, u32[]{:S(2)}, u32[]{:S(2)}) collective-permute-start(bf16[2,192,1024]{2,1,0:T(8,128)(2,1)S(1)} %copy-done.43), channel_id=1, source_target_pairs={{0,4},{4,0},{1,5},{5,1},{2,6},{6,2},{3,7},{7,3},{8,12},{12,8},{9,1... | collective-permute-start | bytes 2359304 | tf_op jit(solution)/shard_map/ppermute | solution.py:928
  329.5 40.0 %collective-permute-start.17 = (bf16[2,192,1024]{2,1,0:T(8,128)(2,1)S(1)}, bf16[2,192,1024]{2,1,0:T(8,128)(2,1)S(1)}, u32[]{:S(2)}, u32[]{:S(2)}) collective-permute-start(bf16[2,192,1024]{2,1,0:T(8,128)(2,1)S(1)} %get-tuple-element.96), channel_id=1, source_target_pairs={{0,4},{4,0},{1,5},{5,1},{2,6},{6,2},{3,7},{7,3},{8,12},{12,8},{9,1... | collective-permute-start | bytes 2359304 | tf_op jit(solution)/shard_map/ppermute | solution.py:928
  348.2 24.2 %collective-permute-start.19 = (bf16[2,192,1024]{2,1,0:T(8,128)(2,1)S(1)}, bf16[2,192,1024]{2,1,0:T(8,128)(2,1)S(1)}, u32[]{:S(2)}, u32[]{:S(2)}) collective-permute-start(bf16[2,192,1024]{2,1,0:T(8,128)(2,1)S(1)} %get-tuple-element.104), channel_id=1, source_target_pairs={{0,4},{4,0},{1,5},{5,1},{2,6},{6,2},{3,7},{7,3},{8,12},{12,8},{9,1... | collective-permute-start | bytes 2359304 | tf_op jit(solution)/shard_map/ppermute | solution.py:928
  348.9 42.5 %copy-start.21 = (f32[128,768]{1,0:T(8,128)}, f32[128,768]{1,0:T(8,128)S(1)}, u32[]{:S(2)}) copy-start(f32[128,768]{1,0:T(8,128)S(1)} %convert_add_fusion.refs_11_) | copy-start | bytes 1179652
  348.9 17.9 %copy-start.3 = (bf16[1024,768]{1,0:T(8,128)(2,1)S(1)}, bf16[1024,768]{1,0:T(8,128)(2,1)}, u32[]{:S(2)}) copy-start(bf16[1024,768]{1,0:T(8,128)(2,1)} %copy-done.1) | copy-start | bytes 4718596
  348.9 17.9 %copy-start.30 = (f32[2,192,1024]{2,1,0:T(8,128)S(1)}, f32[2,192,1024]{2,1,0:T(8,128)}, u32[]{:S(2)}) copy-start(f32[2,192,1024]{2,1,0:T(8,128)} %copy-done.29) | copy-start | bytes 4718596
  366.8 8.4 %collective-permute-start.23 = (bf16[2,192,1024]{2,1,0:T(8,128)(2,1)S(1)}, bf16[2,192,1024]{2,1,0:T(8,128)(2,1)S(1)}, u32[]{:S(2)}, u32[]{:S(2)}) collective-permute-start(bf16[2,192,1024]{2,1,0:T(8,128)(2,1)S(1)} %get-tuple-element.108), channel_id=1, source_target_pairs={{0,4},{4,0},{1,5},{5,1},{2,6},{6,2},{3,7},{7,3},{8,12},{12,8},{9,1... | collective-permute-start | bytes 2359304 | tf_op jit(solution)/shard_map/ppermute | solution.py:928
  379.3 7.4 %collective-permute-start.24 = (bf16[4,4,72,768]{3,2,1,0:T(8,128)(2,1)}, bf16[4,4,72,768]{3,2,1,0:T(8,128)(2,1)}, u32[]{:S(2)}, u32[]{:S(2)}) collective-permute-start(bf16[4,4,72,768]{3,2,1,0:T(8,128)(2,1)} %get-tuple-element.125.refs_6_), channel_id=1, source_target_pairs={{0,4},{4,0},{1,5},{5,1},{2,6},{6,2},{3,7},{7,3},{8,12},{12,8},{9,1... | collective-permute-start | bytes 5308424 | tf_op jit(solution)/shard_map/ppermute | solution.py:792
  381.8 4.9 %copy-start.39 = (s32[4]{0:T(128)S(1)}, s32[4]{0:T(128)}, u32[]{:S(2)}) copy-start(s32[4]{0:T(128)} %copy-done.38) | copy-start | bytes 52
  386.7 3.0 copy-start.27
  390.6 13.3 %collective-permute-start.27 = (bf16[2,4,72,768]{3,2,1,0:T(8,128)(2,1)}, bf16[2,4,72,768]{3,2,1,0:T(8,128)(2,1)S(1)}, u32[]{:S(2)}, u32[]{:S(2)}) collective-permute-start(bf16[2,4,72,768]{3,2,1,0:T(8,128)(2,1)} %get-tuple-element.116), channel_id=1, source_target_pairs={{0,16},{4,12},{8,24},{12,4},{16,0},{20,28},{24,8},{28,20},{1,17},{... | collective-permute-start | bytes 2654216 | tf_op jit(solution)/shard_map/ppermute | solution.py:756
  391.5 26.0 %collective-permute-start.25 = (bf16[512,768]{1,0:T(8,128)(2,1)}, bf16[512,768]{1,0:T(8,128)(2,1)S(1)}, u32[]{:S(2)}, u32[]{:S(2)}) collective-permute-start(bf16[512,768]{1,0:T(8,128)(2,1)} %copy-done.27), channel_id=1, source_target_pairs={{0,0},{1,1},{4,2},{5,3},{2,4},{3,5},{6,6},{7,7},{8,8},{9,9},{12,10... | collective-permute-start | bytes 2359304 | tf_op jit(solution)/shard_map/ppermute | solution.py:742
  395.7 5.0 %slice-start = ((f32[128,768]{1,0:T(8,128)}), f32[4,768]{1,0:T(4,128)S(1)}, s32[]{:S(2)}) async-start(f32[128,768]{1,0:T(8,128)} %copy-done.21), calls=%async_computation.5 | async-start | bytes 24576 | tf_op jit(solution)/shard_map/slice | solution.py:956
  395.7 5.1 %copy-start.22 = (f32[128,768]{1,0:T(8,128)S(1)}, f32[128,768]{1,0:T(8,128)}, u32[]{:S(2)}) copy-start(f32[128,768]{1,0:T(8,128)} %copy-done.21) | copy-start | bytes 1179652
  400.6 6.3 %copy-start.8 = (bf16[512,768]{1,0:T(8,128)(2,1)}, bf16[512,768]{1,0:T(8,128)(2,1)S(1)}, u32[]{:S(2)}) copy-start(bf16[512,768]{1,0:T(8,128)(2,1)S(1)} %finish.3.refs_2_.refs_0_) | copy-start | bytes 2359300
  400.6 26.2 %collective-permute-start.26 = (bf16[512,768]{1,0:T(8,128)(2,1)S(1)}, bf16[512,768]{1,0:T(8,128)(2,1)S(1)}, u32[]{:S(2)}, u32[]{:S(2)}) collective-permute-start(bf16[512,768]{1,0:T(8,128)(2,1)S(1)} %finish.3.refs_2_.refs_0_), channel_id=1, source_target_pairs={{1,0},{0,1},{5,2},{4,3},{3,4},{2,5},{7,6},{6,7},{9,8},{8,9},{13,10... | collective-permute-start | bytes 2359304 | tf_op jit(solution)/shard_map/ppermute | solution.py:742
  401.5 5.4 %copy-start.24 = (bf16[512,768]{1,0:T(8,128)(2,1)S(1)}, bf16[512,768]{1,0:T(8,128)(2,1)}, u32[]{:S(2)}) copy-start(bf16[512,768]{1,0:T(8,128)(2,1)} %copy-done.23) | copy-start | bytes 2359300
  404.1 8.4 %collective-permute-start.28 = (bf16[4,72,768]{2,1,0:T(8,128)(2,1)S(1)}, bf16[4,72,768]{2,1,0:T(8,128)(2,1)S(1)}, u32[]{:S(2)}, u32[]{:S(2)}) collective-permute-start(bf16[4,72,768]{2,1,0:T(8,128)(2,1)S(1)} %get-tuple-element.118), channel_id=1, source_target_pairs={{0,8},{4,20},{8,0},{12,28},{16,24},{20,4},{24,16},{28,12},{1,9},{5... | collective-permute-start | bytes 1327112 | tf_op jit(solution)/shard_map/ppermute | solution.py:756
  406.9 5.6 %copy-start.41 = (s32[4]{0:T(128)S(1)}, s32[4]{0:T(128)}, u32[]{:S(2)}) copy-start(s32[4]{0:T(128)} %copy-done.40) | copy-start | bytes 52
  413.1 24.4 %collective-permute-start.29 = (bf16[72,768]{1,0:T(8,128)(2,1)S(1)}, bf16[72,768]{1,0:T(8,128)(2,1)S(1)}, u32[]{:S(2)}, u32[]{:S(2)}) collective-permute-start(bf16[72,768]{1,0:T(8,128)(2,1)S(1)} %get-tuple-element.120), channel_id=1, source_target_pairs={{0,1},{1,2},{2,3},{3,0},{4,5},{5,6},{6,7},{7,4},{8,9},{9,10},{10,1... | collective-permute-start | bytes 331784 | tf_op jit(solution)/shard_map/ppermute | solution.py:759
  413.2 35.4 %collective-permute-start.30 = (bf16[72,768]{1,0:T(8,128)(2,1)S(1)}, bf16[72,768]{1,0:T(8,128)(2,1)S(1)}, u32[]{:S(2)}, u32[]{:S(2)}) collective-permute-start(bf16[72,768]{1,0:T(8,128)(2,1)S(1)} %get-tuple-element.121), channel_id=1, source_target_pairs={{0,2},{1,3},{2,0},{3,1},{4,6},{5,7},{6,4},{7,5},{8,10},{9,11},{10,... | collective-permute-start | bytes 331784 | tf_op jit(solution)/shard_map/ppermute | solution.py:759
  415.7 32.8 %collective-permute-start.31 = (bf16[72,768]{1,0:T(8,128)(2,1)S(1)}, bf16[72,768]{1,0:T(8,128)(2,1)S(1)}, u32[]{:S(2)}, u32[]{:S(2)}) collective-permute-start(bf16[72,768]{1,0:T(8,128)(2,1)S(1)} %get-tuple-element.122), channel_id=1, source_target_pairs={{0,3},{1,0},{2,1},{3,2},{4,7},{5,4},{6,5},{7,6},{8,11},{9,8},{10,9... | collective-permute-start | bytes 331784 | tf_op jit(solution)/shard_map/ppermute | solution.py:759
  (24 other events, 27.6 us)
Sparse Core Ops, SparseCore 0:
  11.1 149.0 all-gather.2
  258.3 90.6 reduce-scatter.2
  379.9 34.7 reduce-scatter.4
